TPU v7x, 1024 devices: a whole 4x8x16 slice. The times are simulated.
1024 devices in a mesh: dp: 64 (over z, y_hi, core), bal: 4 (over x), tensor: 4 (over y_lo).
Axes of the slice: x: 4, y: 8 (y_hi: 2, y_lo: 4; y = y_hi * 4 + y_lo), z: 16, core: 2. Of those that a mesh axis runs over, the one named last changes fastest.
Arguments:
- tiles: bfloat16 [64, 4, 16, 1280, 128], P('dp', 'bal', None, 'tensor'), may hold values from -6 to 6
- tile_counts: int32 [64, 4], P('dp'), may hold values from 1 to 16, 32 in all within a row
- doc_order: int32 [64, 4], P('dp'), may hold values from 0 to 3, each once within a row
- qkv_weight: bfloat16 [3, 1280, 1280], P(None, 'dp', 'tensor'), may hold values from -6 to 6
- out_weight: bfloat16 [1280, 1280], P('dp', 'tensor'), may hold values from -0.625 to 0.625
Outputs:
- encoded: bfloat16 [64, 32, 1280, 128], P('dp', 'bal', 'tensor')
Inputs may be any that keep to these rules, and one draw needn't show every extreme that they name: `tile_counts`: each row sums to 32, and in every row some document has exactly 16 tiles. `doc_order`: each row names every document once.
All inputs are finite; a program needn't handle non-finite values.
Results may differ from a plain program's by a relative error of at most 0.012.
Values may be sent and summed in bfloat16 or wider, within the bound.
No kernel may reach another device: no remote copies, remote signals or barrier semaphores. Data moves between devices by JAX's collectives and lax.ppermute only.
A program may use at most 64 MiB of HBM per device.

v0:
```python
import jax
import jax.numpy as jnp
from jax import lax
from jax.sharding import PartitionSpec as P

D = 1280
HDIM = 80
CAP = 8


EPSILON = 1e-06


def sent_to_all(shard, axis):
    length = lax.axis_size(axis)
    return lax.all_to_all(
        jnp.broadcast_to(shard[None], (length, *shard.shape)), axis, 0, 0, tiled=True
    )


def of_everyone(shard, axis):
    return sent_to_all(shard, axis).sum(axis=0)


def packed_total(arrays, axis):
    ends = [0]
    for a in arrays:
        ends.append(ends[-1] + a.size)
    subtotal = of_everyone(jnp.concatenate([a.ravel() for a in arrays]), axis)
    return tuple((subtotal[b:e].reshape(a.shape) for a, b, e in zip(arrays, ends, ends[1:])))


def in_order(tiles, dim):
    shape = list(tiles.shape[1:])
    shape[dim] *= tiles.shape[0]
    return jnp.moveaxis(tiles, 0, dim).reshape(shape)


def gathered_copies(shard, axis, dim):
    tiles = sent_to_all(shard, axis)
    return in_order(tiles, dim)


def rows_first(arrays, axis, dims):
    turned = [jnp.moveaxis(a, dim, 0) for a, dim in zip(arrays, dims)]
    widths = [t[0].size for t in turned]
    both = jnp.concatenate([t.reshape(-1, w) for t, w in zip(turned, widths)], axis=1)
    out = lax.all_gather(both, axis, axis=0, tiled=True)
    tiles = jnp.split(out, [sum(widths[:k]) for k in range(1, len(widths))], axis=1)
    return tuple(
        (
            jnp.moveaxis(b.reshape(-1, *t.shape[1:]), 0, dim)
            for b, t, dim in zip(tiles, turned, dims)
        )
    )


def layout(counts, ordering):
    doc_ids = jnp.arange(counts.shape[0], dtype=jnp.int32)
    position = jnp.sum(
        jnp.where(ordering[None, :] == doc_ids[:, None], doc_ids[None, :], 0), axis=1
    )
    starts = jnp.sum(jnp.where(position[None, :] < position[:, None], counts[None, :], 0), axis=1)
    return (doc_ids, starts)


def local(tiles, tile_counts, doc_order, qkv_weight, out_weight):
    bal_size = lax.axis_size("bal")
    owner_idx = lax.axis_index("bal")
    counts = tile_counts[0]
    doc_ids, starts = layout(counts, doc_order[0])
    own_tiles = tiles[0, 0]
    slot_count, slices, patches = own_tiles.shape
    pair_count = slot_count // bal_size
    own_start = jnp.sum(jnp.where(doc_ids == owner_idx, starts, 0))
    own_count = jnp.sum(jnp.where(doc_ids == owner_idx, counts, 0))
    target_dev = jnp.arange(bal_size, dtype=jnp.int32)[:, None]
    pair_rank = jnp.arange(pair_count, dtype=jnp.int32)[None, :]
    tile_pick = (pair_rank * bal_size + (target_dev - own_start) % bal_size).reshape(-1)
    is_live = (tile_pick < own_count).astype(jnp.bfloat16)
    outbound = jnp.take(own_tiles, tile_pick, axis=0) * is_live[:, None, None]
    outbound = outbound.reshape(bal_size, pair_count, slices * patches)
    arrived = lax.all_to_all(outbound, "bal", split_axis=0, concat_axis=0, tiled=True)
    arrived = arrived.reshape(bal_size * pair_count, slices, patches)
    packed = jnp.arange(CAP, dtype=jnp.int32) * bal_size + owner_idx
    inside = (starts[None, :] <= packed[:, None]) & (packed[:, None] < (starts + counts)[None, :])
    source = jnp.sum(jnp.where(inside, doc_ids[None, :], 0), axis=1)
    offset = packed - jnp.sum(jnp.where(inside, starts[None, :], 0), axis=1)
    chosen = jnp.take(arrived, source * pair_count + offset // bal_size, axis=0)
    values = chosen.astype(jnp.float32)
    moments = packed_total((jnp.sum(values, axis=1), jnp.sum(values * values, axis=1)), "tensor")
    row_mean = moments[0] / D
    row_var = moments[1] / D - row_mean * row_mean
    scaled = ((values - row_mean[:, None, :]) * lax.rsqrt(row_var + EPSILON)[:, None, :]).astype(
        jnp.bfloat16
    )
    normed = gathered_copies(scaled, "tensor", 1)
    full_qkv, full_out = rows_first((qkv_weight, out_weight), "dp", (1, 0))
    projected = jnp.einsum("cdp,kdf->kcfp", normed, full_qkv, preferred_element_type=jnp.float32)
    head_count = slices // HDIM
    projected = projected.astype(jnp.bfloat16).reshape(3, CAP, head_count, HDIM, patches)
    scores = jnp.einsum(
        "rhet,rhes->rhts", projected[0], projected[1], preferred_element_type=jnp.float32
    ) * HDIM ** (-0.5)
    probs = jax.nn.softmax(scores, axis=-1).astype(jnp.bfloat16)
    context = jnp.einsum("rhts,rhes->rhet", probs, projected[2], preferred_element_type=jnp.float32)
    context = context.astype(jnp.bfloat16).reshape(CAP, slices, patches)
    partial_value = jnp.einsum("cep,fe->cfp", context, full_out, preferred_element_type=jnp.float32)
    summed = lax.psum_scatter(
        partial_value.astype(jnp.bfloat16), "tensor", scatter_dimension=1, tiled=True
    ).astype(jnp.float32)
    encoded = (chosen.astype(jnp.float32) + summed).astype(jnp.bfloat16)
    encoded = encoded.reshape(CAP, slices * patches)
    pair_back = max(1, CAP // bal_size)
    back_rank = jnp.arange(pair_back, dtype=jnp.int32)[None, :]
    residue = (owner_idx - target_dev * CAP) % bal_size
    within = back_rank * bal_size + residue
    is_valid = within < CAP
    enc_slot = jnp.where(is_valid, (target_dev * CAP + within - owner_idx) // bal_size, 0).reshape(
        -1
    )
    outgoing = (
        jnp.take(encoded, enc_slot, axis=0) * is_valid.reshape(-1).astype(jnp.bfloat16)[:, None]
    )
    outgoing = outgoing.reshape(bal_size, pair_back, slices * patches)
    returned = lax.all_to_all(outgoing, "bal", split_axis=0, concat_axis=0, tiled=True)
    returned = returned.reshape(bal_size * pair_back, slices * patches)
    final_slot = jnp.arange(CAP, dtype=jnp.int32)
    final_pos = owner_idx * CAP + final_slot
    gather_idx = final_pos % bal_size * pair_back + final_slot // bal_size
    result = jnp.take(returned, gather_idx, axis=0).reshape(1, CAP, slices, patches)
    return result


def solution(mesh):
    placed = (
        P("dp", "bal", None, "tensor", None),
        P("dp", None),
        P("dp", None),
        P(None, "dp", "tensor"),
        P("dp", "tensor"),
    )
    return jax.shard_map(
        local, mesh=mesh, in_specs=placed, out_specs=P("dp", "bal", "tensor", None), check_vma=False
    )
```

profile of v0, /device:TPU:1, one launch (start us, length us, event | category | flops | bytes accessed | tf_op | source)
XLA Modules:
  0.0 306.8 jit_solution(3161585960590717676)
XLA Ops:
  7.6 1.4 maximum_bitcast_fusion
  9.8 1.3 fusion.19
  14.1 1.8 gather_fusion
  15.9 1.6 gather.14
  17.5 1.8 select_multiply_fusion
  19.3 4.8 %all-to-all-start = ((bf16[4,4,40960]{2,1,0:T(4,128)(2,1)}), bf16[4,4,40960]{2,1,0:T(4,128)(2,1)S(1)}, u32[]{:S(2)}, u32[]{:S(2)}) async-start(bf16[4,4,40960]{2,1,0:T(4,128)(2,1)} %select_multiply_fusion), calls=%async_computation | async-start | bytes 2621440 | tf_op jit(solution)/shard_map/all_to_all | solution.py:83
  24.3 11.0 %all-to-all-done = bf16[4,4,40960]{2,1,0:T(4,128)(2,1)S(1)} async-done(((bf16[4,4,40960]{2,1,0:T(4,128)(2,1)}), bf16[4,4,40960]{2,1,0:T(4,128)(2,1)S(1)}, u32[]{:S(2)}, u32[]{:S(2)}) %all-to-all-start) | async-done | bytes 1310752 | tf_op jit(solution)/shard_map/all_to_all | solution.py:83
  35.3 2.2 reshape.313
  37.5 2.0 gather_fusion.1
  39.8 14.8 %all_to_all.21 = f32[4,1,2048]{2,1,0:T(1,128)S(1)} all-to-all(f32[4,1,2048]{2,1,0:T(1,128)S(1)} %broadcast_in_dim.114), channel_id=1, replica_groups=mesh['dp'=64,'bal'=4,'tensor'=4] {'tensor'}, dimensions={0} | all-to-all | bytes 65536 | tf_op jit(solution)/shard_map/all_to_all | solution.py:16
  55.6 58.9 %all_to_all.22 = bf16[4,8,320,128]{3,2,1,0:T(8,128)(2,1)S(1)} all-to-all(bf16[4,8,320,128]{3,2,1,0:T(8,128)(2,1)S(1)} %broadcast_in_dim.115), channel_id=1, replica_groups=mesh['dp'=64,'bal'=4,'tensor'=4] {'tensor'}, dimensions={0} | all-to-all | bytes 5242880 | tf_op jit(solution)/shard_map/all_to_all | solution.py:16
  114.5 1.8 copy.30
  116.3 67.2 %all-gather.3.cloned.1.call-done = bf16[64,20,1280]{2,1,0:T(8,128)(2,1)} async-done(((bf16[1,20,1280]{2,1,0:T(8,128)(2,1)}), bf16[64,20,1280]{2,1,0:T(8,128)(2,1)}) %all-gather.3.cloned.1.call-update) | async-done | bytes 3276816 | tf_op jit(solution)/shard_map/all_gather | solution.py:48
  183.5 6.1 %reshape.359 = bf16[1280,1280]{1,0:T(8,128)(2,1)} reshape(bf16[64,20,1280]{2,1,0:T(8,128)(2,1)} %all-gather.3.cloned.1.call-done) | data formatting | bytes 6553600
  189.6 3.5 %split.9 = bf16[1280,960]{1,0:T(8,128)(2,1)} slice(bf16[1280,1280]{1,0:T(8,128)(2,1)} %reshape.359), slice={[0:1280], [0:960]} | slice | bytes 4915200 | tf_op jit(solution)/shard_map/split | solution.py:49
  193.1 4.3 %copy.28 = bf16[1280,960]{0,1:T(8,128)(2,1)} copy(bf16[1280,960]{1,0:T(8,128)(2,1)} %split.9) | data formatting | bytes 4915200 | tf_op jit(solution)/shard_map/split | solution.py:49
  197.4 5.2 %convert_bitcast_fusion = bf16[3,8,320,128]{3,2,1,0:T(8,128)(2,1)S(1)} fusion(bf16[3,1280,320,1]{1,2,3,0:T(8,128)(2,1)} %bitcast.79, bf16[8,1280,128,1]{2,1,0,3:T(8,128)(2,1)} %bitcast.78), kind=kOutput, calls=%fused_computation.13 | convolution fusion | flops 2517565440 | bytes 7045120 | tf_op jit(solution)/shard_map/cdp,kdf->kcfp/dot_general | solution.py:99
  203.6 3.3 %fusion.29 = (f32[8,4,128]{2,1,0:T(4,128)S(1)}, f32[8,4,128,128]{2,3,1,0:T(8,128)}) fusion(bf16[8,4,80,128]{3,2,1,0:T(8,128)(2,1)} %bitcast.82, bf16[8,4,80,128]{3,2,1,0:T(8,128)(2,1)S(1)} %bitcast.81), kind=kOutput, calls=%fused_computation.110 | convolution fusion | flops 85459072 | bytes 3424256 | tf_op jit(solution)/shard_map/sub | solution.py:105
  206.9 2.1 convolution_convert_fusion.1
  209.0 4.3 %fusion.1 = bf16[8,1280,128]{2,1,0:T(8,128)(2,1)} fusion(bf16[8,320,128]{2,1,0:T(8,128)(2,1)S(1)} %bitcast.88, bf16[1280,1280]{1,0:T(8,128)(2,1)} %reshape.359), kind=kOutput, calls=%fused_computation.6 | convolution fusion | flops 840171520 | bytes 4259840 | tf_op jit(solution)/shard_map/cep,fe->cfp/dot_general | solution.py:108
  213.7 66.0 %reduce-scatter.2.cloned.1.call-done = bf16[8,320,128]{2,1,0:T(8,128)(2,1)} async-done(((bf16[8,1280,128]{2,1,0:T(8,128)(2,1)}), bf16[8,320,128]{2,1,0:T(8,128)(2,1)}) %reduce-scatter.2.cloned.1.call-update) | async-done | bytes 655376 | tf_op jit(solution)/shard_map/reduce_scatter | solution.py:109
  279.7 1.4 fusion.8
  283.9 4.0 %all-to-all-start.3 = ((bf16[4,2,40960]{2,1,0:T(2,128)(2,1)}), bf16[4,2,40960]{2,1,0:T(2,128)(2,1)S(1)}, u32[]{:S(2)}, u32[]{:S(2)}) async-start(bf16[4,2,40960]{2,1,0:T(2,128)(2,1)} %reshape.321), calls=%async_computation.4 | async-start | bytes 1310720 | tf_op jit(solution)/shard_map/all_to_all | solution.py:126
  287.9 9.8 %all-to-all-done.3 = bf16[4,2,40960]{2,1,0:T(2,128)(2,1)S(1)} async-done(((bf16[4,2,40960]{2,1,0:T(2,128)(2,1)}), bf16[4,2,40960]{2,1,0:T(2,128)(2,1)S(1)}, u32[]{:S(2)}, u32[]{:S(2)}) %all-to-all-start.3) | async-done | bytes 655392 | tf_op jit(solution)/shard_map/all_to_all | solution.py:126
  (53 shorter events, 12.7 us)
Async XLA Ops:
  6.5 7.6 %copy-start = (bf16[1,1,16,320,128]{4,3,2,1,0:T(8,128)(2,1)S(1)}, bf16[1,1,16,320,128]{4,3,2,1,0:T(8,128)(2,1)}, u32[]{:S(2)}) copy-start(bf16[1,1,16,320,128]{4,3,2,1,0:T(8,128)(2,1)} %param.7) | copy-start | bytes 3932164
  6.5 177.0 %all-gather.3.cloned.1.call-start = ((), (), s32[]{:S(2)}) async-start(), calls=%async_computation.6 | async-start | bytes 3993600 | tf_op jit(solution)/shard_map/all_gather | solution.py:48
  17.5 6.6 %copy-start.1 = (s32[1,4]{1,0:T(1,128)S(1)}, s32[1,4]{1,0:T(1,128)}, u32[]{:S(2)}) copy-start(s32[1,4]{1,0:T(1,128)} %param.8) | copy-start | bytes 52
  19.3 16.0 %all-to-all-start = ((bf16[4,4,40960]{2,1,0:T(4,128)(2,1)}), bf16[4,4,40960]{2,1,0:T(4,128)(2,1)S(1)}, u32[]{:S(2)}, u32[]{:S(2)}) async-start(bf16[4,4,40960]{2,1,0:T(4,128)(2,1)} %select_multiply_fusion), calls=%async_computation | async-start | bytes 2621440 | tf_op jit(solution)/shard_map/all_to_all | solution.py:83
  24.1 255.6 %reduce-scatter.2.cloned.1.call-start = ((), (), s32[]{:S(2)}) async-start(), calls=%async_computation.5 | async-start | bytes 3276800 | tf_op jit(solution)/shard_map/reduce_scatter | solution.py:109
  283.9 13.8 %all-to-all-start.3 = ((bf16[4,2,40960]{2,1,0:T(2,128)(2,1)}), bf16[4,2,40960]{2,1,0:T(2,128)(2,1)S(1)}, u32[]{:S(2)}, u32[]{:S(2)}) async-start(bf16[4,2,40960]{2,1,0:T(2,128)(2,1)} %reshape.321), calls=%async_computation.4 | async-start | bytes 1310720 | tf_op jit(solution)/shard_map/all_to_all | solution.py:126
Sparse Core Ops, SparseCore 0:
  11.7 171.7 all-gather.2
  213.4 66.2 reduce-scatter.1
where the time goes:
time: 309 us; the launch traced here: 307 us
  waiting for transfers between devices  154 us (50%)
  blocking collectives  73.7 us (24%)
  local copies, waits for them, and re-layouts  31 us (10%)
  matrix products  14.9 us (5%)
  between operations  13.6 us (4%)
  other arithmetic  10.8 us (3%)
  starting transfers between devices  8.81 us (3%)
    all_to_all x2, blocking collectives, sent_to_all(): lax.all_to_all(jnp.broadcast_to(shard[None], (length, *shard.shape)), axi...  73.7 us
    all_gather x1, waiting for transfers between devices, rows_first(): out = lax.all_gather(both, axis, axis=0, tiled=True)  67.2 us
    reduce_scatter x1, waiting for transfers between devices, local(): lax.psum_scatter(partial_value.astype(jnp.bfloat16), 'tensor', scatter_di...  66 us
    all_to_all x1, waiting for transfers between devices, local(): lax.all_to_all(outbound, 'bal', split_axis=0, concat_axis=0, tiled=True)  11 us
    all_to_all x1, waiting for transfers between devices, local(): lax.all_to_all(outgoing, 'bal', split_axis=0, concat_axis=0, tiled=True)  9.76 us
    split x2, local copies, waits for them, and re-layouts, rows_first(): jnp.split(out, [sum(widths[:k]) for k in range(1, len(widths))], axis=1)  7.82 us
    unnamed x6, local copies, waits for them, and re-layouts  6.55 us
  transfers between devices with their start and end apart: 4, of which 4 were waited for; matrix products, arithmetic and copies ran while one was open for 6% of the time, Pallas kernels for 0%

commit v1 on v0

v1 whole, which is shorter than its diff:
```python
import functools

import jax
import jax.numpy as jnp
from jax import lax
from jax.experimental import pallas as pl
from jax.experimental.pallas import tpu as pltpu
from jax.sharding import Mesh, PartitionSpec as P

D = 1280
HDIM = 80
PATCH = 128
SLOTS = 16
LOCAL = 2
WIDTH = LOCAL * HDIM
EPSILON = 1e-06
VMEM = 48 * 2**20


def vmem_params():
    return pltpu.CompilerParams(vmem_limit_bytes=VMEM)


def rotate_body(start_ref, tiles_ref, out_ref):
    start = start_ref[0]

    def one(slot, carry):
        out_ref[(slot + start) & (SLOTS - 1)] = tiles_ref[slot]
        return carry

    lax.fori_loop(0, SLOTS, one, 0)


def rotate(tiles, start):
    return pl.pallas_call(
        rotate_body,
        out_shape=jax.ShapeDtypeStruct(tiles.shape, tiles.dtype),
        in_specs=[pl.BlockSpec(memory_space=pltpu.SMEM), pl.BlockSpec(memory_space=pltpu.VMEM)],
        out_specs=pl.BlockSpec(memory_space=pltpu.VMEM),
        compiler_params=vmem_params(),
        name="rotate",
    )(start, tiles)


def normalise_body(pick_ref, tile_ref, source_ref, normed_ref):
    tile = tile_ref[0]
    source_ref[0] = tile
    values = tile.astype(jnp.float32)
    center = values - jnp.mean(values, axis=0, keepdims=True)
    spread = jnp.mean(center * center, axis=0, keepdims=True)
    normed_ref[0] = (center * lax.rsqrt(spread + EPSILON)).T.astype(jnp.bfloat16)


def normalise(arrived, pick):
    return pl.pallas_call(
        normalise_body,
        out_shape=(
            jax.ShapeDtypeStruct((2, D, PATCH), jnp.bfloat16),
            jax.ShapeDtypeStruct((2, PATCH, D), jnp.bfloat16),
        ),
        grid_spec=pltpu.PrefetchScalarGridSpec(
            num_scalar_prefetch=1,
            grid=(2,),
            in_specs=[pl.BlockSpec((1, D, PATCH), lambda j, pick: (pick[j], 0, 0))],
            out_specs=(
                pl.BlockSpec((1, D, PATCH), lambda j, pick: (j, 0, 0)),
                pl.BlockSpec((1, PATCH, D), lambda j, pick: (j, 0, 0)),
            ),
        ),
        compiler_params=vmem_params(),
        name="normalise",
    )(pick, arrived)


def attend(qkv):
    contexts = []
    for head in range(LOCAL):
        low = head * HDIM
        query = qkv[low : low + HDIM]
        key = qkv[WIDTH + low : WIDTH + low + HDIM]
        value = qkv[2 * WIDTH + low : 2 * WIDTH + low + HDIM]
        scores = lax.dot_general(
            key, query, (((0,), (0,)), ((), ())), preferred_element_type=jnp.float32
        ) * HDIM ** (-0.5)
        weights = jnp.exp(scores - jnp.max(scores, axis=0, keepdims=True))
        probs = (weights / jnp.sum(weights, axis=0, keepdims=True)).astype(jnp.bfloat16)
        contexts.append(jnp.dot(value, probs, preferred_element_type=jnp.float32))
    return jnp.concatenate(contexts, axis=0).astype(jnp.bfloat16)


def encode_body(own_ref, other_ref, weight_ref, own_out_ref, other_out_ref, total_ref):
    step = pl.program_id(0)
    weight = weight_ref[...].reshape(D, 4 * WIDTH)
    into = weight[:, : 3 * WIDTH]
    out = weight[:, 3 * WIDTH :]
    contexts = []
    for normed_ref in (own_ref, other_ref):
        normed = normed_ref[...].reshape(2 * PATCH, D)
        projected = jnp.dot(normed, into, preferred_element_type=jnp.float32)
        projected = projected.T.astype(jnp.bfloat16)
        for tile in range(2):
            contexts.append(attend(projected[:, tile * PATCH : (tile + 1) * PATCH]))
    context = jnp.concatenate(contexts, axis=1)
    partial_value = jnp.dot(out, context, preferred_element_type=jnp.float32)

    @pl.when(step == 0)
    def _():
        total_ref[...] = partial_value

    @pl.when(step > 0)
    def _():
        total_ref[...] += partial_value

    @pl.when(step == pl.num_programs(0) - 1)
    def _():
        for tile in range(4):
            target = (own_out_ref, other_out_ref)[tile // 2]
            block = total_ref[:, tile * PATCH : (tile + 1) * PATCH]
            target[tile % 2] = block.astype(jnp.bfloat16)


def encode(own, other, weights):
    steps = weights.shape[1]
    whole = pl.BlockSpec((2, PATCH, D), lambda s: (0, 0, 0))
    result = pl.BlockSpec((2, D, PATCH), lambda s: (0, 0, 0))
    part = jax.ShapeDtypeStruct((2, D, PATCH), jnp.bfloat16)
    return pl.pallas_call(
        encode_body,
        out_shape=(part, part),
        grid=(steps,),
        in_specs=[
            whole,
            whole,
            pl.BlockSpec(
                (weights.shape[0], 1, *weights.shape[2:]), lambda s: (0, s, 0, 0)
            ),
        ],
        out_specs=(result, result),
        scratch_shapes=[pltpu.VMEM((D, 4 * PATCH), jnp.float32)],
        compiler_params=vmem_params(),
        name="encode",
    )(own, other, weights)


def layout(counts, ordering):
    doc_ids = jnp.arange(counts.shape[0], dtype=jnp.int32)
    position = jnp.sum(
        jnp.where(ordering[None, :] == doc_ids[:, None], doc_ids[None, :], 0), axis=1
    )
    starts = jnp.sum(jnp.where(position[None, :] < position[:, None], counts[None, :], 0), axis=1)
    return doc_ids, starts


def local(tiles, tile_counts, doc_order, qkv_weight, out_weight):
    bal_hi, bal_lo = lax.axis_index("bal_hi"), lax.axis_index("bal_lo")
    tensor = lax.axis_index("tensor")
    swap = [(0, 1), (1, 0)]

    rows = qkv_weight.shape[1]
    kinds = [qkv_weight[k] for k in range(3)] + [out_weight]
    halves = jnp.stack(
        [
            jnp.concatenate([w[:, c * WIDTH : (c + 1) * WIDTH] for w in kinds], axis=1)
            for c in range(2)
        ]
    )
    outgoing = jnp.broadcast_to(halves[None, :, None], (2, 2, 4, rows, 4 * WIDTH))
    ring = lax.all_to_all(
        outgoing.reshape(16, rows, 4 * WIDTH), ("y_hi", "core", "tensor"), 0, 0, tiled=True
    )
    ring = ring.reshape(2, 2, 4, rows, 4 * WIDTH).transpose(2, 0, 1, 3, 4)
    ring = ring.reshape(4 * 4 * rows, 4 * WIDTH)
    weights = lax.all_gather(ring, "z", axis=0, tiled=True)
    weights = weights.reshape(-1, 4, 4 * rows, 4 * WIDTH)

    counts = tile_counts[0]
    doc_ids, starts = layout(counts, doc_order[0])
    ends = starts + counts
    own_start = jnp.sum(jnp.where(doc_ids == bal_hi * 2 + bal_lo, starts, 0))
    outbound = rotate(tiles[0, 0], own_start.reshape(1))
    outbound, ring = lax.optimization_barrier((outbound, ring))
    arrived = lax.all_to_all(outbound, ("bal_lo", "bal_hi", "tensor"), 0, 0, tiled=True)
    place = bal_lo * 8 + bal_hi * 4 + tensor
    packed = place + jnp.arange(2, dtype=jnp.int32) * SLOTS
    inside = (starts[None, :] <= packed[:, None]) & (packed[:, None] < ends[None, :])
    doc = jnp.sum(jnp.where(inside, doc_ids[None, :], 0), axis=1)
    source, normed = normalise(arrived.reshape(4, D, PATCH), doc % 2 * 2 + doc // 2)
    other = lax.ppermute(normed, "core", swap)

    own_part, other_part = encode(normed, other, weights)
    back_part = lax.ppermute(other_part, "core", swap)
    encoded = (
        source.astype(jnp.float32) + own_part.astype(jnp.float32) + back_part.astype(jnp.float32)
    ).astype(jnp.bfloat16)
    returned = lax.all_to_all(
        encoded.reshape(8, D // 4, PATCH), ("bal_hi", "tensor"), 0, 0, tiled=True
    )
    return returned[None]


def solution(mesh):
    z = mesh.shape["dp"] // 4
    devices = mesh.devices.reshape(z, 2, 2, 2, 2, 4)
    fine = Mesh(devices, ("z", "y_hi", "core", "bal_hi", "bal_lo", "tensor"))
    dp, bal = ("z", "y_hi", "core"), ("bal_hi", "bal_lo")
    placed = (
        P(dp, bal, None, "tensor", None),
        P(dp, None),
        P(dp, None),
        P(None, dp, "tensor"),
        P(dp, "tensor"),
    )
    return jax.shard_map(
        local, mesh=fine, in_specs=placed, out_specs=P(dp, bal, "tensor", None), check_vma=False
    )
```

time: 309 us -> 180 us (0.58)
  waiting for transfers between devices: 154 us -> 78.9 us
  local copies, waits for them, and re-layouts: 31 us -> 3.82 us
  blocking collectives: 73.7 us -> 56 us
  Pallas kernels: 0 us -> 16.2 us
  matrix products: 14.9 us -> 0 us
  other arithmetic: 10.8 us -> 1.58 us
    reduce_scatter x1 -> x0, waiting for transfers between devices: 66 us -> none  [local(): lax.psum_scatter(partial_value.astype(jnp.bfloat16), 'tensor', scatter_di...]
    all_gather x1, waiting for transfers between devices: 67.2 us -> 41.9 us  [local(): weights = lax.all_gather(ring, 'z', axis=0, tiled=True)]
    all_to_all x2, blocking collectives: 73.7 us -> 56 us  [the longest x1 30.6 us: local(): lax.all_to_all(outgoing.reshape(16, rows, 4 * WIDTH), ('y_hi', 'core', 't...]
    pallas_call x0 -> x3, Pallas kernels: none -> 16.2 us  [the longest x1 12.7 us: encode(): pl.pallas_call(encode_body, out_shape=(part, part), grid=(steps,), in_spe...]
    all_to_all x2 -> x1, waiting for transfers between devices: 20.7 us -> 33.6 us  [local(): lax.all_to_all(outbound, ('bal_lo', 'bal_hi', 'tensor'), 0, 0, tiled=True)]
    dot_general x3 -> x0, matrix products: 11.6 us -> none  [the longest x1 5.18 us: local(): jnp.einsum('cdp,kdf->kcfp', normed, full_qkv, preferred_element_type=jnp....]
    split x2 -> x0, local copies, waits for them, and re-layouts: 7.82 us -> none  [rows_first(): jnp.split(out, [sum(widths[:k]) for k in range(1, len(widths))], axis=1)]
    gather x5 -> x0, local copies, waits for them, and re-layouts: 7.3 us -> none  [the longest x2 3.36 us: local(): outbound = jnp.take(own_tiles, tile_pick, axis=0) * is_live[:, None, None]]
  transfers between devices with their start and end apart: 4 -> 4, of which waited for: 4 -> 4; matrix products, arithmetic and copies ran while one was open for 6% -> 1% of each run, Pallas kernels for 0% -> 2%
where the time goes in v1:
time: 180 us
  waiting for transfers between devices  78.9 us (44%)
  blocking collectives  56 us (31%)
  Pallas kernels  16.2 us (9%)
  between operations  13.5 us (8%)
  starting transfers between devices  9.96 us (6%)
  local copies, waits for them, and re-layouts  3.82 us (2%)
    all_gather x1, waiting for transfers between devices, local(): weights = lax.all_gather(ring, 'z', axis=0, tiled=True)  41.9 us
    all_to_all x1, waiting for transfers between devices, local(): lax.all_to_all(outbound, ('bal_lo', 'bal_hi', 'tensor'), 0, 0, tiled=True)  33.6 us
    all_to_all x1, blocking collectives, local(): lax.all_to_all(outgoing.reshape(16, rows, 4 * WIDTH), ('y_hi', 'core', 't...  30.6 us
    all_to_all x1, blocking collectives, local(): lax.all_to_all(encoded.reshape(8, D // 4, PATCH), ('bal_hi', 'tensor'), 0...  25.4 us
    pallas_call x1, Pallas kernels, encode(): pl.pallas_call(encode_body, out_shape=(part, part), grid=(steps,), in_spe...  12.7 us
    all_to_all x1, starting transfers between devices, local(): lax.all_to_all(outbound, ('bal_lo', 'bal_hi', 'tensor'), 0, 0, tiled=True)  4.7 us
  transfers between devices with their start and end apart: 4, of which 4 were waited for; matrix products, arithmetic and copies ran while one was open for 1% of the time, Pallas kernels for 2%

profile of v1, /device:TPU:1, one launch (start us, length us, event | category | flops | bytes accessed | tf_op | source)
XLA Modules:
  0.0 180.0 jit_solution(13441257036601761593)
XLA Ops:
  6.5 0.9 fusion.8
  7.4 0.8 slice_bitcast_fusion.2
  8.4 0.1 maximum_bitcast_fusion
  8.6 30.6 %all_to_all.15 = bf16[16,20,640]{2,1,0:T(8,128)(2,1)S(1)} all-to-all(bf16[16,20,640]{2,1,0:T(8,128)(2,1)S(1)} %bitcast.35), channel_id=1, replica_groups=mesh['z'=16,'y_hi'=2,'core'=2,'bal_hi'=2,'bal_lo'=2,'tensor'=4] {'y_hi',..., dimensions={0} | all-to-all | bytes 819200 | tf_op jit(solution)/shard_map/all_to_all | solution.py:168
  39.2 0.2 copy.14
  39.4 0.1 copy.11
  39.4 0.8 reshape.34
  40.3 0.1 select_reduce_fusion.1
  40.4 0.2 select_reduce_fusion
  40.6 0.7 fusion.3
  41.3 1.8 %rotate.1 = bf16[16,320,128]{2,1,0:T(8,128)(2,1)} custom-call(s32[1]{0:T(128)} %bitcast.4.start_ref, bf16[16,320,128]{2,1,0:T(8,128)(2,1)S(1)} %bitcast.30), custom_call_target="tpu_custom_call" | custom-call | tf_op jit(solution)/shard_map/rotate/pallas_call | solution.py:35
  43.1 4.7 %all-to-all-start.1 = ((bf16[16,320,128]{2,1,0:T(8,128)(2,1)}), bf16[16,320,128]{2,1,0:T(8,128)(2,1)S(1)}, u32[]{:S(2)}, u32[]{:S(2)}) async-start(bf16[16,320,128]{2,1,0:T(8,128)(2,1)} %rotate.1), calls=%async_computation.1 | async-start | bytes 2621440 | tf_op jit(solution)/shard_map/all_to_all | solution.py:182
  47.9 0.2 fusion
  48.1 33.6 %all-to-all-done.1 = bf16[16,320,128]{2,1,0:T(8,128)(2,1)S(1)} async-done(((bf16[16,320,128]{2,1,0:T(8,128)(2,1)}), bf16[16,320,128]{2,1,0:T(8,128)(2,1)S(1)}, u32[]{:S(2)}, u32[]{:S(2)}) %all-to-all-start.1) | async-done | bytes 1310752 | tf_op jit(solution)/shard_map/all_to_all | solution.py:182
  81.6 1.7 normalise.1
  83.4 2.5 %collective-permute-start = (bf16[2,128,1280]{2,1,0:T(8,128)(2,1)S(1)}, bf16[2,128,1280]{2,1,0:T(8,128)(2,1)S(1)}, u32[]{:S(2)}, u32[]{:S(2)}) collective-permute-start(bf16[2,128,1280]{2,1,0:T(8,128)(2,1)S(1)} %get-tuple-element.12.own_ref), channel_id=1, source_target_pairs={{0,16},{16,0},{1,17},{17,1},{2,18},{18,2},{3,19},{19,3},{4,20},{20... | collective-permute-start | bytes 1966088 | tf_op jit(solution)/shard_map/ppermute | solution.py:188
  85.9 1.7 collective-permute-done.other_ref
  87.7 41.9 %all-gather.2.cloned.1.call-done = bf16[5120,640]{1,0:T(8,128)(2,1)} async-done(((bf16[320,640]{1,0:T(8,128)(2,1)}), bf16[5120,640]{1,0:T(8,128)(2,1)}) %all-gather.2.cloned.1.call-update) | async-done | bytes 6553616 | tf_op jit(solution)/shard_map/all_gather | solution.py:173
  129.5 12.7 %encode.1 = (bf16[2,1280,128]{2,1,0:T(8,128)(2,1)S(1)}, bf16[2,1280,128]{2,1,0:T(8,128)(2,1)S(1)}) custom-call(bf16[2,128,1280]{2,1,0:T(8,128)(2,1)S(1)} %get-tuple-element.12.own_ref, bf16[2,128,1280]{2,1,0:T(8,128)(2,1)S(1)} %collective-permute-done.other_ref, bf16[16,4,80,640]{3,2,1,0:T(8,128)(2,1)} %bitcast.31), custom_call_target="tpu_custom_call" | custom-call | tf_op jit(solution)/shard_map/encode/pallas_call | solution.py:127
  142.2 2.7 %collective-permute-start.1 = (bf16[2,1280,128]{2,1,0:T(8,128)(2,1)S(1)}, bf16[2,1280,128]{2,1,0:T(8,128)(2,1)S(1)}, u32[]{:S(2)}, u32[]{:S(2)}) collective-permute-start(bf16[2,1280,128]{2,1,0:T(8,128)(2,1)S(1)} %get-tuple-element.14), channel_id=1, source_target_pairs={{0,16},{16,0},{1,17},{17,1},{2,18},{18,2},{3,19},{19,3},{4,20},{20... | collective-permute-start | bytes 1966088 | tf_op jit(solution)/shard_map/ppermute | solution.py:191
  145.0 1.7 collective-permute-done.1
  146.7 0.3 add_convert_fusion
  146.9 25.4 %all_to_all.16 = bf16[8,320,128]{2,1,0:T(8,128)(2,1)S(1)} all-to-all(bf16[8,320,128]{2,1,0:T(8,128)(2,1)S(1)} %bitcast.32), channel_id=1, replica_groups=mesh['z'=16,'y_hi'=2,'core'=2,'bal_hi'=2,'bal_lo'=2,'tensor'=4] {'bal_hi..., dimensions={0} | all-to-all | bytes 1310720 | tf_op jit(solution)/shard_map/all_to_all | solution.py:195
  172.3 0.8 copy.16
  (16 shorter events, 0.3 us)
Async XLA Ops:
  6.5 123.0 %all-gather.2.cloned.1.call-start = ((), (), s32[]{:S(2)}) async-start(), calls=%async_computation.3 | async-start | bytes 6963200 | tf_op jit(solution)/shard_map/all_gather | solution.py:173
  39.3 1.0 copy-start.2
  39.3 1.1 copy-start.1
  39.3 2.0 %copy-start = (bf16[1,1,16,320,128]{4,3,2,1,0:T(8,128)(2,1)S(1)}, bf16[1,1,16,320,128]{4,3,2,1,0:T(8,128)(2,1)}, u32[]{:S(2)}) copy-start(bf16[1,1,16,320,128]{4,3,2,1,0:T(8,128)(2,1)} %param.5) | copy-start | bytes 3932164
  43.1 38.5 %all-to-all-start.1 = ((bf16[16,320,128]{2,1,0:T(8,128)(2,1)}), bf16[16,320,128]{2,1,0:T(8,128)(2,1)S(1)}, u32[]{:S(2)}, u32[]{:S(2)}) async-start(bf16[16,320,128]{2,1,0:T(8,128)(2,1)} %rotate.1), calls=%async_computation.1 | async-start | bytes 2621440 | tf_op jit(solution)/shard_map/all_to_all | solution.py:182
  83.4 4.3 %collective-permute-start = (bf16[2,128,1280]{2,1,0:T(8,128)(2,1)S(1)}, bf16[2,128,1280]{2,1,0:T(8,128)(2,1)S(1)}, u32[]{:S(2)}, u32[]{:S(2)}) collective-permute-start(bf16[2,128,1280]{2,1,0:T(8,128)(2,1)S(1)} %get-tuple-element.12.own_ref), channel_id=1, source_target_pairs={{0,16},{16,0},{1,17},{17,1},{2,18},{18,2},{3,19},{19,3},{4,20},{20... | collective-permute-start | bytes 1966088 | tf_op jit(solution)/shard_map/ppermute | solution.py:188
  142.2 4.4 %collective-permute-start.1 = (bf16[2,1280,128]{2,1,0:T(8,128)(2,1)S(1)}, bf16[2,1280,128]{2,1,0:T(8,128)(2,1)S(1)}, u32[]{:S(2)}, u32[]{:S(2)}) collective-permute-start(bf16[2,1280,128]{2,1,0:T(8,128)(2,1)S(1)} %get-tuple-element.14), channel_id=1, source_target_pairs={{0,16},{16,0},{1,17},{17,1},{2,18},{18,2},{3,19},{19,3},{4,20},{20... | collective-permute-start | bytes 1966088 | tf_op jit(solution)/shard_map/ppermute | solution.py:191
Sparse Core Ops, SparseCore 0:
  40.4 89.0 all-gather.1

commit v2 on v1

--- a/solution.py
+++ b/solution.py
@@ -11,10 +11,11 @@
 HDIM = 80
 PATCH = 128
 SLOTS = 16
+BLOCKS = 16
 LOCAL = 2
 WIDTH = LOCAL * HDIM
 EPSILON = 1e-06
-VMEM = 48 * 2**20
+VMEM = 24 * 2**20
 
 
 def vmem_params():
@@ -88,58 +89,84 @@
     return jnp.concatenate(contexts, axis=0).astype(jnp.bfloat16)
 
 
-def encode_body(own_ref, other_ref, weight_ref, own_out_ref, other_out_ref, total_ref):
-    step = pl.program_id(0)
-    weight = weight_ref[...].reshape(D, 4 * WIDTH)
-    into = weight[:, : 3 * WIDTH]
-    out = weight[:, 3 * WIDTH :]
-    contexts = []
-    for normed_ref in (own_ref, other_ref):
-        normed = normed_ref[...].reshape(2 * PATCH, D)
-        projected = jnp.dot(normed, into, preferred_element_type=jnp.float32)
-        projected = projected.T.astype(jnp.bfloat16)
-        for tile in range(2):
-            contexts.append(attend(projected[:, tile * PATCH : (tile + 1) * PATCH]))
-    context = jnp.concatenate(contexts, axis=1)
-    partial_value = jnp.dot(out, context, preferred_element_type=jnp.float32)
-
-    @pl.when(step == 0)
-    def _():
-        total_ref[...] = partial_value
-
-    @pl.when(step > 0)
-    def _():
-        total_ref[...] += partial_value
-
-    @pl.when(step == pl.num_programs(0) - 1)
-    def _():
-        for tile in range(4):
-            target = (own_out_ref, other_out_ref)[tile // 2]
-            block = total_ref[:, tile * PATCH : (tile + 1) * PATCH]
-            target[tile % 2] = block.astype(jnp.bfloat16)
-
-
-def encode(own, other, weights):
-    steps = weights.shape[1]
-    whole = pl.BlockSpec((2, PATCH, D), lambda s: (0, 0, 0))
-    result = pl.BlockSpec((2, D, PATCH), lambda s: (0, 0, 0))
+def block_z(where_ref, k):
+    hop = (k + 1) // 2 * (1 if k % 2 else -1)
+    return (where_ref[0] + where_ref[1] * hop) & (BLOCKS - 1)
+
+
+def encode_body(where_ref, own_ref, other_ref, *refs):
+    blocks = refs[:BLOCKS]
+    own_out_ref, other_out_ref, weight_ref, total_ref, sems = refs[BLOCKS:]
+    group_count = weight_ref.shape[1]
+
+    def copies(group):
+        return [
+            pltpu.make_async_copy(
+                block.at[group], weight_ref.at[block_z(where_ref, k), group], sems.at[group, k]
+            )
+            for k, block in enumerate(blocks)
+        ]
+
+    for group in range(group_count):
+        for copy in copies(group):
+            copy.start()
+    for group in range(group_count):
+        for copy in copies(group):
+            copy.wait()
+        weight = weight_ref[:, group].reshape(D, 4 * WIDTH)
+        into = weight[:, : 3 * WIDTH]
+        out = weight[:, 3 * WIDTH :]
+        contexts = []
+        for normed_ref in (own_ref, other_ref):
+            normed = normed_ref[...].reshape(2 * PATCH, D)
+            projected = jnp.dot(normed, into, preferred_element_type=jnp.float32)
+            projected = projected.T.astype(jnp.bfloat16)
+            for tile in range(2):
+                contexts.append(attend(projected[:, tile * PATCH : (tile + 1) * PATCH]))
+        context = jnp.concatenate(contexts, axis=1)
+        partial_value = jnp.dot(out, context, preferred_element_type=jnp.float32)
+        if group == 0:
+            total_ref[...] = partial_value
+        else:
+            total_ref[...] += partial_value
+    for tile in range(4):
+        target = (own_out_ref, other_out_ref)[tile // 2]
+        block = total_ref[:, tile * PATCH : (tile + 1) * PATCH]
+        target[tile % 2] = block.astype(jnp.bfloat16)
+
+
+def encode(where, own, other, blocks):
+    in_vmem = pl.BlockSpec(memory_space=pltpu.VMEM)
     part = jax.ShapeDtypeStruct((2, D, PATCH), jnp.bfloat16)
+    group_count = blocks[0].shape[0]
     return pl.pallas_call(
         encode_body,
         out_shape=(part, part),
-        grid=(steps,),
-        in_specs=[
-            whole,
-            whole,
-            pl.BlockSpec(
-                (weights.shape[0], 1, *weights.shape[2:]), lambda s: (0, s, 0, 0)
-            ),
+        in_specs=[pl.BlockSpec(memory_space=pltpu.SMEM), in_vmem, in_vmem]
+        + [pl.BlockSpec(memory_space=pl.ANY)] * len(blocks),
+        out_specs=(in_vmem, in_vmem),
+        scratch_shapes=[
+            pltpu.VMEM((BLOCKS, *blocks[0].shape), jnp.bfloat16),
+            pltpu.VMEM((D, 4 * PATCH), jnp.float32),
+            pltpu.SemaphoreType.DMA((group_count, BLOCKS)),
         ],
-        out_specs=(result, result),
-        scratch_shapes=[pltpu.VMEM((D, 4 * PATCH), jnp.float32)],
         compiler_params=vmem_params(),
         name="encode",
-    )(own, other, weights)
+    )(where, own, other, *[pltpu.with_memory_space_constraint(b, pltpu.HBM) for b in blocks])
+
+
+def around_z(block):
+    length = lax.axis_size("z")
+    ways = (
+        [(2 * i + c, (i + 1 - 2 * c) % length * 2 + c) for i in range(length) for c in range(2)],
+        [(2 * i + c, (i - 1 + 2 * c) % length * 2 + c) for i in range(length) for c in range(2)],
+    )
+    held, blocks = [block, block], [block]
+    for hop in range(1, length // 2 + 1):
+        for chain in range(2 if 2 * hop < length else 1):
+            held[chain] = lax.ppermute(held[chain], ("z", "core"), ways[chain])
+            blocks.append(held[chain])
+    return blocks
 
 
 def layout(counts, ordering):
@@ -168,10 +195,8 @@
     ring = lax.all_to_all(
         outgoing.reshape(16, rows, 4 * WIDTH), ("y_hi", "core", "tensor"), 0, 0, tiled=True
     )
-    ring = ring.reshape(2, 2, 4, rows, 4 * WIDTH).transpose(2, 0, 1, 3, 4)
-    ring = ring.reshape(4 * 4 * rows, 4 * WIDTH)
-    weights = lax.all_gather(ring, "z", axis=0, tiled=True)
-    weights = weights.reshape(-1, 4, 4 * rows, 4 * WIDTH)
+    block = ring.reshape(2, 2, 4, rows, 4 * WIDTH).transpose(2, 0, 1, 3, 4)
+    blocks = around_z(block.reshape(4, 4 * rows, 4 * WIDTH))
 
     counts = tile_counts[0]
     doc_ids, starts = layout(counts, doc_order[0])
@@ -187,7 +212,8 @@
     source, normed = normalise(arrived.reshape(4, D, PATCH), doc % 2 * 2 + doc // 2)
     other = lax.ppermute(normed, "core", swap)
 
-    own_part, other_part = encode(normed, other, weights)
+    where = jnp.stack([lax.axis_index("z"), 2 * lax.axis_index("core") - 1]).astype(jnp.int32)
+    own_part, other_part = encode(where, normed, other, blocks)
     back_part = lax.ppermute(other_part, "core", swap)
     encoded = (
         source.astype(jnp.float32) + own_part.astype(jnp.float32) + back_part.astype(jnp.float32)

time: 180 us -> 193 us (1.072)
  starting transfers between devices: 9.96 us -> 75.4 us
  waiting for transfers between devices: 78.9 us -> 36.5 us
  between operations: 13.5 us -> 0.41 us
  blocking collectives: 56 us -> 58.5 us
    ppermute x0 -> x15, starting transfers between devices: none -> 56.5 us  [around_z(): held[chain] = lax.ppermute(held[chain], ('z', 'core'), ways[chain])]
    all_gather x1 -> x0, waiting for transfers between devices: 41.9 us -> none  [local(): weights = lax.all_gather(ring, 'z', axis=0, tiled=True)]
    ppermute x0 -> x15, waiting for transfers between devices: none -> 34.8 us  [around_z(): held[chain] = lax.ppermute(held[chain], ('z', 'core'), ways[chain])]
    all_to_all x1, waiting for transfers between devices: 33.6 us -> 0.01 us  [local(): lax.all_to_all(outbound, ('bal_lo', 'bal_hi', 'tensor'), 0, 0, tiled=True)]
    ppermute x1, starting transfers between devices: 2.55 us -> 6.18 us  [local(): other = lax.ppermute(normed, 'core', swap)]
    ppermute x1, starting transfers between devices: 2.71 us -> 5.45 us  [local(): back_part = lax.ppermute(other_part, 'core', swap)]
    all_to_all x1, starting transfers between devices: 4.7 us -> 7.24 us  [local(): lax.all_to_all(outbound, ('bal_lo', 'bal_hi', 'tensor'), 0, 0, tiled=True)]
    all_to_all x1, blocking collectives: 25.4 us -> 27.8 us  [local(): lax.all_to_all(encoded.reshape(8, D // 4, PATCH), ('bal_hi', 'tensor'), 0...]
  transfers between devices with their start and end apart: 4 -> 18, of which waited for: 4 -> 10; matrix products, arithmetic and copies ran while one was open for 1% -> 1% of each run, Pallas kernels for 2% -> 2%
where the time goes in v2:
time: 193 us; the launch traced here: 192 us
  starting transfers between devices  75.4 us (39%)
  blocking collectives  58.5 us (30%)
  waiting for transfers between devices  36.5 us (19%)
  Pallas kernels  16.7 us (9%)
  local copies, waits for them, and re-layouts  2.98 us (2%)
    ppermute x15, starting transfers between devices, around_z(): held[chain] = lax.ppermute(held[chain], ('z', 'core'), ways[chain])  56.5 us
    ppermute x15, waiting for transfers between devices, around_z(): held[chain] = lax.ppermute(held[chain], ('z', 'core'), ways[chain])  34.8 us
    all_to_all x1, blocking collectives, local(): lax.all_to_all(outgoing.reshape(16, rows, 4 * WIDTH), ('y_hi', 'core', 't...  30.7 us
    all_to_all x1, blocking collectives, local(): lax.all_to_all(encoded.reshape(8, D // 4, PATCH), ('bal_hi', 'tensor'), 0...  27.8 us
    pallas_call x1, Pallas kernels, encode(): pl.pallas_call(encode_body, out_shape=(part, part), in_specs=[pl.BlockSpe...  13.1 us
    all_to_all x1, starting transfers between devices, local(): lax.all_to_all(outbound, ('bal_lo', 'bal_hi', 'tensor'), 0, 0, tiled=True)  7.24 us
    ppermute x1, starting transfers between devices, local(): other = lax.ppermute(normed, 'core', swap)  6.18 us
    ppermute x1, starting transfers between devices, local(): back_part = lax.ppermute(other_part, 'core', swap)  5.45 us
  transfers between devices with their start and end apart: 18, of which 10 were waited for; matrix products, arithmetic and copies ran while one was open for 1% of the time, Pallas kernels for 2%

profile of v2, /device:TPU:1, one launch (start us, length us, event | category | flops | bytes accessed | tf_op | source)
XLA Modules:
  0.0 192.1 jit_solution(14569282586450194656)
XLA Ops:
  2.1 30.7 %all_to_all.15 = bf16[16,20,640]{2,1,0:T(8,128)(2,1)S(1)} all-to-all(bf16[16,20,640]{2,1,0:T(8,128)(2,1)S(1)} %bitcast.36), channel_id=1, replica_groups=mesh['z'=16,'y_hi'=2,'core'=2,'bal_hi'=2,'bal_lo'=2,'tensor'=4] {'y_hi',..., dimensions={0} | all-to-all | bytes 819200 | tf_op jit(solution)/shard_map/all_to_all | solution.py:195
  33.0 9.6 %collective-permute-start.1 = (bf16[4,80,640]{2,1,0:T(8,128)(2,1)S(1)}, bf16[4,80,640]{2,1,0:T(8,128)(2,1)S(1)}, u32[]{:S(2)}, u32[]{:S(2)}) collective-permute-start(bf16[4,80,640]{2,1,0:T(8,128)(2,1)S(1)} %copy.20.refs_0_), channel_id=1, source_target_pairs={{0,64},{16,976},{64,128},{80,16},{128,192},{144,80},{192,256},{208... | collective-permute-start | bytes 1228808 | tf_op jit(solution)/shard_map/ppermute | solution.py:167
  45.6 7.2 %all-to-all-start.1 = ((bf16[16,320,128]{2,1,0:T(8,128)(2,1)}), bf16[16,320,128]{2,1,0:T(8,128)(2,1)S(1)}, u32[]{:S(2)}, u32[]{:S(2)}) async-start(bf16[16,320,128]{2,1,0:T(8,128)(2,1)} %rotate.1), calls=%async_computation.1 | async-start | bytes 2621440 | tf_op jit(solution)/shard_map/all_to_all | solution.py:207
  52.8 1.9 collective-permute-start.2
  54.8 4.6 %collective-permute-start.3 = (bf16[4,80,640]{2,1,0:T(8,128)(2,1)S(1)}, bf16[4,80,640]{2,1,0:T(8,128)(2,1)S(1)}, u32[]{:S(2)}, u32[]{:S(2)}) collective-permute-start(bf16[4,80,640]{2,1,0:T(8,128)(2,1)S(1)} %collective-permute-done.1.refs_1_), channel_id=1, source_target_pairs={{0,64},{16,976},{64,128},{80,16},{128,192},{144,80},{192,256},{208... | collective-permute-start | bytes 1228808 | tf_op jit(solution)/shard_map/ppermute | solution.py:167
  59.3 5.5 %collective-permute-done.2.refs_2_ = bf16[4,80,640]{2,1,0:T(8,128)(2,1)S(1)} collective-permute-done((bf16[4,80,640]{2,1,0:T(8,128)(2,1)S(1)}, bf16[4,80,640]{2,1,0:T(8,128)(2,1)S(1)}, u32[]{:S(2)}, u32[]{:S(2)}) %collective-permute-start.2) | collective-permute-done | bytes 409632 | tf_op jit(solution)/shard_map/ppermute | solution.py:167
  66.8 4.6 %collective-permute-start.5 = (bf16[4,80,640]{2,1,0:T(8,128)(2,1)S(1)}, bf16[4,80,640]{2,1,0:T(8,128)(2,1)S(1)}, u32[]{:S(2)}, u32[]{:S(2)}) collective-permute-start(bf16[4,80,640]{2,1,0:T(8,128)(2,1)S(1)} %collective-permute-done.3.refs_3_), channel_id=1, source_target_pairs={{0,64},{16,976},{64,128},{80,16},{128,192},{144,80},{192,256},{208... | collective-permute-start | bytes 1228808 | tf_op jit(solution)/shard_map/ppermute | solution.py:167
  71.3 4.6 %collective-permute-done.4.refs_4_ = bf16[4,80,640]{2,1,0:T(8,128)(2,1)S(1)} collective-permute-done((bf16[4,80,640]{2,1,0:T(8,128)(2,1)S(1)}, bf16[4,80,640]{2,1,0:T(8,128)(2,1)S(1)}, u32[]{:S(2)}, u32[]{:S(2)}) %collective-permute-start.4) | collective-permute-done | bytes 409632 | tf_op jit(solution)/shard_map/ppermute | solution.py:167
  77.8 4.6 %collective-permute-start.7 = (bf16[4,80,640]{2,1,0:T(8,128)(2,1)S(1)}, bf16[4,80,640]{2,1,0:T(8,128)(2,1)}, u32[]{:S(2)}, u32[]{:S(2)}) collective-permute-start(bf16[4,80,640]{2,1,0:T(8,128)(2,1)S(1)} %collective-permute-done.5.refs_5_), channel_id=1, source_target_pairs={{0,64},{16,976},{64,128},{80,16},{128,192},{144,80},{192,256},{208... | collective-permute-start | bytes 1228808 | tf_op jit(solution)/shard_map/ppermute | solution.py:167
  82.4 3.5 %collective-permute-done.6.refs_6_ = bf16[4,80,640]{2,1,0:T(8,128)(2,1)} collective-permute-done((bf16[4,80,640]{2,1,0:T(8,128)(2,1)S(1)}, bf16[4,80,640]{2,1,0:T(8,128)(2,1)}, u32[]{:S(2)}, u32[]{:S(2)}) %collective-permute-start.6) | collective-permute-done | bytes 409632 | tf_op jit(solution)/shard_map/ppermute | solution.py:167
  87.8 4.6 %collective-permute-start.9 = (bf16[4,80,640]{2,1,0:T(8,128)(2,1)}, bf16[4,80,640]{2,1,0:T(8,128)(2,1)}, u32[]{:S(2)}, u32[]{:S(2)}) collective-permute-start(bf16[4,80,640]{2,1,0:T(8,128)(2,1)} %collective-permute-done.7.refs_7_), channel_id=1, source_target_pairs={{0,64},{16,976},{64,128},{80,16},{128,192},{144,80},{192,256},{208... | collective-permute-start | bytes 1228808 | tf_op jit(solution)/shard_map/ppermute | solution.py:167
  92.4 3.7 %collective-permute-done.8.refs_8_ = bf16[4,80,640]{2,1,0:T(8,128)(2,1)} collective-permute-done((bf16[4,80,640]{2,1,0:T(8,128)(2,1)}, bf16[4,80,640]{2,1,0:T(8,128)(2,1)}, u32[]{:S(2)}, u32[]{:S(2)}) %collective-permute-start.8) | collective-permute-done | bytes 409632 | tf_op jit(solution)/shard_map/ppermute | solution.py:167
  98.0 2.5 %collective-permute-done.9.refs_9_ = bf16[4,80,640]{2,1,0:T(8,128)(2,1)} collective-permute-done((bf16[4,80,640]{2,1,0:T(8,128)(2,1)}, bf16[4,80,640]{2,1,0:T(8,128)(2,1)}, u32[]{:S(2)}, u32[]{:S(2)}) %collective-permute-start.9) | collective-permute-done | bytes 409632 | tf_op jit(solution)/shard_map/ppermute | solution.py:167
  100.6 5.0 %collective-permute-start.11 = (bf16[4,80,640]{2,1,0:T(8,128)(2,1)}, bf16[4,80,640]{2,1,0:T(8,128)(2,1)}, u32[]{:S(2)}, u32[]{:S(2)}) collective-permute-start(bf16[4,80,640]{2,1,0:T(8,128)(2,1)} %collective-permute-done.9.refs_9_), channel_id=1, source_target_pairs={{0,64},{16,976},{64,128},{80,16},{128,192},{144,80},{192,256},{208... | collective-permute-start | bytes 1228808 | tf_op jit(solution)/shard_map/ppermute | solution.py:167
  108.5 5.7 %collective-permute-done.11.refs_11_ = bf16[4,80,640]{2,1,0:T(8,128)(2,1)} collective-permute-done((bf16[4,80,640]{2,1,0:T(8,128)(2,1)}, bf16[4,80,640]{2,1,0:T(8,128)(2,1)}, u32[]{:S(2)}, u32[]{:S(2)}) %collective-permute-start.11) | collective-permute-done | bytes 409632 | tf_op jit(solution)/shard_map/ppermute | solution.py:167
  114.2 5.3 %collective-permute-start.13 = (bf16[4,80,640]{2,1,0:T(8,128)(2,1)}, bf16[4,80,640]{2,1,0:T(8,128)(2,1)}, u32[]{:S(2)}, u32[]{:S(2)}) collective-permute-start(bf16[4,80,640]{2,1,0:T(8,128)(2,1)} %collective-permute-done.11.refs_11_), channel_id=1, source_target_pairs={{0,64},{16,976},{64,128},{80,16},{128,192},{144,80},{192,256},{208... | collective-permute-start | bytes 1228808 | tf_op jit(solution)/shard_map/ppermute | solution.py:167
  121.4 6.2 %collective-permute-start = (bf16[2,128,1280]{2,1,0:T(8,128)(2,1)S(1)}, bf16[2,128,1280]{2,1,0:T(8,128)(2,1)S(1)}, u32[]{:S(2)}, u32[]{:S(2)}) collective-permute-start(bf16[2,128,1280]{2,1,0:T(8,128)(2,1)S(1)} %get-tuple-element.12.own_ref), channel_id=1, source_target_pairs={{0,16},{16,0},{1,17},{17,1},{2,18},{18,2},{3,19},{19,3},{4,20},{20... | collective-permute-start | bytes 1966088 | tf_op jit(solution)/shard_map/ppermute | solution.py:213
  127.6 1.9 collective-permute-start.14
  129.5 4.9 %collective-permute-start.15 = (bf16[4,80,640]{2,1,0:T(8,128)(2,1)}, bf16[4,80,640]{2,1,0:T(8,128)(2,1)}, u32[]{:S(2)}, u32[]{:S(2)}) collective-permute-start(bf16[4,80,640]{2,1,0:T(8,128)(2,1)} %collective-permute-done.13.refs_13_), channel_id=1, source_target_pairs={{0,64},{16,976},{64,128},{80,16},{128,192},{144,80},{192,256},{208... | collective-permute-start | bytes 1228808 | tf_op jit(solution)/shard_map/ppermute | solution.py:167
  134.4 3.5 %collective-permute-done.14.refs_14_ = bf16[4,80,640]{2,1,0:T(8,128)(2,1)S(1)} collective-permute-done((bf16[4,80,640]{2,1,0:T(8,128)(2,1)}, bf16[4,80,640]{2,1,0:T(8,128)(2,1)S(1)}, u32[]{:S(2)}, u32[]{:S(2)}) %collective-permute-start.14) | collective-permute-done | bytes 409632 | tf_op jit(solution)/shard_map/ppermute | solution.py:167
  138.0 5.0 %collective-permute-done.15.refs_15_ = bf16[4,80,640]{2,1,0:T(8,128)(2,1)} collective-permute-done((bf16[4,80,640]{2,1,0:T(8,128)(2,1)}, bf16[4,80,640]{2,1,0:T(8,128)(2,1)}, u32[]{:S(2)}, u32[]{:S(2)}) %collective-permute-start.15) | collective-permute-done | bytes 409632 | tf_op jit(solution)/shard_map/ppermute | solution.py:167
  143.0 13.1 %encode.1 = (bf16[2,1280,128]{2,1,0:T(8,128)(2,1)S(1)}, bf16[2,1280,128]{2,1,0:T(8,128)(2,1)S(1)}) custom-call(s32[2]{0:T(128)S(1)} %pad_add_fusion.where_ref, bf16[2,128,1280]{2,1,0:T(8,128)(2,1)S(1)} %get-tuple-element.12.own_ref, bf16[2,128,1280]{2,1,0:T(8,128)(2,1)S(1)} %collective-permute-done.other_ref, bf16[4,80,640]{2,1,0:T(8,128)(2,1)} %copy-done.1, ...), custom_call_target="tpu_custom_call" | custom-call | tf_op jit(solution)/shard_map/encode/pallas_call | solution.py:142
  156.1 5.5 %collective-permute-start.16 = (bf16[2,1280,128]{2,1,0:T(8,128)(2,1)S(1)}, bf16[2,1280,128]{2,1,0:T(8,128)(2,1)S(1)}, u32[]{:S(2)}, u32[]{:S(2)}) collective-permute-start(bf16[2,1280,128]{2,1,0:T(8,128)(2,1)S(1)} %get-tuple-element.14), channel_id=1, source_target_pairs={{0,16},{16,0},{1,17},{17,1},{2,18},{18,2},{3,19},{19,3},{4,20},{20... | collective-permute-start | bytes 1966088 | tf_op jit(solution)/shard_map/ppermute | solution.py:217
  163.5 27.8 %all_to_all.16 = bf16[8,320,128]{2,1,0:T(8,128)(2,1)S(1)} all-to-all(bf16[8,320,128]{2,1,0:T(8,128)(2,1)S(1)} %bitcast.33), channel_id=1, replica_groups=mesh['z'=16,'y_hi'=2,'core'=2,'bal_hi'=2,'bal_lo'=2,'tensor'=4] {'bal_hi..., dimensions={0} | all-to-all | bytes 1310720 | tf_op jit(solution)/shard_map/all_to_all | solution.py:221
  (57 shorter events, 20.3 us)
Async XLA Ops:
  2.1 41.6 %copy-start = (bf16[1,1,16,320,128]{4,3,2,1,0:T(8,128)(2,1)S(1)}, bf16[1,1,16,320,128]{4,3,2,1,0:T(8,128)(2,1)}, u32[]{:S(2)}) copy-start(bf16[1,1,16,320,128]{4,3,2,1,0:T(8,128)(2,1)} %param.5) | copy-start | bytes 3932164
  33.0 21.7 %collective-permute-start.1 = (bf16[4,80,640]{2,1,0:T(8,128)(2,1)S(1)}, bf16[4,80,640]{2,1,0:T(8,128)(2,1)S(1)}, u32[]{:S(2)}, u32[]{:S(2)}) collective-permute-start(bf16[4,80,640]{2,1,0:T(8,128)(2,1)S(1)} %copy.20.refs_0_), channel_id=1, source_target_pairs={{0,64},{16,976},{64,128},{80,16},{128,192},{144,80},{192,256},{208... | collective-permute-start | bytes 1228808 | tf_op jit(solution)/shard_map/ppermute | solution.py:167
  45.6 74.0 %all-to-all-start.1 = ((bf16[16,320,128]{2,1,0:T(8,128)(2,1)}), bf16[16,320,128]{2,1,0:T(8,128)(2,1)S(1)}, u32[]{:S(2)}, u32[]{:S(2)}) async-start(bf16[16,320,128]{2,1,0:T(8,128)(2,1)} %rotate.1), calls=%async_computation.1 | async-start | bytes 2621440 | tf_op jit(solution)/shard_map/all_to_all | solution.py:207
  52.8 12.0 %collective-permute-start.2 = (bf16[4,80,640]{2,1,0:T(8,128)(2,1)S(1)}, bf16[4,80,640]{2,1,0:T(8,128)(2,1)S(1)}, u32[]{:S(2)}, u32[]{:S(2)}) collective-permute-start(bf16[4,80,640]{2,1,0:T(8,128)(2,1)S(1)} %copy.20.refs_0_), channel_id=1, source_target_pairs={{0,960},{16,80},{64,0},{80,144},{128,64},{144,208},{192,128},{208,... | collective-permute-start | bytes 1228808 | tf_op jit(solution)/shard_map/ppermute | solution.py:167
  54.8 88.2 %copy-start.2 = (bf16[4,80,640]{2,1,0:T(8,128)(2,1)}, bf16[4,80,640]{2,1,0:T(8,128)(2,1)S(1)}, u32[]{:S(2)}) copy-start(bf16[4,80,640]{2,1,0:T(8,128)(2,1)S(1)} %collective-permute-done.1.refs_1_) | copy-start | bytes 1228804
  54.8 12.0 %collective-permute-start.3 = (bf16[4,80,640]{2,1,0:T(8,128)(2,1)S(1)}, bf16[4,80,640]{2,1,0:T(8,128)(2,1)S(1)}, u32[]{:S(2)}, u32[]{:S(2)}) collective-permute-start(bf16[4,80,640]{2,1,0:T(8,128)(2,1)S(1)} %collective-permute-done.1.refs_1_), channel_id=1, source_target_pairs={{0,64},{16,976},{64,128},{80,16},{128,192},{144,80},{192,256},{208... | collective-permute-start | bytes 1228808 | tf_op jit(solution)/shard_map/ppermute | solution.py:167
  64.8 54.8 %copy-start.3 = (bf16[4,80,640]{2,1,0:T(8,128)(2,1)}, bf16[4,80,640]{2,1,0:T(8,128)(2,1)S(1)}, u32[]{:S(2)}) copy-start(bf16[4,80,640]{2,1,0:T(8,128)(2,1)S(1)} %collective-permute-done.2.refs_2_) | copy-start | bytes 1228804
  64.8 11.1 %collective-permute-start.4 = (bf16[4,80,640]{2,1,0:T(8,128)(2,1)S(1)}, bf16[4,80,640]{2,1,0:T(8,128)(2,1)S(1)}, u32[]{:S(2)}, u32[]{:S(2)}) collective-permute-start(bf16[4,80,640]{2,1,0:T(8,128)(2,1)S(1)} %collective-permute-done.2.refs_2_), channel_id=1, source_target_pairs={{0,960},{16,80},{64,0},{80,144},{128,64},{144,208},{192,128},{208,... | collective-permute-start | bytes 1228808 | tf_op jit(solution)/shard_map/ppermute | solution.py:167
  66.8 52.8 %copy-start.4 = (bf16[4,80,640]{2,1,0:T(8,128)(2,1)}, bf16[4,80,640]{2,1,0:T(8,128)(2,1)S(1)}, u32[]{:S(2)}) copy-start(bf16[4,80,640]{2,1,0:T(8,128)(2,1)S(1)} %collective-permute-done.3.refs_3_) | copy-start | bytes 1228804
  66.8 11.1 %collective-permute-start.5 = (bf16[4,80,640]{2,1,0:T(8,128)(2,1)S(1)}, bf16[4,80,640]{2,1,0:T(8,128)(2,1)S(1)}, u32[]{:S(2)}, u32[]{:S(2)}) collective-permute-start(bf16[4,80,640]{2,1,0:T(8,128)(2,1)S(1)} %collective-permute-done.3.refs_3_), channel_id=1, source_target_pairs={{0,64},{16,976},{64,128},{80,16},{128,192},{144,80},{192,256},{208... | collective-permute-start | bytes 1228808 | tf_op jit(solution)/shard_map/ppermute | solution.py:167
  75.9 67.1 %copy-start.5 = (bf16[4,80,640]{2,1,0:T(8,128)(2,1)}, bf16[4,80,640]{2,1,0:T(8,128)(2,1)S(1)}, u32[]{:S(2)}) copy-start(bf16[4,80,640]{2,1,0:T(8,128)(2,1)S(1)} %collective-permute-done.4.refs_4_) | copy-start | bytes 1228804
  75.9 10.0 %collective-permute-start.6 = (bf16[4,80,640]{2,1,0:T(8,128)(2,1)S(1)}, bf16[4,80,640]{2,1,0:T(8,128)(2,1)}, u32[]{:S(2)}, u32[]{:S(2)}) collective-permute-start(bf16[4,80,640]{2,1,0:T(8,128)(2,1)S(1)} %collective-permute-done.4.refs_4_), channel_id=1, source_target_pairs={{0,960},{16,80},{64,0},{80,144},{128,64},{144,208},{192,128},{208,... | collective-permute-start | bytes 1228808 | tf_op jit(solution)/shard_map/ppermute | solution.py:167
  77.8 41.8 %copy-start.6 = (bf16[4,80,640]{2,1,0:T(8,128)(2,1)}, bf16[4,80,640]{2,1,0:T(8,128)(2,1)S(1)}, u32[]{:S(2)}) copy-start(bf16[4,80,640]{2,1,0:T(8,128)(2,1)S(1)} %collective-permute-done.5.refs_5_) | copy-start | bytes 1228804
  77.8 10.0 %collective-permute-start.7 = (bf16[4,80,640]{2,1,0:T(8,128)(2,1)S(1)}, bf16[4,80,640]{2,1,0:T(8,128)(2,1)}, u32[]{:S(2)}, u32[]{:S(2)}) collective-permute-start(bf16[4,80,640]{2,1,0:T(8,128)(2,1)S(1)} %collective-permute-done.5.refs_5_), channel_id=1, source_target_pairs={{0,64},{16,976},{64,128},{80,16},{128,192},{144,80},{192,256},{208... | collective-permute-start | bytes 1228808 | tf_op jit(solution)/shard_map/ppermute | solution.py:167
  85.9 10.2 %collective-permute-start.8 = (bf16[4,80,640]{2,1,0:T(8,128)(2,1)}, bf16[4,80,640]{2,1,0:T(8,128)(2,1)}, u32[]{:S(2)}, u32[]{:S(2)}) collective-permute-start(bf16[4,80,640]{2,1,0:T(8,128)(2,1)} %collective-permute-done.6.refs_6_), channel_id=1, source_target_pairs={{0,960},{16,80},{64,0},{80,144},{128,64},{144,208},{192,128},{208,... | collective-permute-start | bytes 1228808 | tf_op jit(solution)/shard_map/ppermute | solution.py:167
  87.8 12.7 %collective-permute-start.9 = (bf16[4,80,640]{2,1,0:T(8,128)(2,1)}, bf16[4,80,640]{2,1,0:T(8,128)(2,1)}, u32[]{:S(2)}, u32[]{:S(2)}) collective-permute-start(bf16[4,80,640]{2,1,0:T(8,128)(2,1)} %collective-permute-done.7.refs_7_), channel_id=1, source_target_pairs={{0,64},{16,976},{64,128},{80,16},{128,192},{144,80},{192,256},{208... | collective-permute-start | bytes 1228808 | tf_op jit(solution)/shard_map/ppermute | solution.py:167
  96.1 10.5 %collective-permute-start.10 = (bf16[4,80,640]{2,1,0:T(8,128)(2,1)}, bf16[4,80,640]{2,1,0:T(8,128)(2,1)}, u32[]{:S(2)}, u32[]{:S(2)}) collective-permute-start(bf16[4,80,640]{2,1,0:T(8,128)(2,1)} %collective-permute-done.8.refs_8_), channel_id=1, source_target_pairs={{0,960},{16,80},{64,0},{80,144},{128,64},{144,208},{192,128},{208,... | collective-permute-start | bytes 1228808 | tf_op jit(solution)/shard_map/ppermute | solution.py:167
  100.6 13.7 %collective-permute-start.11 = (bf16[4,80,640]{2,1,0:T(8,128)(2,1)}, bf16[4,80,640]{2,1,0:T(8,128)(2,1)}, u32[]{:S(2)}, u32[]{:S(2)}) collective-permute-start(bf16[4,80,640]{2,1,0:T(8,128)(2,1)} %collective-permute-done.9.refs_9_), channel_id=1, source_target_pairs={{0,64},{16,976},{64,128},{80,16},{128,192},{144,80},{192,256},{208... | collective-permute-start | bytes 1228808 | tf_op jit(solution)/shard_map/ppermute | solution.py:167
  106.6 20.9 %collective-permute-start.12 = (bf16[4,80,640]{2,1,0:T(8,128)(2,1)}, bf16[4,80,640]{2,1,0:T(8,128)(2,1)}, u32[]{:S(2)}, u32[]{:S(2)}) collective-permute-start(bf16[4,80,640]{2,1,0:T(8,128)(2,1)} %collective-permute-done.10.refs_10_), channel_id=1, source_target_pairs={{0,960},{16,80},{64,0},{80,144},{128,64},{144,208},{192,128},{208,... | collective-permute-start | bytes 1228808 | tf_op jit(solution)/shard_map/ppermute | solution.py:167
  114.2 15.2 %collective-permute-start.13 = (bf16[4,80,640]{2,1,0:T(8,128)(2,1)}, bf16[4,80,640]{2,1,0:T(8,128)(2,1)}, u32[]{:S(2)}, u32[]{:S(2)}) collective-permute-start(bf16[4,80,640]{2,1,0:T(8,128)(2,1)} %collective-permute-done.11.refs_11_), channel_id=1, source_target_pairs={{0,64},{16,976},{64,128},{80,16},{128,192},{144,80},{192,256},{208... | collective-permute-start | bytes 1228808 | tf_op jit(solution)/shard_map/ppermute | solution.py:167
  121.4 16.6 %collective-permute-start = (bf16[2,128,1280]{2,1,0:T(8,128)(2,1)S(1)}, bf16[2,128,1280]{2,1,0:T(8,128)(2,1)S(1)}, u32[]{:S(2)}, u32[]{:S(2)}) collective-permute-start(bf16[2,128,1280]{2,1,0:T(8,128)(2,1)S(1)} %get-tuple-element.12.own_ref), channel_id=1, source_target_pairs={{0,16},{16,0},{1,17},{17,1},{2,18},{18,2},{3,19},{19,3},{4,20},{20... | collective-permute-start | bytes 1966088 | tf_op jit(solution)/shard_map/ppermute | solution.py:213
  127.6 10.4 %collective-permute-start.14 = (bf16[4,80,640]{2,1,0:T(8,128)(2,1)}, bf16[4,80,640]{2,1,0:T(8,128)(2,1)S(1)}, u32[]{:S(2)}, u32[]{:S(2)}) collective-permute-start(bf16[4,80,640]{2,1,0:T(8,128)(2,1)} %collective-permute-done.12.refs_12_), channel_id=1, source_target_pairs={{0,960},{16,80},{64,0},{80,144},{128,64},{144,208},{192,128},{208,... | collective-permute-start | bytes 1228808 | tf_op jit(solution)/shard_map/ppermute | solution.py:167
  129.5 13.5 %collective-permute-start.15 = (bf16[4,80,640]{2,1,0:T(8,128)(2,1)}, bf16[4,80,640]{2,1,0:T(8,128)(2,1)}, u32[]{:S(2)}, u32[]{:S(2)}) collective-permute-start(bf16[4,80,640]{2,1,0:T(8,128)(2,1)} %collective-permute-done.13.refs_13_), channel_id=1, source_target_pairs={{0,64},{16,976},{64,128},{80,16},{128,192},{144,80},{192,256},{208... | collective-permute-start | bytes 1228808 | tf_op jit(solution)/shard_map/ppermute | solution.py:167
  156.1 7.2 %collective-permute-start.16 = (bf16[2,1280,128]{2,1,0:T(8,128)(2,1)S(1)}, bf16[2,1280,128]{2,1,0:T(8,128)(2,1)S(1)}, u32[]{:S(2)}, u32[]{:S(2)}) collective-permute-start(bf16[2,1280,128]{2,1,0:T(8,128)(2,1)S(1)} %get-tuple-element.14), channel_id=1, source_target_pairs={{0,16},{16,0},{1,17},{17,1},{2,18},{18,2},{3,19},{19,3},{4,20},{20... | collective-permute-start | bytes 1966088 | tf_op jit(solution)/shard_map/ppermute | solution.py:217
  (4 other events, 106.2 us)

commit v3 on v1

v3 whole, which is shorter than its diff:
```python
import jax
import jax.numpy as jnp
from jax import lax
from jax.experimental import pallas as pl
from jax.experimental.pallas import tpu as pltpu
from jax.sharding import Mesh, PartitionSpec as P

D = 1280
HDIM = 80
PATCH = 128
SLOTS = 16
ZS = 16
GROUPS = 4
PIECES = 4
LOCAL = 2
WIDTH = LOCAL * HDIM
EPSILON = 1e-06
VMEM = 32 * 2**20
LOG2E = 1.4426950408889634


def vmem_params():
    return pltpu.CompilerParams(vmem_limit_bytes=VMEM)


def rotate_body(start_ref, tiles_ref, out_ref):
    start = start_ref[0]

    def one(slot, carry):
        out_ref[(slot + start) & (SLOTS - 1)] = tiles_ref[slot]
        return carry

    lax.fori_loop(0, SLOTS, one, 0)


def rotate(tiles, start):
    return pl.pallas_call(
        rotate_body,
        out_shape=jax.ShapeDtypeStruct(tiles.shape, tiles.dtype),
        in_specs=[pl.BlockSpec(memory_space=pltpu.SMEM), pl.BlockSpec(memory_space=pltpu.VMEM)],
        out_specs=pl.BlockSpec(memory_space=pltpu.VMEM),
        compiler_params=vmem_params(),
        name="rotate",
    )(start, tiles)


def by_half(rows):
    parts = rows.reshape(ZS, 2, D // (2 * ZS), rows.shape[-1])
    return jnp.concatenate([parts[:, h].reshape(D // 2, rows.shape[-1]) for h in range(2)], axis=0)


def by_z(rows):
    parts = rows.reshape(2, ZS, 1, D // (2 * ZS), rows.shape[-1])
    return jnp.concatenate([parts[0], parts[1]], axis=1).reshape(D, rows.shape[-1])


def normalise_body(pick_ref, tile_ref, source_ref, normed_ref):
    tile = tile_ref[0]
    source_ref[0] = tile
    values = tile.astype(jnp.float32)
    center = values - jnp.mean(values, axis=0, keepdims=True)
    spread = jnp.mean(center * center, axis=0, keepdims=True)
    normed = by_half(center * lax.rsqrt(spread + EPSILON))
    normed_ref[0] = normed.T.astype(jnp.bfloat16)


def normalise(arrived, pick):
    return pl.pallas_call(
        normalise_body,
        out_shape=(
            jax.ShapeDtypeStruct((2, D, PATCH), jnp.bfloat16),
            jax.ShapeDtypeStruct((2, PATCH, D), jnp.bfloat16),
        ),
        grid_spec=pltpu.PrefetchScalarGridSpec(
            num_scalar_prefetch=1,
            grid=(2,),
            in_specs=[pl.BlockSpec((1, D, PATCH), lambda j, pick: (pick[j], 0, 0))],
            out_specs=(
                pl.BlockSpec((1, D, PATCH), lambda j, pick: (j, 0, 0)),
                pl.BlockSpec((1, PATCH, D), lambda j, pick: (j, 0, 0)),
            ),
        ),
        compiler_params=vmem_params(),
        name="normalise",
    )(pick, arrived)


def attend(qkv):
    pairs = [(tile, head) for tile in range(4) for head in range(LOCAL)]

    def part(kind, tile, head):
        low = kind * WIDTH + head * HDIM
        return qkv[low : low + HDIM, tile * PATCH : (tile + 1) * PATCH]

    scores = [
        lax.dot_general(
            part(1, *pair), part(0, *pair), (((0,), (0,)), ((), ())),
            preferred_element_type=jnp.float32,
        )
        for pair in pairs
    ]
    scale = HDIM ** (-0.5) * LOG2E
    powers = [jnp.exp2((s - jnp.max(s, axis=0, keepdims=True)) * scale) for s in scores]
    inverse = [1.0 / jnp.sum(p, axis=0, keepdims=True) for p in powers]
    contexts = [
        (
            jnp.dot(part(2, *pair), p.astype(jnp.bfloat16), preferred_element_type=jnp.float32) * i
        ).astype(jnp.bfloat16)
        for pair, p, i in zip(pairs, powers, inverse)
    ]
    return jnp.concatenate(
        [
            jnp.concatenate(contexts[tile * LOCAL : (tile + 1) * LOCAL], axis=0)
            for tile in range(4)
        ],
        axis=1,
    )


def encode_body(y_ref, own_ref, other_ref, *refs):
    pieces = refs[: GROUPS * PIECES]
    own_out_ref, other_out_ref, weight_ref, out_ref, context_ref, sems = refs[GROUPS * PIECES :]

    def copies(group):
        made = []
        for k in range(PIECES):
            y_hi = ((y_ref[0] + group + k // 2 * GROUPS) >> 2) & 1
            made.append(
                pltpu.make_async_copy(
                    pieces[group * PIECES + k], weight_ref.at[group, y_hi, k % 2], sems.at[group, k]
                )
            )
        return made

    for group in range(GROUPS):
        for copy in copies(group):
            copy.start()
    normed = jnp.concatenate(
        [ref[...].reshape(2 * PATCH, D) for ref in (own_ref, other_ref)], axis=0
    )
    for group in range(GROUPS):
        for copy in copies(group):
            copy.wait()
        weight = weight_ref[group].reshape(D, 4 * WIDTH)
        projected = jnp.dot(normed, weight[:, : 3 * WIDTH], preferred_element_type=jnp.float32)
        context_ref[group * WIDTH : (group + 1) * WIDTH] = attend(projected.astype(jnp.bfloat16).T)
        out_ref[group] = weight[:, 3 * WIDTH :]
    out = jnp.concatenate([out_ref[group] for group in range(GROUPS)], axis=1)
    total = by_z(jnp.dot(out, context_ref[...], preferred_element_type=jnp.float32))
    for tile in range(4):
        target = (own_out_ref, other_out_ref)[tile // 2]
        target[tile % 2] = total[:, tile * PATCH : (tile + 1) * PATCH].astype(jnp.bfloat16)


def encode(y, own, other, pieces):
    in_vmem = pl.BlockSpec(memory_space=pltpu.VMEM)
    part = jax.ShapeDtypeStruct((2, D, PATCH), jnp.bfloat16)
    in_hbm = [pltpu.with_memory_space_constraint(p, pltpu.HBM) for p in pieces]
    return pl.pallas_call(
        encode_body,
        out_shape=(part, part),
        in_specs=[pl.BlockSpec(memory_space=pltpu.SMEM), in_vmem, in_vmem]
        + [pl.BlockSpec(memory_space=pl.ANY)] * len(pieces),
        out_specs=(in_vmem, in_vmem),
        scratch_shapes=[
            pltpu.VMEM((GROUPS, 2, 2, D // 4, 4 * WIDTH), jnp.bfloat16),
            pltpu.VMEM((GROUPS, D, WIDTH), jnp.bfloat16),
            pltpu.VMEM((GROUPS * WIDTH, 4 * PATCH), jnp.bfloat16),
            pltpu.SemaphoreType.DMA((GROUPS, PIECES)),
        ],
        compiler_params=vmem_params(),
        name="encode",
    )(y, own, other, *in_hbm)


def around_y(block):
    length = 2 * GROUPS
    half = block.shape[0] // 2
    up = [(i, (i + 1) % length) for i in range(length)]
    down = [(i, (i - 1) % length) for i in range(length)]
    halves = [block[:half], block[half:]]
    rising, falling = list(halves), list(halves)
    found = {(0, 0): halves[0], (0, 1): halves[1]}
    for hop in range(1, length // 2 + 1):
        last = 2 * hop == length
        for k in range(2):
            if not last or k == 0:
                rising[k] = lax.ppermute(rising[k], ("y_hi", "tensor"), up)
                found[length - hop, k] = rising[k]
            if not last or k == 1:
                falling[k] = lax.ppermute(falling[k], ("y_hi", "tensor"), down)
                found[hop, k] = falling[k]
    return [
        found[group + k // 2 * GROUPS, k % 2] for group in range(GROUPS) for k in range(PIECES)
    ]


def layout(counts, ordering):
    doc_ids = jnp.arange(counts.shape[0], dtype=jnp.int32)
    position = jnp.sum(
        jnp.where(ordering[None, :] == doc_ids[:, None], doc_ids[None, :], 0), axis=1
    )
    starts = jnp.sum(jnp.where(position[None, :] < position[:, None], counts[None, :], 0), axis=1)
    return doc_ids, starts


def local(tiles, tile_counts, doc_order, qkv_weight, out_weight):
    bal_hi, bal_lo = lax.axis_index("bal_hi"), lax.axis_index("bal_lo")
    tensor = lax.axis_index("tensor")
    swap = [(0, 1), (1, 0)]

    rows = qkv_weight.shape[1]
    kinds = [qkv_weight[k] for k in range(3)] + [out_weight]
    halves = jnp.stack(
        [
            jnp.concatenate([w[:, c * WIDTH : (c + 1) * WIDTH] for w in kinds], axis=1)
            for c in range(2)
        ]
    )
    both = lax.all_to_all(halves, "core", 0, 0, tiled=True).reshape(2 * rows, 4 * WIDTH)

    counts = tile_counts[0]
    doc_ids, starts = layout(counts, doc_order[0])
    ends = starts + counts
    own_start = jnp.sum(jnp.where(doc_ids == bal_hi * 2 + bal_lo, starts, 0))
    outbound = rotate(tiles[0, 0], own_start.reshape(1))
    outbound, both = lax.optimization_barrier((outbound, both))
    arrived = lax.all_to_all(outbound, ("bal_lo", "bal_hi", "tensor"), 0, 0, tiled=True)
    block = lax.all_gather(both, "z", axis=0, tiled=True)
    pieces = around_y(block)
    place = bal_lo * 8 + bal_hi * 4 + tensor
    packed = place + jnp.arange(2, dtype=jnp.int32) * SLOTS
    inside = (starts[None, :] <= packed[:, None]) & (packed[:, None] < ends[None, :])
    doc = jnp.sum(jnp.where(inside, doc_ids[None, :], 0), axis=1)
    source, normed = normalise(arrived.reshape(4, D, PATCH), doc % 2 * 2 + doc // 2)
    other = lax.ppermute(normed, "core", swap)

    y = lax.axis_index("y_hi") * 4 + tensor
    own_part, other_part = encode(y.reshape(1).astype(jnp.int32), normed, other, pieces)
    back_part = lax.ppermute(other_part, "core", swap)
    encoded = (
        source.astype(jnp.float32) + own_part.astype(jnp.float32) + back_part.astype(jnp.float32)
    ).astype(jnp.bfloat16)
    returned = lax.all_to_all(
        encoded.reshape(8, D // 4, PATCH), ("bal_hi", "tensor"), 0, 0, tiled=True
    )
    return returned[None]


def solution(mesh):
    z = mesh.shape["dp"] // 4
    devices = mesh.devices.reshape(z, 2, 2, 2, 2, 4)
    fine = Mesh(devices, ("z", "y_hi", "core", "bal_hi", "bal_lo", "tensor"))
    dp, bal = ("z", "y_hi", "core"), ("bal_hi", "bal_lo")
    placed = (
        P(dp, bal, None, "tensor", None),
        P(dp, None),
        P(dp, None),
        P(None, dp, "tensor"),
        P(dp, "tensor"),
    )
    return jax.shard_map(
        local, mesh=fine, in_specs=placed, out_specs=P(dp, bal, "tensor", None), check_vma=False
    )
```

time: 180 us -> 178 us (0.989)
  starting transfers between devices: 9.96 us -> 81.3 us
  waiting for transfers between devices: 78.9 us -> 17.8 us
  between operations: 13.5 us -> 0.37 us
  Pallas kernels: 16.2 us -> 11.7 us
  blocking collectives: 56 us -> 58.1 us
  other arithmetic: 1.58 us -> 3.46 us
    ppermute x0 -> x14, starting transfers between devices: none -> 44.4 us  [the longest x7 30.5 us: around_y(): falling[k] = lax.ppermute(falling[k], ('y_hi', 'tensor'), down)]
    all_gather x1 -> x0, waiting for transfers between devices: 41.9 us -> none  [local(): weights = lax.all_gather(ring, 'z', axis=0, tiled=True)]
    all_to_all x1, waiting for transfers between devices: 33.6 us -> 0.01 us  [local(): lax.all_to_all(outbound, ('bal_lo', 'bal_hi', 'tensor'), 0, 0, tiled=True)]
    all_gather x0 -> x1, blocking collectives: none -> 32 us  [local(): block = lax.all_gather(both, 'z', axis=0, tiled=True)]
    all_to_all x1 -> x0, blocking collectives: 30.6 us -> none  [local(): lax.all_to_all(outgoing.reshape(16, rows, 4 * WIDTH), ('y_hi', 'core', 't...]
    all_to_all x0 -> x1, starting transfers between devices: none -> 17.4 us  [local(): lax.all_to_all(halves, 'core', 0, 0, tiled=True)]
    ppermute x0 -> x14, waiting for transfers between devices: none -> 16.1 us  [the longest x7 11 us: around_y(): falling[k] = lax.ppermute(falling[k], ('y_hi', 'tensor'), down)]
    ppermute x1, starting transfers between devices: 2.55 us -> 12.7 us  [local(): other = lax.ppermute(normed, 'core', swap)]
  transfers between devices with their start and end apart: 4 -> 18, of which waited for: 4 -> 6; matrix products, arithmetic and copies ran while one was open for 1% -> 1% of each run, Pallas kernels for 2% -> 2%
where the time goes in v3:
time: 178 us; the launch traced here: 177 us
  starting transfers between devices  81.3 us (46%)
  blocking collectives  58.1 us (33%)
  waiting for transfers between devices  17.8 us (10%)
  Pallas kernels  11.7 us (7%)
  local copies, waits for them, and re-layouts  4.12 us (2%)
  other arithmetic  3.46 us (2%)
    all_gather x1, blocking collectives, local(): block = lax.all_gather(both, 'z', axis=0, tiled=True)  32 us
    ppermute x7, starting transfers between devices, around_y(): falling[k] = lax.ppermute(falling[k], ('y_hi', 'tensor'), down)  30.5 us
    all_to_all x1, blocking collectives, local(): lax.all_to_all(encoded.reshape(8, D // 4, PATCH), ('bal_hi', 'tensor'), 0...  26.2 us
    all_to_all x1, starting transfers between devices, local(): lax.all_to_all(halves, 'core', 0, 0, tiled=True)  17.4 us
    ppermute x7, starting transfers between devices, around_y(): rising[k] = lax.ppermute(rising[k], ('y_hi', 'tensor'), up)  13.9 us
    ppermute x1, starting transfers between devices, local(): other = lax.ppermute(normed, 'core', swap)  12.7 us
    ppermute x7, waiting for transfers between devices, around_y(): falling[k] = lax.ppermute(falling[k], ('y_hi', 'tensor'), down)  11 us
    pallas_call x1, Pallas kernels, encode(): pl.pallas_call(encode_body, out_shape=(part, part), in_specs=[pl.BlockSpe...  8.15 us
  transfers between devices with their start and end apart: 18, of which 6 were waited for; matrix products, arithmetic and copies ran while one was open for 1% of the time, Pallas kernels for 2%

profile of v3, /device:TPU:1, one launch (start us, length us, event | category | flops | bytes accessed | tf_op | source)
XLA Modules:
  0.0 176.9 jit_solution(12698618851866167444)
XLA Ops:
  2.6 17.4 %all-to-all-start = ((bf16[2,20,640]{2,1,0:T(8,128)(2,1)}), bf16[2,20,640]{2,1,0:T(8,128)(2,1)S(1)}, u32[]{:S(2)}, u32[]{:S(2)}) async-start(bf16[2,20,640]{2,1,0:T(8,128)(2,1)} %pad_maximum_fusion), calls=%async_computation | async-start | bytes 122880 | tf_op jit(solution)/shard_map/all_to_all | solution.py:220
  25.5 3.7 %all-to-all-start.1 = ((bf16[16,320,128]{2,1,0:T(8,128)(2,1)}), bf16[16,320,128]{2,1,0:T(8,128)(2,1)S(1)}, u32[]{:S(2)}, u32[]{:S(2)}) async-start(bf16[16,320,128]{2,1,0:T(8,128)(2,1)} %rotate.1), calls=%async_computation.1 | async-start | bytes 2621440 | tf_op jit(solution)/shard_map/all_to_all | solution.py:228
  29.2 32.0 %all_gather.3 = bf16[640,640]{1,0:T(8,128)(2,1)S(1)} all-gather(bf16[40,640]{1,0:T(8,128)(2,1)S(1)} %reshape.25), channel_id=1, replica_groups=mesh['z'=16,'y_hi'=2,'core'=2,'bal_hi'=2,'bal_lo'=2,'tensor'=4] {'z'}, dimensions={0}, use_global_device_ids=true | all-gather | bytes 870400 | tf_op jit(solution)/shard_map/all_gather | solution.py:229
  61.3 5.1 %collective-permute-start.5 = (bf16[320,640]{1,0:T(8,128)(2,1)S(1)}, bf16[320,640]{1,0:T(8,128)(2,1)S(1)}, u32[]{:S(2)}, u32[]{:S(2)}) collective-permute-start(bf16[320,640]{1,0:T(8,128)(2,1)S(1)} %get-tuple-element.17.refs_1_), channel_id=1, source_target_pairs={{0,35},{1,0},{2,1},{3,2},{32,3},{33,32},{34,33},{35,34},{4,39},{5,... | collective-permute-start | bytes 1228808 | tf_op jit(solution)/shard_map/ppermute | solution.py:191
  66.4 1.9 %collective-permute-start.1 = (bf16[320,640]{1,0:T(8,128)(2,1)S(1)}, bf16[320,640]{1,0:T(8,128)(2,1)S(1)}, u32[]{:S(2)}, u32[]{:S(2)}) collective-permute-start(bf16[320,640]{1,0:T(8,128)(2,1)S(1)} %get-tuple-element.18.refs_0_), channel_id=1, source_target_pairs={{0,1},{1,2},{2,3},{3,32},{32,33},{33,34},{34,35},{35,0},{4,5},{5,6... | collective-permute-start | bytes 1228808 | tf_op jit(solution)/shard_map/ppermute | solution.py:188
  68.3 1.9 %collective-permute-start.10 = (bf16[320,640]{1,0:T(8,128)(2,1)S(1)}, bf16[320,640]{1,0:T(8,128)(2,1)}, u32[]{:S(2)}, u32[]{:S(2)}) collective-permute-start(bf16[320,640]{1,0:T(8,128)(2,1)S(1)} %get-tuple-element.17.refs_1_), channel_id=1, source_target_pairs={{0,1},{1,2},{2,3},{3,32},{32,33},{33,34},{34,35},{35,0},{4,5},{5,6... | collective-permute-start | bytes 1228808 | tf_op jit(solution)/shard_map/ppermute | solution.py:188
  70.3 4.6 %collective-permute-start.9 = (bf16[320,640]{1,0:T(8,128)(2,1)S(1)}, bf16[320,640]{1,0:T(8,128)(2,1)}, u32[]{:S(2)}, u32[]{:S(2)}) collective-permute-start(bf16[320,640]{1,0:T(8,128)(2,1)S(1)} %get-tuple-element.18.refs_0_), channel_id=1, source_target_pairs={{0,35},{1,0},{2,1},{3,2},{32,3},{33,32},{34,33},{35,34},{4,39},{5,... | collective-permute-start | bytes 1228808 | tf_op jit(solution)/shard_map/ppermute | solution.py:191
  74.9 3.4 %collective-permute-start.6 = (bf16[320,640]{1,0:T(8,128)(2,1)S(1)}, bf16[320,640]{1,0:T(8,128)(2,1)}, u32[]{:S(2)}, u32[]{:S(2)}) collective-permute-start(bf16[320,640]{1,0:T(8,128)(2,1)S(1)} %collective-permute-done.5.refs_5_), channel_id=1, source_target_pairs={{0,35},{1,0},{2,1},{3,2},{32,3},{33,32},{34,33},{35,34},{4,39},{5,... | collective-permute-start | bytes 1228808 | tf_op jit(solution)/shard_map/ppermute | solution.py:191
  78.3 1.9 %collective-permute-start.2 = (bf16[320,640]{1,0:T(8,128)(2,1)S(1)}, bf16[320,640]{1,0:T(8,128)(2,1)}, u32[]{:S(2)}, u32[]{:S(2)}) collective-permute-start(bf16[320,640]{1,0:T(8,128)(2,1)S(1)} %collective-permute-done.1.refs_14_), channel_id=1, source_target_pairs={{0,1},{1,2},{2,3},{3,32},{32,33},{33,34},{34,35},{35,0},{4,5},{5,6... | collective-permute-start | bytes 1228808 | tf_op jit(solution)/shard_map/ppermute | solution.py:188
  80.4 2.5 %collective-permute-done.10.refs_15_ = bf16[320,640]{1,0:T(8,128)(2,1)} collective-permute-done((bf16[320,640]{1,0:T(8,128)(2,1)S(1)}, bf16[320,640]{1,0:T(8,128)(2,1)}, u32[]{:S(2)}, u32[]{:S(2)}) %collective-permute-start.10) | collective-permute-done | bytes 409632 | tf_op jit(solution)/shard_map/ppermute | solution.py:188
  82.9 1.9 %collective-permute-start.11 = (bf16[320,640]{1,0:T(8,128)(2,1)}, bf16[320,640]{1,0:T(8,128)(2,1)}, u32[]{:S(2)}, u32[]{:S(2)}) collective-permute-start(bf16[320,640]{1,0:T(8,128)(2,1)} %collective-permute-done.10.refs_15_), channel_id=1, source_target_pairs={{0,1},{1,2},{2,3},{3,32},{32,33},{33,34},{34,35},{35,0},{4,5},{5,6... | collective-permute-start | bytes 1228808 | tf_op jit(solution)/shard_map/ppermute | solution.py:188
  84.8 4.6 %collective-permute-start.13 = (bf16[320,640]{1,0:T(8,128)(2,1)}, bf16[320,640]{1,0:T(8,128)(2,1)}, u32[]{:S(2)}, u32[]{:S(2)}) collective-permute-start(bf16[320,640]{1,0:T(8,128)(2,1)} %collective-permute-done.9.refs_4_), channel_id=1, source_target_pairs={{0,35},{1,0},{2,1},{3,2},{32,3},{33,32},{34,33},{35,34},{4,39},{5,... | collective-permute-start | bytes 1228808 | tf_op jit(solution)/shard_map/ppermute | solution.py:191
  90.7 5.4 %collective-permute-start.7 = (bf16[320,640]{1,0:T(8,128)(2,1)}, bf16[320,640]{1,0:T(8,128)(2,1)}, u32[]{:S(2)}, u32[]{:S(2)}) collective-permute-start(bf16[320,640]{1,0:T(8,128)(2,1)} %collective-permute-done.6.refs_9_), channel_id=1, source_target_pairs={{0,35},{1,0},{2,1},{3,2},{32,3},{33,32},{34,33},{35,34},{4,39},{5,... | collective-permute-start | bytes 1228808 | tf_op jit(solution)/shard_map/ppermute | solution.py:191
  96.1 1.9 %collective-permute-start.3 = (bf16[320,640]{1,0:T(8,128)(2,1)}, bf16[320,640]{1,0:T(8,128)(2,1)}, u32[]{:S(2)}, u32[]{:S(2)}) collective-permute-start(bf16[320,640]{1,0:T(8,128)(2,1)} %collective-permute-done.2.refs_10_), channel_id=1, source_target_pairs={{0,1},{1,2},{2,3},{3,32},{32,33},{33,34},{34,35},{35,0},{4,5},{5,6... | collective-permute-start | bytes 1228808 | tf_op jit(solution)/shard_map/ppermute | solution.py:188
  99.8 12.7 %collective-permute-start = (bf16[2,128,1280]{2,1,0:T(8,128)(2,1)S(1)}, bf16[2,128,1280]{2,1,0:T(8,128)(2,1)S(1)}, u32[]{:S(2)}, u32[]{:S(2)}) collective-permute-start(bf16[2,128,1280]{2,1,0:T(8,128)(2,1)S(1)} %get-tuple-element.13.own_ref), channel_id=1, source_target_pairs={{0,16},{16,0},{1,17},{17,1},{2,18},{18,2},{3,19},{19,3},{4,20},{20... | collective-permute-start | bytes 1966088 | tf_op jit(solution)/shard_map/ppermute | solution.py:236
  112.6 1.9 %collective-permute-start.12 = (bf16[320,640]{1,0:T(8,128)(2,1)}, bf16[320,640]{1,0:T(8,128)(2,1)S(1)}, u32[]{:S(2)}, u32[]{:S(2)}) collective-permute-start(bf16[320,640]{1,0:T(8,128)(2,1)} %collective-permute-done.11.refs_11_), channel_id=1, source_target_pairs={{0,1},{1,2},{2,3},{3,32},{32,33},{33,34},{34,35},{35,0},{4,5},{5,6... | collective-permute-start | bytes 1228808 | tf_op jit(solution)/shard_map/ppermute | solution.py:188
  114.5 4.6 %collective-permute-start.14 = (bf16[320,640]{1,0:T(8,128)(2,1)}, bf16[320,640]{1,0:T(8,128)(2,1)}, u32[]{:S(2)}, u32[]{:S(2)}) collective-permute-start(bf16[320,640]{1,0:T(8,128)(2,1)} %collective-permute-done.13.refs_8_), channel_id=1, source_target_pairs={{0,35},{1,0},{2,1},{3,2},{32,3},{33,32},{34,33},{35,34},{4,39},{5,... | collective-permute-start | bytes 1228808 | tf_op jit(solution)/shard_map/ppermute | solution.py:191
  119.1 2.9 %collective-permute-start.8 = (bf16[320,640]{1,0:T(8,128)(2,1)}, bf16[320,640]{1,0:T(8,128)(2,1)}, u32[]{:S(2)}, u32[]{:S(2)}) collective-permute-start(bf16[320,640]{1,0:T(8,128)(2,1)} %collective-permute-done.7.refs_13_), channel_id=1, source_target_pairs={{0,35},{1,0},{2,1},{3,2},{32,3},{33,32},{34,33},{35,34},{4,39},{5,... | collective-permute-start | bytes 1228808 | tf_op jit(solution)/shard_map/ppermute | solution.py:191
  122.0 2.4 %collective-permute-start.4 = (bf16[320,640]{1,0:T(8,128)(2,1)}, bf16[320,640]{1,0:T(8,128)(2,1)}, u32[]{:S(2)}, u32[]{:S(2)}) collective-permute-start(bf16[320,640]{1,0:T(8,128)(2,1)} %collective-permute-done.3.refs_6_), channel_id=1, source_target_pairs={{0,1},{1,2},{2,3},{3,32},{32,33},{33,34},{34,35},{35,0},{4,5},{5,6... | collective-permute-start | bytes 1228808 | tf_op jit(solution)/shard_map/ppermute | solution.py:188
  124.4 2.6 %collective-permute-done.12.refs_7_ = bf16[320,640]{1,0:T(8,128)(2,1)S(1)} collective-permute-done((bf16[320,640]{1,0:T(8,128)(2,1)}, bf16[320,640]{1,0:T(8,128)(2,1)S(1)}, u32[]{:S(2)}, u32[]{:S(2)}) %collective-permute-start.12) | collective-permute-done | bytes 409632 | tf_op jit(solution)/shard_map/ppermute | solution.py:188
  127.9 8.8 %collective-permute-done.8.refs_3_ = bf16[320,640]{1,0:T(8,128)(2,1)} collective-permute-done((bf16[320,640]{1,0:T(8,128)(2,1)}, bf16[320,640]{1,0:T(8,128)(2,1)}, u32[]{:S(2)}, u32[]{:S(2)}) %collective-permute-start.8) | collective-permute-done | bytes 409632 | tf_op jit(solution)/shard_map/ppermute | solution.py:191
  136.8 8.1 %encode.1 = (bf16[2,1280,128]{2,1,0:T(8,128)(2,1)S(1)}, bf16[2,1280,128]{2,1,0:T(8,128)(2,1)S(1)}) custom-call(s32[1]{0:T(128)} %bitcast.12.y_ref, bf16[2,128,1280]{2,1,0:T(8,128)(2,1)S(1)} %get-tuple-element.13.own_ref, bf16[2,128,1280]{2,1,0:T(8,128)(2,1)S(1)} %collective-permute-done.other_ref, bf16[320,640]{1,0:T(8,128)(2,1)} %copy-done.2, ...), custom_call_target="tpu_custom_call" | custom-call | tf_op jit(solution)/shard_map/encode/pallas_call | solution.py:159
  144.9 3.0 %collective-permute-start.15 = (bf16[2,1280,128]{2,1,0:T(8,128)(2,1)S(1)}, bf16[2,1280,128]{2,1,0:T(8,128)(2,1)S(1)}, u32[]{:S(2)}, u32[]{:S(2)}) collective-permute-start(bf16[2,1280,128]{2,1,0:T(8,128)(2,1)S(1)} %get-tuple-element.16), channel_id=1, source_target_pairs={{0,16},{16,0},{1,17},{17,1},{2,18},{18,2},{3,19},{19,3},{4,20},{20... | collective-permute-start | bytes 1966088 | tf_op jit(solution)/shard_map/ppermute | solution.py:240
  149.9 26.2 %all_to_all.15 = bf16[8,320,128]{2,1,0:T(8,128)(2,1)S(1)} all-to-all(bf16[8,320,128]{2,1,0:T(8,128)(2,1)S(1)} %bitcast.26), channel_id=1, replica_groups=mesh['z'=16,'y_hi'=2,'core'=2,'bal_hi'=2,'bal_lo'=2,'tensor'=4] {'bal_hi..., dimensions={0} | all-to-all | bytes 1310720 | tf_op jit(solution)/shard_map/all_to_all | solution.py:244
  (49 shorter events, 15.2 us)
Async XLA Ops:
  2.6 22.9 %all-to-all-start = ((bf16[2,20,640]{2,1,0:T(8,128)(2,1)}), bf16[2,20,640]{2,1,0:T(8,128)(2,1)S(1)}, u32[]{:S(2)}, u32[]{:S(2)}) async-start(bf16[2,20,640]{2,1,0:T(8,128)(2,1)} %pad_maximum_fusion), calls=%async_computation | async-start | bytes 122880 | tf_op jit(solution)/shard_map/all_to_all | solution.py:220
  25.5 72.6 %all-to-all-start.1 = ((bf16[16,320,128]{2,1,0:T(8,128)(2,1)}), bf16[16,320,128]{2,1,0:T(8,128)(2,1)S(1)}, u32[]{:S(2)}, u32[]{:S(2)}) async-start(bf16[16,320,128]{2,1,0:T(8,128)(2,1)} %rotate.1), calls=%async_computation.1 | async-start | bytes 2621440 | tf_op jit(solution)/shard_map/all_to_all | solution.py:228
  29.2 51.0 %copy-start.6 = (s32[1,4]{1,0:T(1,128)S(1)}, s32[1,4]{1,0:T(1,128)}, u32[]{:S(2)}) copy-start(s32[1,4]{1,0:T(1,128)} %param.6) | copy-start | bytes 52
  61.2 75.5 %copy-start.1 = (bf16[320,640]{1,0:T(8,128)(2,1)}, bf16[320,640]{1,0:T(8,128)(2,1)S(1)}, u32[]{:S(2)}) copy-start(bf16[320,640]{1,0:T(8,128)(2,1)S(1)} %get-tuple-element.17.refs_1_) | copy-start | bytes 1228804
  61.3 75.5 %copy-start.2 = (bf16[320,640]{1,0:T(8,128)(2,1)}, bf16[320,640]{1,0:T(8,128)(2,1)S(1)}, u32[]{:S(2)}) copy-start(bf16[320,640]{1,0:T(8,128)(2,1)S(1)} %get-tuple-element.18.refs_0_) | copy-start | bytes 1228804
  61.3 13.6 %collective-permute-start.5 = (bf16[320,640]{1,0:T(8,128)(2,1)S(1)}, bf16[320,640]{1,0:T(8,128)(2,1)S(1)}, u32[]{:S(2)}, u32[]{:S(2)}) collective-permute-start(bf16[320,640]{1,0:T(8,128)(2,1)S(1)} %get-tuple-element.17.refs_1_), channel_id=1, source_target_pairs={{0,35},{1,0},{2,1},{3,2},{32,3},{33,32},{34,33},{35,34},{4,39},{5,... | collective-permute-start | bytes 1228808 | tf_op jit(solution)/shard_map/ppermute | solution.py:191
  66.4 11.8 %collective-permute-start.1 = (bf16[320,640]{1,0:T(8,128)(2,1)S(1)}, bf16[320,640]{1,0:T(8,128)(2,1)S(1)}, u32[]{:S(2)}, u32[]{:S(2)}) collective-permute-start(bf16[320,640]{1,0:T(8,128)(2,1)S(1)} %get-tuple-element.18.refs_0_), channel_id=1, source_target_pairs={{0,1},{1,2},{2,3},{3,32},{32,33},{33,34},{34,35},{35,0},{4,5},{5,6... | collective-permute-start | bytes 1228808 | tf_op jit(solution)/shard_map/ppermute | solution.py:188
  68.3 14.6 %collective-permute-start.10 = (bf16[320,640]{1,0:T(8,128)(2,1)S(1)}, bf16[320,640]{1,0:T(8,128)(2,1)}, u32[]{:S(2)}, u32[]{:S(2)}) collective-permute-start(bf16[320,640]{1,0:T(8,128)(2,1)S(1)} %get-tuple-element.17.refs_1_), channel_id=1, source_target_pairs={{0,1},{1,2},{2,3},{3,32},{32,33},{33,34},{34,35},{35,0},{4,5},{5,6... | collective-permute-start | bytes 1228808 | tf_op jit(solution)/shard_map/ppermute | solution.py:188
  70.3 14.6 %collective-permute-start.9 = (bf16[320,640]{1,0:T(8,128)(2,1)S(1)}, bf16[320,640]{1,0:T(8,128)(2,1)}, u32[]{:S(2)}, u32[]{:S(2)}) collective-permute-start(bf16[320,640]{1,0:T(8,128)(2,1)S(1)} %get-tuple-element.18.refs_0_), channel_id=1, source_target_pairs={{0,35},{1,0},{2,1},{3,2},{32,3},{33,32},{34,33},{35,34},{4,39},{5,... | collective-permute-start | bytes 1228808 | tf_op jit(solution)/shard_map/ppermute | solution.py:191
  74.9 23.2 %copy-start.3 = (bf16[320,640]{1,0:T(8,128)(2,1)}, bf16[320,640]{1,0:T(8,128)(2,1)S(1)}, u32[]{:S(2)}) copy-start(bf16[320,640]{1,0:T(8,128)(2,1)S(1)} %collective-permute-done.5.refs_5_) | copy-start | bytes 1228804
  74.9 15.8 %collective-permute-start.6 = (bf16[320,640]{1,0:T(8,128)(2,1)S(1)}, bf16[320,640]{1,0:T(8,128)(2,1)}, u32[]{:S(2)}, u32[]{:S(2)}) collective-permute-start(bf16[320,640]{1,0:T(8,128)(2,1)S(1)} %collective-permute-done.5.refs_5_), channel_id=1, source_target_pairs={{0,35},{1,0},{2,1},{3,2},{32,3},{33,32},{34,33},{35,34},{4,39},{5,... | collective-permute-start | bytes 1228808 | tf_op jit(solution)/shard_map/ppermute | solution.py:191
  78.3 19.8 %copy-start.4 = (bf16[320,640]{1,0:T(8,128)(2,1)}, bf16[320,640]{1,0:T(8,128)(2,1)S(1)}, u32[]{:S(2)}) copy-start(bf16[320,640]{1,0:T(8,128)(2,1)S(1)} %collective-permute-done.1.refs_14_) | copy-start | bytes 1228804
  78.3 17.8 %collective-permute-start.2 = (bf16[320,640]{1,0:T(8,128)(2,1)S(1)}, bf16[320,640]{1,0:T(8,128)(2,1)}, u32[]{:S(2)}, u32[]{:S(2)}) collective-permute-start(bf16[320,640]{1,0:T(8,128)(2,1)S(1)} %collective-permute-done.1.refs_14_), channel_id=1, source_target_pairs={{0,1},{1,2},{2,3},{3,32},{32,33},{33,34},{34,35},{35,0},{4,5},{5,6... | collective-permute-start | bytes 1228808 | tf_op jit(solution)/shard_map/ppermute | solution.py:188
  82.9 29.7 %collective-permute-start.11 = (bf16[320,640]{1,0:T(8,128)(2,1)}, bf16[320,640]{1,0:T(8,128)(2,1)}, u32[]{:S(2)}, u32[]{:S(2)}) collective-permute-start(bf16[320,640]{1,0:T(8,128)(2,1)} %collective-permute-done.10.refs_15_), channel_id=1, source_target_pairs={{0,1},{1,2},{2,3},{3,32},{32,33},{33,34},{34,35},{35,0},{4,5},{5,6... | collective-permute-start | bytes 1228808 | tf_op jit(solution)/shard_map/ppermute | solution.py:188
  84.8 29.7 %collective-permute-start.13 = (bf16[320,640]{1,0:T(8,128)(2,1)}, bf16[320,640]{1,0:T(8,128)(2,1)}, u32[]{:S(2)}, u32[]{:S(2)}) collective-permute-start(bf16[320,640]{1,0:T(8,128)(2,1)} %collective-permute-done.9.refs_4_), channel_id=1, source_target_pairs={{0,35},{1,0},{2,1},{3,2},{32,3},{33,32},{34,33},{35,34},{4,39},{5,... | collective-permute-start | bytes 1228808 | tf_op jit(solution)/shard_map/ppermute | solution.py:191
  90.7 28.4 %collective-permute-start.7 = (bf16[320,640]{1,0:T(8,128)(2,1)}, bf16[320,640]{1,0:T(8,128)(2,1)}, u32[]{:S(2)}, u32[]{:S(2)}) collective-permute-start(bf16[320,640]{1,0:T(8,128)(2,1)} %collective-permute-done.6.refs_9_), channel_id=1, source_target_pairs={{0,35},{1,0},{2,1},{3,2},{32,3},{33,32},{34,33},{35,34},{4,39},{5,... | collective-permute-start | bytes 1228808 | tf_op jit(solution)/shard_map/ppermute | solution.py:191
  96.1 25.9 %collective-permute-start.3 = (bf16[320,640]{1,0:T(8,128)(2,1)}, bf16[320,640]{1,0:T(8,128)(2,1)}, u32[]{:S(2)}, u32[]{:S(2)}) collective-permute-start(bf16[320,640]{1,0:T(8,128)(2,1)} %collective-permute-done.2.refs_10_), channel_id=1, source_target_pairs={{0,1},{1,2},{2,3},{3,32},{32,33},{33,34},{34,35},{35,0},{4,5},{5,6... | collective-permute-start | bytes 1228808 | tf_op jit(solution)/shard_map/ppermute | solution.py:188
  99.8 36.9 %collective-permute-start = (bf16[2,128,1280]{2,1,0:T(8,128)(2,1)S(1)}, bf16[2,128,1280]{2,1,0:T(8,128)(2,1)S(1)}, u32[]{:S(2)}, u32[]{:S(2)}) collective-permute-start(bf16[2,128,1280]{2,1,0:T(8,128)(2,1)S(1)} %get-tuple-element.13.own_ref), channel_id=1, source_target_pairs={{0,16},{16,0},{1,17},{17,1},{2,18},{18,2},{3,19},{19,3},{4,20},{20... | collective-permute-start | bytes 1966088 | tf_op jit(solution)/shard_map/ppermute | solution.py:236
  112.6 14.4 %collective-permute-start.12 = (bf16[320,640]{1,0:T(8,128)(2,1)}, bf16[320,640]{1,0:T(8,128)(2,1)S(1)}, u32[]{:S(2)}, u32[]{:S(2)}) collective-permute-start(bf16[320,640]{1,0:T(8,128)(2,1)} %collective-permute-done.11.refs_11_), channel_id=1, source_target_pairs={{0,1},{1,2},{2,3},{3,32},{32,33},{33,34},{34,35},{35,0},{4,5},{5,6... | collective-permute-start | bytes 1228808 | tf_op jit(solution)/shard_map/ppermute | solution.py:188
  114.5 13.4 %collective-permute-start.14 = (bf16[320,640]{1,0:T(8,128)(2,1)}, bf16[320,640]{1,0:T(8,128)(2,1)}, u32[]{:S(2)}, u32[]{:S(2)}) collective-permute-start(bf16[320,640]{1,0:T(8,128)(2,1)} %collective-permute-done.13.refs_8_), channel_id=1, source_target_pairs={{0,35},{1,0},{2,1},{3,2},{32,3},{33,32},{34,33},{35,34},{4,39},{5,... | collective-permute-start | bytes 1228808 | tf_op jit(solution)/shard_map/ppermute | solution.py:191
  119.1 17.6 %collective-permute-start.8 = (bf16[320,640]{1,0:T(8,128)(2,1)}, bf16[320,640]{1,0:T(8,128)(2,1)}, u32[]{:S(2)}, u32[]{:S(2)}) collective-permute-start(bf16[320,640]{1,0:T(8,128)(2,1)} %collective-permute-done.7.refs_13_), channel_id=1, source_target_pairs={{0,35},{1,0},{2,1},{3,2},{32,3},{33,32},{34,33},{35,34},{4,39},{5,... | collective-permute-start | bytes 1228808 | tf_op jit(solution)/shard_map/ppermute | solution.py:191
  122.0 14.7 %collective-permute-start.4 = (bf16[320,640]{1,0:T(8,128)(2,1)}, bf16[320,640]{1,0:T(8,128)(2,1)}, u32[]{:S(2)}, u32[]{:S(2)}) collective-permute-start(bf16[320,640]{1,0:T(8,128)(2,1)} %collective-permute-done.3.refs_6_), channel_id=1, source_target_pairs={{0,1},{1,2},{2,3},{3,32},{32,33},{33,34},{34,35},{35,0},{4,5},{5,6... | collective-permute-start | bytes 1228808 | tf_op jit(solution)/shard_map/ppermute | solution.py:188
  127.0 9.8 %copy-start.5 = (bf16[320,640]{1,0:T(8,128)(2,1)}, bf16[320,640]{1,0:T(8,128)(2,1)S(1)}, u32[]{:S(2)}) copy-start(bf16[320,640]{1,0:T(8,128)(2,1)S(1)} %collective-permute-done.12.refs_7_) | copy-start | bytes 1228804
  144.9 4.7 %collective-permute-start.15 = (bf16[2,1280,128]{2,1,0:T(8,128)(2,1)S(1)}, bf16[2,1280,128]{2,1,0:T(8,128)(2,1)S(1)}, u32[]{:S(2)}, u32[]{:S(2)}) collective-permute-start(bf16[2,1280,128]{2,1,0:T(8,128)(2,1)S(1)} %get-tuple-element.16), channel_id=1, source_target_pairs={{0,16},{16,0},{1,17},{17,1},{2,18},{18,2},{3,19},{19,3},{4,20},{20... | collective-permute-start | bytes 1966088 | tf_op jit(solution)/shard_map/ppermute | solution.py:240
  (1 other events, 1.3 us)

commit v4 on v3

v4 whole, which is shorter than its diff:
```python
import jax
import jax.numpy as jnp
from jax import lax
from jax.experimental import pallas as pl
from jax.experimental.pallas import tpu as pltpu
from jax.sharding import Mesh, PartitionSpec as P

D = 1280
HDIM = 80
PATCH = 128
SLOTS = 16
DOCS = 4
ZS = 16
GROUPS = 4
PIECES = 4
EARLY, LATE = (2, 1, 3), (0,)
LOCAL = 2
WIDTH = LOCAL * HDIM
EPSILON = 1e-06
VMEM = 32 * 2**20
LOG2E = 1.4426950408889634


def vmem_params():
    return pltpu.CompilerParams(vmem_limit_bytes=VMEM)


def cut_body(qkv_ref, out_ref, halves_ref):
    for core in range(2):
        low = core * WIDTH
        kinds = [qkv_ref[k, :, low : low + WIDTH] for k in range(3)] + [out_ref[:, low : low + WIDTH]]
        halves_ref[core] = jnp.concatenate(kinds, axis=1)


def cut(qkv_weight, out_weight):
    return pl.pallas_call(
        cut_body,
        out_shape=jax.ShapeDtypeStruct((2, out_weight.shape[0], 4 * WIDTH), jnp.bfloat16),
        compiler_params=vmem_params(),
        name="cut",
    )(qkv_weight, out_weight)


def in_turn(counts_ref, order_ref):
    first, turns = 0, []
    for turn in range(DOCS):
        doc = order_ref[turn]
        turns.append((doc, first, counts_ref[doc]))
        first = first + counts_ref[doc]
    return turns


def rotate_body(where_ref, counts_ref, order_ref, tiles_ref, out_ref, sems):
    start = 0
    for doc, first, _ in in_turn(counts_ref, order_ref):
        start = jnp.where(doc == where_ref[0], first, start)
    copies = [
        pltpu.make_async_copy(
            tiles_ref.at[slot], out_ref.at[(slot + start) & (SLOTS - 1)], sems.at[slot]
        )
        for slot in range(SLOTS)
    ]
    for copy in copies:
        copy.start()
    for copy in copies:
        copy.wait()


def rotate(where, counts, order, tiles):
    in_smem = pl.BlockSpec(memory_space=pltpu.SMEM)
    return pl.pallas_call(
        rotate_body,
        out_shape=jax.ShapeDtypeStruct(tiles.shape, tiles.dtype),
        in_specs=[in_smem, in_smem, in_smem, pl.BlockSpec(memory_space=pl.ANY)],
        out_specs=pl.BlockSpec(memory_space=pl.ANY),
        scratch_shapes=[pltpu.SemaphoreType.DMA((SLOTS,))],
        compiler_params=vmem_params(),
        name="rotate",
    )(where, counts, order, pltpu.with_memory_space_constraint(tiles, pltpu.HBM))


def by_half(rows):
    parts = rows.reshape(ZS, 2, D // (2 * ZS), rows.shape[-1])
    return jnp.concatenate([parts[:, h].reshape(D // 2, rows.shape[-1]) for h in range(2)], axis=0)


def by_z(rows):
    parts = rows.reshape(2, ZS, 1, D // (2 * ZS), rows.shape[-1])
    return jnp.concatenate([parts[0], parts[1]], axis=1).reshape(D, rows.shape[-1])


def normalise_body(where_ref, counts_ref, order_ref, tile_ref, source_ref, normed_ref):
    tile = tile_ref[0]
    source_ref[0] = tile
    values = tile.astype(jnp.float32)
    center = values - jnp.mean(values, axis=0, keepdims=True)
    spread = jnp.mean(center * center, axis=0, keepdims=True)
    normed = by_half(center * lax.rsqrt(spread + EPSILON))
    normed_ref[0] = normed.T.astype(jnp.bfloat16)


def normalise(where, counts, order, arrived):
    def pick(j, where_ref, counts_ref, order_ref):
        packed = where_ref[1] + j * SLOTS
        owner = 0
        for doc, first, count in in_turn(counts_ref, order_ref):
            owner = jnp.where((first <= packed) & (packed < first + count), doc, owner)
        return (owner & 1) * 2 + (owner >> 1), 0, 0

    def same(j, *_):
        return j, 0, 0

    return pl.pallas_call(
        normalise_body,
        out_shape=(
            jax.ShapeDtypeStruct((2, D, PATCH), jnp.bfloat16),
            jax.ShapeDtypeStruct((2, PATCH, D), jnp.bfloat16),
        ),
        grid_spec=pltpu.PrefetchScalarGridSpec(
            num_scalar_prefetch=3,
            grid=(2,),
            in_specs=[pl.BlockSpec((1, D, PATCH), pick)],
            out_specs=(pl.BlockSpec((1, D, PATCH), same), pl.BlockSpec((1, PATCH, D), same)),
        ),
        compiler_params=vmem_params(),
        name="normalise",
    )(where, counts, order, arrived)


def attend(qkv):
    pairs = [(tile, head) for tile in range(4) for head in range(LOCAL)]

    def part(kind, tile, head):
        low = kind * WIDTH + head * HDIM
        return qkv[low : low + HDIM, tile * PATCH : (tile + 1) * PATCH]

    scores = [
        lax.dot_general(
            part(1, *pair), part(0, *pair), (((0,), (0,)), ((), ())),
            preferred_element_type=jnp.float32,
        )
        for pair in pairs
    ]
    scale = HDIM ** (-0.5) * LOG2E
    powers = [jnp.exp2((s - jnp.max(s, axis=0, keepdims=True)) * scale) for s in scores]
    inverse = [1.0 / jnp.sum(p, axis=0, keepdims=True) for p in powers]
    contexts = [
        (
            jnp.dot(part(2, *pair), p.astype(jnp.bfloat16), preferred_element_type=jnp.float32) * i
        ).astype(jnp.bfloat16)
        for pair, p, i in zip(pairs, powers, inverse)
    ]
    return jnp.concatenate(
        [
            jnp.concatenate(contexts[tile * LOCAL : (tile + 1) * LOCAL], axis=0)
            for tile in range(4)
        ],
        axis=1,
    )


def group_contexts(groups, where_ref, own_ref, other_ref, pieces, weight_ref, sems):
    def copies(n, group):
        made = []
        for k in range(PIECES):
            y_hi = ((where_ref[2] + group + k // 2 * GROUPS) >> 2) & 1
            made.append(
                pltpu.make_async_copy(
                    pieces[n * PIECES + k], weight_ref.at[n, y_hi, k % 2], sems.at[n, k]
                )
            )
        return made

    for n, group in enumerate(groups):
        for copy in copies(n, group):
            copy.start()
    normed = jnp.concatenate(
        [ref[...].reshape(2 * PATCH, D) for ref in (own_ref, other_ref)], axis=0
    )
    contexts, outs = [], []
    for n, group in enumerate(groups):
        for copy in copies(n, group):
            copy.wait()
        weight = weight_ref[n].reshape(D, 4 * WIDTH)
        projected = jnp.dot(normed, weight[:, : 3 * WIDTH], preferred_element_type=jnp.float32)
        contexts.append(attend(projected.astype(jnp.bfloat16).T))
        outs.append(weight[:, 3 * WIDTH :])
    return jnp.dot(
        jnp.concatenate(outs, axis=1),
        jnp.concatenate(contexts, axis=0),
        preferred_element_type=jnp.float32,
    )


def early_body(where_ref, own_ref, other_ref, *refs):
    count = len(EARLY) * PIECES
    total_ref, weight_ref, sems = refs[count:]
    total_ref[...] = group_contexts(
        EARLY, where_ref, own_ref, other_ref, refs[:count], weight_ref, sems
    )


def late_body(where_ref, own_ref, other_ref, early_ref, *refs):
    count = len(LATE) * PIECES
    own_out_ref, other_out_ref, weight_ref, sems = refs[count:]
    total = group_contexts(LATE, where_ref, own_ref, other_ref, refs[:count], weight_ref, sems)
    total = by_z(total + early_ref[...])
    for tile in range(4):
        target = (own_out_ref, other_out_ref)[tile // 2]
        target[tile % 2] = total[:, tile * PATCH : (tile + 1) * PATCH].astype(jnp.bfloat16)


def encode(body, groups, out_shape, where, arrays, pieces):
    in_vmem = pl.BlockSpec(memory_space=pltpu.VMEM)
    taken = [pieces[group * PIECES + k] for group in groups for k in range(PIECES)]
    if groups == EARLY:
        taken = [pltpu.with_memory_space_constraint(t, pltpu.HBM) for t in taken]
    flops = 2 * 4 * PATCH * D * 4 * WIDTH * len(groups)
    return pl.pallas_call(
        body,
        out_shape=out_shape,
        in_specs=[pl.BlockSpec(memory_space=pltpu.SMEM)]
        + [in_vmem] * len(arrays)
        + [pl.BlockSpec(memory_space=pl.ANY)] * len(taken),
        out_specs=jax.tree.map(lambda _: in_vmem, out_shape),
        scratch_shapes=[
            pltpu.VMEM((len(groups), 2, 2, D // 4, 4 * WIDTH), jnp.bfloat16),
            pltpu.SemaphoreType.DMA((len(groups), PIECES)),
        ],
        compiler_params=vmem_params(),
        cost_estimate=pl.CostEstimate(
            flops=flops, bytes_accessed=len(groups) * D * 8 * WIDTH, transcendentals=0
        ),
        name=body.__name__,
    )(where, *arrays, *taken)


def around_y(block):
    length = 2 * GROUPS
    half = block.shape[0] // 2
    up = [(i, (i + 1) % length) for i in range(length)]
    down = [(i, (i - 1) % length) for i in range(length)]
    halves = [block[:half], block[half:]]
    rising, falling = list(halves), list(halves)
    found = {(0, 0): halves[0], (0, 1): halves[1]}
    for hop in range(1, length // 2 + 1):
        last = 2 * hop == length
        for k in range(2):
            if not last or k == 0:
                rising[k] = lax.ppermute(rising[k], ("y_hi", "tensor"), up)
                found[length - hop, k] = rising[k]
            if not last or k == 1:
                falling[k] = lax.ppermute(falling[k], ("y_hi", "tensor"), down)
                found[hop, k] = falling[k]
    return [
        found[group + k // 2 * GROUPS, k % 2] for group in range(GROUPS) for k in range(PIECES)
    ]


def local(tiles, tile_counts, doc_order, qkv_weight, out_weight):
    bal_hi, bal_lo = lax.axis_index("bal_hi"), lax.axis_index("bal_lo")
    tensor = lax.axis_index("tensor")
    swap = [(0, 1), (1, 0)]

    place = bal_lo * 8 + bal_hi * 4 + tensor
    y = lax.axis_index("y_hi") * 4 + tensor
    where = jnp.stack([bal_hi * 2 + bal_lo, place, y]).astype(jnp.int32)
    counts, order = tile_counts[0], doc_order[0]

    halves = cut(qkv_weight, out_weight)
    both = lax.all_to_all(halves, "core", 0, 0, tiled=True).reshape(-1, 4 * WIDTH)

    outbound = rotate(where, counts, order, tiles[0, 0])
    outbound, both = lax.optimization_barrier((outbound, both))
    arrived = lax.all_to_all(outbound, ("bal_lo", "bal_hi", "tensor"), 0, 0, tiled=True)
    block = lax.all_gather(both, "z", axis=0, tiled=True)
    pieces = around_y(block)
    source, normed = normalise(where, counts, order, arrived.reshape(4, D, PATCH))
    other = lax.ppermute(normed, "core", swap)

    early = jax.ShapeDtypeStruct((D, 4 * PATCH), jnp.float32)
    part = jax.ShapeDtypeStruct((2, D, PATCH), jnp.bfloat16)
    total = encode(early_body, EARLY, early, where, (normed, other), pieces)
    own_part, other_part = encode(
        late_body, LATE, (part, part), where, (normed, other, total), pieces
    )
    back_part = lax.ppermute(other_part, "core", swap)
    encoded = (
        source.astype(jnp.float32) + own_part.astype(jnp.float32) + back_part.astype(jnp.float32)
    ).astype(jnp.bfloat16)
    returned = lax.all_to_all(
        encoded.reshape(8, D // 4, PATCH), ("bal_hi", "tensor"), 0, 0, tiled=True
    )
    return returned[None]


def solution(mesh):
    z = mesh.shape["dp"] // 4
    devices = mesh.devices.reshape(z, 2, 2, 2, 2, 4)
    fine = Mesh(devices, ("z", "y_hi", "core", "bal_hi", "bal_lo", "tensor"))
    dp, bal = ("z", "y_hi", "core"), ("bal_hi", "bal_lo")
    placed = (
        P(dp, bal, None, "tensor", None),
        P(dp, None),
        P(dp, None),
        P(None, dp, "tensor"),
        P(dp, "tensor"),
    )
    return jax.shard_map(
        local, mesh=fine, in_specs=placed, out_specs=P(dp, bal, "tensor", None), check_vma=False
    )
```

time: 178 us -> 209 us (1.17)
  Pallas kernels: 11.7 us -> 54.2 us
  waiting for transfers between devices: 17.8 us -> 8.88 us
  other arithmetic: 3.46 us -> 0.33 us
    pallas_call x1, Pallas kernels: 1.84 us -> 41.5 us  [rotate(): pl.pallas_call(rotate_body, out_shape=jax.ShapeDtypeStruct(tiles.shape, t...]
    ppermute x7, waiting for transfers between devices: 11 us -> 1.86 us  [around_y(): falling[k] = lax.ppermute(falling[k], ('y_hi', 'tensor'), down)]
    pallas_call x1 -> x3, Pallas kernels: 8.15 us -> 10.9 us  [the longest x2 10.2 us: encode(): pl.pallas_call(body, out_shape=out_shape, in_specs=[pl.BlockSpec(memory_s...]
    reduce_sum x4 -> x0, other arithmetic: 2.44 us -> none  [the longest x1 0.84 us: layout(): jnp.sum(jnp.where(position[None, :] < position[:, None], counts[None, :],...]
    unnamed x15 -> x27, local copies, waits for them, and re-layouts: 2.18 us -> 4.42 us
  transfers between devices with their start and end apart: 18 -> 18, of which waited for: 6 -> 7; matrix products, arithmetic and copies ran while one was open for 1% -> 0% of each run, Pallas kernels for 2% -> 24%
where the time goes in v4:
time: 209 us; the launch traced here: 208 us
  starting transfers between devices  81.6 us (39%)
  blocking collectives  58.3 us (28%)
  Pallas kernels  54.2 us (26%)
  waiting for transfers between devices  8.88 us (4%)
  local copies, waits for them, and re-layouts  4.51 us (2%)
    pallas_call x1, Pallas kernels, rotate(): pl.pallas_call(rotate_body, out_shape=jax.ShapeDtypeStruct(tiles.shape, t...  41.5 us
    all_gather x1, blocking collectives, local(): block = lax.all_gather(both, 'z', axis=0, tiled=True)  32 us
    ppermute x7, starting transfers between devices, around_y(): falling[k] = lax.ppermute(falling[k], ('y_hi', 'tensor'), down)  31 us
    all_to_all x1, blocking collectives, local(): lax.all_to_all(encoded.reshape(8, D // 4, PATCH), ('bal_hi', 'tensor'), 0...  26.3 us
    all_to_all x1, starting transfers between devices, local(): lax.all_to_all(halves, 'core', 0, 0, tiled=True).reshape(-1, 4 * WIDTH)  17.4 us
    ppermute x7, starting transfers between devices, around_y(): rising[k] = lax.ppermute(rising[k], ('y_hi', 'tensor'), up)  15 us
    ppermute x1, starting transfers between devices, local(): other = lax.ppermute(normed, 'core', swap)  11.5 us
    pallas_call x2, Pallas kernels, encode(): pl.pallas_call(body, out_shape=out_shape, in_specs=[pl.BlockSpec(memory_s...  10.2 us
  transfers between devices with their start and end apart: 18, of which 7 were waited for; matrix products, arithmetic and copies ran while one was open for 0% of the time, Pallas kernels for 24%

profile of v4, /device:TPU:1, one launch (start us, length us, event | category | flops | bytes accessed | tf_op | source)
XLA Modules:
  0.0 208.1 jit_solution(2112758026151235286)
XLA Ops:
  2.3 17.4 %all-to-all-start = ((bf16[2,20,640]{2,1,0:T(8,128)(2,1)}), bf16[2,20,640]{2,1,0:T(8,128)(2,1)S(1)}, u32[]{:S(2)}, u32[]{:S(2)}) async-start(bf16[2,20,640]{2,1,0:T(8,128)(2,1)} %cut.1), calls=%async_computation | async-start | bytes 122880 | tf_op jit(solution)/shard_map/all_to_all | solution.py:271
  21.1 41.5 %rotate.1 = bf16[16,320,128]{2,1,0:T(8,128)(2,1)} custom-call(s32[3]{0:T(128)S(1)} %pad_add_fusion.where_ref, s32[4]{0:T(128)S(1)} %bitcast.10, s32[4]{0:T(128)S(1)} %bitcast.12, bf16[16,320,128]{2,1,0:T(8,128)(2,1)} %bitcast.16), custom_call_target="tpu_custom_call" | custom-call | tf_op jit(solution)/shard_map/rotate/pallas_call | solution.py:71
  62.6 3.7 %all-to-all-start.1 = ((bf16[16,320,128]{2,1,0:T(8,128)(2,1)}), bf16[16,320,128]{2,1,0:T(8,128)(2,1)S(1)}, u32[]{:S(2)}, u32[]{:S(2)}) async-start(bf16[16,320,128]{2,1,0:T(8,128)(2,1)} %rotate.1), calls=%async_computation.1 | async-start | bytes 2621440 | tf_op jit(solution)/shard_map/all_to_all | solution.py:275
  66.4 32.0 %all_gather.3 = bf16[640,640]{1,0:T(8,128)(2,1)S(1)} all-gather(bf16[40,640]{1,0:T(8,128)(2,1)S(1)} %reshape.9), channel_id=1, replica_groups=mesh['z'=16,'y_hi'=2,'core'=2,'bal_hi'=2,'bal_lo'=2,'tensor'=4] {'z'}, dimensions={0}, use_global_device_ids=true | all-gather | bytes 870400 | tf_op jit(solution)/shard_map/all_gather | solution.py:276
  98.4 3.5 %collective-permute-start.5 = (bf16[320,640]{1,0:T(8,128)(2,1)S(1)}, bf16[320,640]{1,0:T(8,128)(2,1)S(1)}, u32[]{:S(2)}, u32[]{:S(2)}) collective-permute-start(bf16[320,640]{1,0:T(8,128)(2,1)S(1)} %get-tuple-element.18.refs_0_), channel_id=1, source_target_pairs={{0,1},{1,2},{2,3},{3,32},{32,33},{33,34},{34,35},{35,0},{4,5},{5,6... | collective-permute-start | bytes 1228808 | tf_op jit(solution)/shard_map/ppermute | solution.py:250
  101.9 3.6 %collective-permute-start.3 = (bf16[320,640]{1,0:T(8,128)(2,1)S(1)}, bf16[320,640]{1,0:T(8,128)(2,1)S(1)}, u32[]{:S(2)}, u32[]{:S(2)}) collective-permute-start(bf16[320,640]{1,0:T(8,128)(2,1)S(1)} %get-tuple-element.17.refs_1_), channel_id=1, source_target_pairs={{0,35},{1,0},{2,1},{3,2},{32,3},{33,32},{34,33},{35,34},{4,39},{5,... | collective-permute-start | bytes 1228808 | tf_op jit(solution)/shard_map/ppermute | solution.py:253
  105.5 1.9 collective-permute-start.7
  107.4 4.6 %collective-permute-start.1 = (bf16[320,640]{1,0:T(8,128)(2,1)S(1)}, bf16[320,640]{1,0:T(8,128)(2,1)}, u32[]{:S(2)}, u32[]{:S(2)}) collective-permute-start(bf16[320,640]{1,0:T(8,128)(2,1)S(1)} %get-tuple-element.18.refs_0_), channel_id=1, source_target_pairs={{0,35},{1,0},{2,1},{3,2},{32,3},{33,32},{34,33},{35,34},{4,39},{5,... | collective-permute-start | bytes 1228808 | tf_op jit(solution)/shard_map/ppermute | solution.py:253
  112.0 1.9 collective-permute-start.6
  114.0 4.6 %collective-permute-start.4 = (bf16[320,640]{1,0:T(8,128)(2,1)S(1)}, bf16[320,640]{1,0:T(8,128)(2,1)}, u32[]{:S(2)}, u32[]{:S(2)}) collective-permute-start(bf16[320,640]{1,0:T(8,128)(2,1)S(1)} %collective-permute-done.3.refs_5_), channel_id=1, source_target_pairs={{0,35},{1,0},{2,1},{3,2},{32,3},{33,32},{34,33},{35,34},{4,39},{5,... | collective-permute-start | bytes 1228808 | tf_op jit(solution)/shard_map/ppermute | solution.py:253
  120.1 1.9 collective-permute-start.8
  122.0 4.6 %collective-permute-start.2 = (bf16[320,640]{1,0:T(8,128)(2,1)}, bf16[320,640]{1,0:T(8,128)(2,1)}, u32[]{:S(2)}, u32[]{:S(2)}) collective-permute-start(bf16[320,640]{1,0:T(8,128)(2,1)} %collective-permute-done.1.refs_4_), channel_id=1, source_target_pairs={{0,35},{1,0},{2,1},{3,2},{32,3},{33,32},{34,33},{35,34},{4,39},{5,... | collective-permute-start | bytes 1228808 | tf_op jit(solution)/shard_map/ppermute | solution.py:253
  128.4 11.5 %collective-permute-start = (bf16[2,128,1280]{2,1,0:T(8,128)(2,1)S(1)}, bf16[2,128,1280]{2,1,0:T(8,128)(2,1)S(1)}, u32[]{:S(2)}, u32[]{:S(2)}) collective-permute-start(bf16[2,128,1280]{2,1,0:T(8,128)(2,1)S(1)} %get-tuple-element.13.own_ref), channel_id=1, source_target_pairs={{0,16},{16,0},{1,17},{17,1},{2,18},{18,2},{3,19},{19,3},{4,20},{20... | collective-permute-start | bytes 1966088 | tf_op jit(solution)/shard_map/ppermute | solution.py:279
  139.9 1.9 collective-permute-start.9
  141.8 4.6 %collective-permute-start.12 = (bf16[320,640]{1,0:T(8,128)(2,1)}, bf16[320,640]{1,0:T(8,128)(2,1)S(1)}, u32[]{:S(2)}, u32[]{:S(2)}) collective-permute-start(bf16[320,640]{1,0:T(8,128)(2,1)} %collective-permute-done.4.refs_1_), channel_id=1, source_target_pairs={{0,35},{1,0},{2,1},{3,2},{32,3},{33,32},{34,33},{35,34},{4,39},{5,... | collective-permute-start | bytes 1228808 | tf_op jit(solution)/shard_map/ppermute | solution.py:253
  146.4 1.9 collective-permute-start.10
  148.4 4.6 %collective-permute-start.11 = (bf16[320,640]{1,0:T(8,128)(2,1)}, bf16[320,640]{1,0:T(8,128)(2,1)S(1)}, u32[]{:S(2)}, u32[]{:S(2)}) collective-permute-start(bf16[320,640]{1,0:T(8,128)(2,1)} %collective-permute-done.2.refs_0_), channel_id=1, source_target_pairs={{0,35},{1,0},{2,1},{3,2},{32,3},{33,32},{34,33},{35,34},{4,39},{5,... | collective-permute-start | bytes 1228808 | tf_op jit(solution)/shard_map/ppermute | solution.py:253
  154.3 1.9 collective-permute-start.13
  156.2 4.6 %collective-permute-start.14 = (bf16[320,640]{1,0:T(8,128)(2,1)S(1)}, bf16[320,640]{1,0:T(8,128)(2,1)S(1)}, u32[]{:S(2)}, u32[]{:S(2)}) collective-permute-start(bf16[320,640]{1,0:T(8,128)(2,1)S(1)} %collective-permute-done.12.refs_9_), channel_id=1, source_target_pairs={{0,35},{1,0},{2,1},{3,2},{32,3},{33,32},{34,33},{35,34},{4,39},{5,... | collective-permute-start | bytes 1228808 | tf_op jit(solution)/shard_map/ppermute | solution.py:253
  160.8 2.3 %collective-permute-done.10.refs_7_ = bf16[320,640]{1,0:T(8,128)(2,1)S(1)} collective-permute-done((bf16[320,640]{1,0:T(8,128)(2,1)}, bf16[320,640]{1,0:T(8,128)(2,1)S(1)}, u32[]{:S(2)}, u32[]{:S(2)}) %collective-permute-start.10) | collective-permute-done | bytes 409632 | tf_op jit(solution)/shard_map/ppermute | solution.py:250
  164.8 6.9 %early_body.1.early_ref = f32[1280,512]{1,0:T(8,128)S(1)} custom-call(s32[3]{0:T(128)S(1)} %pad_add_fusion.where_ref, bf16[2,128,1280]{2,1,0:T(8,128)(2,1)S(1)} %get-tuple-element.13.own_ref, bf16[2,128,1280]{2,1,0:T(8,128)(2,1)S(1)} %collective-permute-done.other_ref, bf16[320,640]{1,0:T(8,128)(2,1)} %collective-permute-done.2.refs_0_, ...), custom_call_target="tpu_custom_call" | custom-call | flops 2516582400 | bytes 4915200 | tf_op jit(solution)/shard_map/early_body/pallas_call | solution.py:219
  172.7 3.3 %late_body.1 = (bf16[2,1280,128]{2,1,0:T(8,128)(2,1)S(1)}, bf16[2,1280,128]{2,1,0:T(8,128)(2,1)S(1)}) custom-call(s32[3]{0:T(128)S(1)} %pad_add_fusion.where_ref, bf16[2,128,1280]{2,1,0:T(8,128)(2,1)S(1)} %get-tuple-element.13.own_ref, bf16[2,128,1280]{2,1,0:T(8,128)(2,1)S(1)} %collective-permute-done.other_ref, f32[1280,512]{1,0:T(8,128)S(1)} %early_body.1.early_ref, ...), custom_call_target="tpu_custom_call" | custom-call | flops 838860800 | bytes 1638400 | tf_op jit(solution)/shard_map/late_body/pallas_call | solution.py:219
  176.0 3.0 %collective-permute-start.15 = (bf16[2,1280,128]{2,1,0:T(8,128)(2,1)S(1)}, bf16[2,1280,128]{2,1,0:T(8,128)(2,1)S(1)}, u32[]{:S(2)}, u32[]{:S(2)}) collective-permute-start(bf16[2,1280,128]{2,1,0:T(8,128)(2,1)S(1)} %get-tuple-element.16), channel_id=1, source_target_pairs={{0,16},{16,0},{1,17},{17,1},{2,18},{18,2},{3,19},{19,3},{4,20},{20... | collective-permute-start | bytes 1966088 | tf_op jit(solution)/shard_map/ppermute | solution.py:287
  181.0 26.3 %all_to_all.15 = bf16[8,320,128]{2,1,0:T(8,128)(2,1)S(1)} all-to-all(bf16[8,320,128]{2,1,0:T(8,128)(2,1)S(1)} %bitcast.14), channel_id=1, replica_groups=mesh['z'=16,'y_hi'=2,'core'=2,'bal_hi'=2,'bal_lo'=2,'tensor'=4] {'bal_hi..., dimensions={0} | all-to-all | bytes 1310720 | tf_op jit(solution)/shard_map/all_to_all | solution.py:291
  (50 shorter events, 14.0 us)
Async XLA Ops:
  2.3 60.3 %all-to-all-start = ((bf16[2,20,640]{2,1,0:T(8,128)(2,1)}), bf16[2,20,640]{2,1,0:T(8,128)(2,1)S(1)}, u32[]{:S(2)}, u32[]{:S(2)}) async-start(bf16[2,20,640]{2,1,0:T(8,128)(2,1)} %cut.1), calls=%async_computation | async-start | bytes 122880 | tf_op jit(solution)/shard_map/all_to_all | solution.py:271
  62.6 63.9 %all-to-all-start.1 = ((bf16[16,320,128]{2,1,0:T(8,128)(2,1)}), bf16[16,320,128]{2,1,0:T(8,128)(2,1)S(1)}, u32[]{:S(2)}, u32[]{:S(2)}) async-start(bf16[16,320,128]{2,1,0:T(8,128)(2,1)} %rotate.1), calls=%async_computation.1 | async-start | bytes 2621440 | tf_op jit(solution)/shard_map/all_to_all | solution.py:275
  66.4 60.2 %copy-start.3 = (s32[1,4]{1,0:T(1,128)S(1)}, s32[1,4]{1,0:T(1,128)}, u32[]{:S(2)}) copy-start(s32[1,4]{1,0:T(1,128)} %param.6) | copy-start | bytes 52
  66.4 60.2 %copy-start.5 = (s32[1,4]{1,0:T(1,128)S(1)}, s32[1,4]{1,0:T(1,128)}, u32[]{:S(2)}) copy-start(s32[1,4]{1,0:T(1,128)} %param.7) | copy-start | bytes 52
  98.4 13.6 %collective-permute-start.5 = (bf16[320,640]{1,0:T(8,128)(2,1)S(1)}, bf16[320,640]{1,0:T(8,128)(2,1)S(1)}, u32[]{:S(2)}, u32[]{:S(2)}) collective-permute-start(bf16[320,640]{1,0:T(8,128)(2,1)S(1)} %get-tuple-element.18.refs_0_), channel_id=1, source_target_pairs={{0,1},{1,2},{2,3},{3,32},{32,33},{33,34},{34,35},{35,0},{4,5},{5,6... | collective-permute-start | bytes 1228808 | tf_op jit(solution)/shard_map/ppermute | solution.py:250
  101.9 12.1 %collective-permute-start.3 = (bf16[320,640]{1,0:T(8,128)(2,1)S(1)}, bf16[320,640]{1,0:T(8,128)(2,1)S(1)}, u32[]{:S(2)}, u32[]{:S(2)}) collective-permute-start(bf16[320,640]{1,0:T(8,128)(2,1)S(1)} %get-tuple-element.17.refs_1_), channel_id=1, source_target_pairs={{0,35},{1,0},{2,1},{3,2},{32,3},{33,32},{34,33},{35,34},{4,39},{5,... | collective-permute-start | bytes 1228808 | tf_op jit(solution)/shard_map/ppermute | solution.py:253
  105.5 14.6 %collective-permute-start.7 = (bf16[320,640]{1,0:T(8,128)(2,1)S(1)}, bf16[320,640]{1,0:T(8,128)(2,1)S(1)}, u32[]{:S(2)}, u32[]{:S(2)}) collective-permute-start(bf16[320,640]{1,0:T(8,128)(2,1)S(1)} %get-tuple-element.17.refs_1_), channel_id=1, source_target_pairs={{0,1},{1,2},{2,3},{3,32},{32,33},{33,34},{34,35},{35,0},{4,5},{5,6... | collective-permute-start | bytes 1228808 | tf_op jit(solution)/shard_map/ppermute | solution.py:250
  107.4 14.6 %collective-permute-start.1 = (bf16[320,640]{1,0:T(8,128)(2,1)S(1)}, bf16[320,640]{1,0:T(8,128)(2,1)}, u32[]{:S(2)}, u32[]{:S(2)}) collective-permute-start(bf16[320,640]{1,0:T(8,128)(2,1)S(1)} %get-tuple-element.18.refs_0_), channel_id=1, source_target_pairs={{0,35},{1,0},{2,1},{3,2},{32,3},{33,32},{34,33},{35,34},{4,39},{5,... | collective-permute-start | bytes 1228808 | tf_op jit(solution)/shard_map/ppermute | solution.py:253
  112.0 52.1 %copy-start.6 = (bf16[320,640]{1,0:T(8,128)(2,1)}, bf16[320,640]{1,0:T(8,128)(2,1)S(1)}, u32[]{:S(2)}) copy-start(bf16[320,640]{1,0:T(8,128)(2,1)S(1)} %collective-permute-done.5.refs_10_) | copy-start | bytes 1228804
  112.0 27.9 %collective-permute-start.6 = (bf16[320,640]{1,0:T(8,128)(2,1)S(1)}, bf16[320,640]{1,0:T(8,128)(2,1)}, u32[]{:S(2)}, u32[]{:S(2)}) collective-permute-start(bf16[320,640]{1,0:T(8,128)(2,1)S(1)} %collective-permute-done.5.refs_10_), channel_id=1, source_target_pairs={{0,1},{1,2},{2,3},{3,32},{32,33},{33,34},{34,35},{35,0},{4,5},{5,6... | collective-permute-start | bytes 1228808 | tf_op jit(solution)/shard_map/ppermute | solution.py:250
  113.9 50.1 %copy-start.7 = (bf16[320,640]{1,0:T(8,128)(2,1)}, bf16[320,640]{1,0:T(8,128)(2,1)S(1)}, u32[]{:S(2)}) copy-start(bf16[320,640]{1,0:T(8,128)(2,1)S(1)} %collective-permute-done.3.refs_5_) | copy-start | bytes 1228804
  114.0 27.9 %collective-permute-start.4 = (bf16[320,640]{1,0:T(8,128)(2,1)S(1)}, bf16[320,640]{1,0:T(8,128)(2,1)}, u32[]{:S(2)}, u32[]{:S(2)}) collective-permute-start(bf16[320,640]{1,0:T(8,128)(2,1)S(1)} %collective-permute-done.3.refs_5_), channel_id=1, source_target_pairs={{0,35},{1,0},{2,1},{3,2},{32,3},{33,32},{34,33},{35,34},{4,39},{5,... | collective-permute-start | bytes 1228808 | tf_op jit(solution)/shard_map/ppermute | solution.py:253
  120.1 44.0 %copy-start.8 = (bf16[320,640]{1,0:T(8,128)(2,1)}, bf16[320,640]{1,0:T(8,128)(2,1)S(1)}, u32[]{:S(2)}) copy-start(bf16[320,640]{1,0:T(8,128)(2,1)S(1)} %collective-permute-done.7.refs_11_) | copy-start | bytes 1228804
  120.1 26.3 %collective-permute-start.8 = (bf16[320,640]{1,0:T(8,128)(2,1)S(1)}, bf16[320,640]{1,0:T(8,128)(2,1)}, u32[]{:S(2)}, u32[]{:S(2)}) collective-permute-start(bf16[320,640]{1,0:T(8,128)(2,1)S(1)} %collective-permute-done.7.refs_11_), channel_id=1, source_target_pairs={{0,1},{1,2},{2,3},{3,32},{32,33},{33,34},{34,35},{35,0},{4,5},{5,6... | collective-permute-start | bytes 1228808 | tf_op jit(solution)/shard_map/ppermute | solution.py:250
  122.0 26.3 %collective-permute-start.2 = (bf16[320,640]{1,0:T(8,128)(2,1)}, bf16[320,640]{1,0:T(8,128)(2,1)}, u32[]{:S(2)}, u32[]{:S(2)}) collective-permute-start(bf16[320,640]{1,0:T(8,128)(2,1)} %collective-permute-done.1.refs_4_), channel_id=1, source_target_pairs={{0,35},{1,0},{2,1},{3,2},{32,3},{33,32},{34,33},{35,34},{4,39},{5,... | collective-permute-start | bytes 1228808 | tf_op jit(solution)/shard_map/ppermute | solution.py:253
  128.4 35.7 %collective-permute-start = (bf16[2,128,1280]{2,1,0:T(8,128)(2,1)S(1)}, bf16[2,128,1280]{2,1,0:T(8,128)(2,1)S(1)}, u32[]{:S(2)}, u32[]{:S(2)}) collective-permute-start(bf16[2,128,1280]{2,1,0:T(8,128)(2,1)S(1)} %get-tuple-element.13.own_ref), channel_id=1, source_target_pairs={{0,16},{16,0},{1,17},{17,1},{2,18},{18,2},{3,19},{19,3},{4,20},{20... | collective-permute-start | bytes 1966088 | tf_op jit(solution)/shard_map/ppermute | solution.py:279
  139.9 14.4 %collective-permute-start.9 = (bf16[320,640]{1,0:T(8,128)(2,1)}, bf16[320,640]{1,0:T(8,128)(2,1)S(1)}, u32[]{:S(2)}, u32[]{:S(2)}) collective-permute-start(bf16[320,640]{1,0:T(8,128)(2,1)} %collective-permute-done.6.refs_2_), channel_id=1, source_target_pairs={{0,1},{1,2},{2,3},{3,32},{32,33},{33,34},{34,35},{35,0},{4,5},{5,6... | collective-permute-start | bytes 1228808 | tf_op jit(solution)/shard_map/ppermute | solution.py:250
  141.8 14.4 %collective-permute-start.12 = (bf16[320,640]{1,0:T(8,128)(2,1)}, bf16[320,640]{1,0:T(8,128)(2,1)S(1)}, u32[]{:S(2)}, u32[]{:S(2)}) collective-permute-start(bf16[320,640]{1,0:T(8,128)(2,1)} %collective-permute-done.4.refs_1_), channel_id=1, source_target_pairs={{0,35},{1,0},{2,1},{3,2},{32,3},{33,32},{34,33},{35,34},{4,39},{5,... | collective-permute-start | bytes 1228808 | tf_op jit(solution)/shard_map/ppermute | solution.py:253
  146.4 16.6 %collective-permute-start.10 = (bf16[320,640]{1,0:T(8,128)(2,1)}, bf16[320,640]{1,0:T(8,128)(2,1)S(1)}, u32[]{:S(2)}, u32[]{:S(2)}) collective-permute-start(bf16[320,640]{1,0:T(8,128)(2,1)} %collective-permute-done.8.refs_3_), channel_id=1, source_target_pairs={{0,1},{1,2},{2,3},{3,32},{32,33},{33,34},{34,35},{35,0},{4,5},{5,6... | collective-permute-start | bytes 1228808 | tf_op jit(solution)/shard_map/ppermute | solution.py:250
  148.4 15.7 %collective-permute-start.11 = (bf16[320,640]{1,0:T(8,128)(2,1)}, bf16[320,640]{1,0:T(8,128)(2,1)S(1)}, u32[]{:S(2)}, u32[]{:S(2)}) collective-permute-start(bf16[320,640]{1,0:T(8,128)(2,1)} %collective-permute-done.2.refs_0_), channel_id=1, source_target_pairs={{0,35},{1,0},{2,1},{3,2},{32,3},{33,32},{34,33},{35,34},{4,39},{5,... | collective-permute-start | bytes 1228808 | tf_op jit(solution)/shard_map/ppermute | solution.py:253
  154.3 9.8 %copy-start.9 = (bf16[320,640]{1,0:T(8,128)(2,1)}, bf16[320,640]{1,0:T(8,128)(2,1)S(1)}, u32[]{:S(2)}) copy-start(bf16[320,640]{1,0:T(8,128)(2,1)S(1)} %collective-permute-done.9.refs_6_) | copy-start | bytes 1228804
  154.3 17.6 %collective-permute-start.13 = (bf16[320,640]{1,0:T(8,128)(2,1)S(1)}, bf16[320,640]{1,0:T(8,128)(2,1)S(1)}, u32[]{:S(2)}, u32[]{:S(2)}) collective-permute-start(bf16[320,640]{1,0:T(8,128)(2,1)S(1)} %collective-permute-done.9.refs_6_), channel_id=1, source_target_pairs={{0,1},{1,2},{2,3},{3,32},{32,33},{33,34},{34,35},{35,0},{4,5},{5,6... | collective-permute-start | bytes 1228808 | tf_op jit(solution)/shard_map/ppermute | solution.py:250
  156.2 16.5 %collective-permute-start.14 = (bf16[320,640]{1,0:T(8,128)(2,1)S(1)}, bf16[320,640]{1,0:T(8,128)(2,1)S(1)}, u32[]{:S(2)}, u32[]{:S(2)}) collective-permute-start(bf16[320,640]{1,0:T(8,128)(2,1)S(1)} %collective-permute-done.12.refs_9_), channel_id=1, source_target_pairs={{0,35},{1,0},{2,1},{3,2},{32,3},{33,32},{34,33},{35,34},{4,39},{5,... | collective-permute-start | bytes 1228808 | tf_op jit(solution)/shard_map/ppermute | solution.py:253
  176.0 4.7 %collective-permute-start.15 = (bf16[2,1280,128]{2,1,0:T(8,128)(2,1)S(1)}, bf16[2,1280,128]{2,1,0:T(8,128)(2,1)S(1)}, u32[]{:S(2)}, u32[]{:S(2)}) collective-permute-start(bf16[2,1280,128]{2,1,0:T(8,128)(2,1)S(1)} %get-tuple-element.16), channel_id=1, source_target_pairs={{0,16},{16,0},{1,17},{17,1},{2,18},{18,2},{3,19},{19,3},{4,20},{20... | collective-permute-start | bytes 1966088 | tf_op jit(solution)/shard_map/ppermute | solution.py:287
  (7 other events, 12.5 us)

commit v5 on v4

--- a/solution.py
+++ b/solution.py
@@ -38,7 +38,7 @@
         out_shape=jax.ShapeDtypeStruct((2, out_weight.shape[0], 4 * WIDTH), jnp.bfloat16),
         compiler_params=vmem_params(),
         name="cut",
-    )(qkv_weight, out_weight)
+    )(*[pltpu.with_memory_space_constraint(w, pltpu.HBM) for w in (qkv_weight, out_weight)])
 
 
 def in_turn(counts_ref, order_ref):
@@ -72,7 +72,7 @@
         rotate_body,
         out_shape=jax.ShapeDtypeStruct(tiles.shape, tiles.dtype),
         in_specs=[in_smem, in_smem, in_smem, pl.BlockSpec(memory_space=pl.ANY)],
-        out_specs=pl.BlockSpec(memory_space=pl.ANY),
+        out_specs=pl.BlockSpec(memory_space=pltpu.VMEM),
         scratch_shapes=[pltpu.SemaphoreType.DMA((SLOTS,))],
         compiler_params=vmem_params(),
         name="rotate",

time: 209 us -> 170 us (0.81)
  Pallas kernels: 54.2 us -> 16.6 us
    pallas_call x1, Pallas kernels: 41.5 us -> 3.13 us  [rotate(): pl.pallas_call(rotate_body, out_shape=jax.ShapeDtypeStruct(tiles.shape, t...]
    unnamed x27 -> x23, local copies, waits for them, and re-layouts: 4.42 us -> 2.89 us
  transfers between devices with their start and end apart: 18 -> 18, of which waited for: 7 -> 7; matrix products, arithmetic and copies ran while one was open for 0% -> 0% of each run, Pallas kernels for 24% -> 7%
where the time goes in v5:
time: 170 us; the launch traced here: 169 us
  starting transfers between devices  81.6 us (48%)
  blocking collectives  58.2 us (34%)
  Pallas kernels  16.6 us (10%)
  waiting for transfers between devices  8.87 us (5%)
  local copies, waits for them, and re-layouts  2.97 us (2%)
    all_gather x1, blocking collectives, local(): block = lax.all_gather(both, 'z', axis=0, tiled=True)  32 us
    ppermute x7, starting transfers between devices, around_y(): falling[k] = lax.ppermute(falling[k], ('y_hi', 'tensor'), down)  31 us
    all_to_all x1, blocking collectives, local(): lax.all_to_all(encoded.reshape(8, D // 4, PATCH), ('bal_hi', 'tensor'), 0...  26.3 us
    all_to_all x1, starting transfers between devices, local(): lax.all_to_all(halves, 'core', 0, 0, tiled=True).reshape(-1, 4 * WIDTH)  17.4 us
    ppermute x7, starting transfers between devices, around_y(): rising[k] = lax.ppermute(rising[k], ('y_hi', 'tensor'), up)  15 us
    ppermute x1, starting transfers between devices, local(): other = lax.ppermute(normed, 'core', swap)  11.5 us
    pallas_call x2, Pallas kernels, encode(): pl.pallas_call(body, out_shape=out_shape, in_specs=[pl.BlockSpec(memory_s...  10.2 us
    ppermute x7, waiting for transfers between devices, around_y(): rising[k] = lax.ppermute(rising[k], ('y_hi', 'tensor'), up)  5.3 us
  transfers between devices with their start and end apart: 18, of which 7 were waited for; matrix products, arithmetic and copies ran while one was open for 0% of the time, Pallas kernels for 7%

profile of v5, /device:TPU:1, one launch (start us, length us, event | category | flops | bytes accessed | tf_op | source)
XLA Modules:
  0.0 169.0 jit_solution(11116461397535583306)
XLA Ops:
  1.5 17.4 %all-to-all-start = ((bf16[2,20,640]{2,1,0:T(8,128)(2,1)}), bf16[2,20,640]{2,1,0:T(8,128)(2,1)S(1)}, u32[]{:S(2)}, u32[]{:S(2)}) async-start(bf16[2,20,640]{2,1,0:T(8,128)(2,1)} %cut.1), calls=%async_computation | async-start | bytes 122880 | tf_op jit(solution)/shard_map/all_to_all | solution.py:271
  20.4 3.1 %rotate.1 = bf16[16,320,128]{2,1,0:T(8,128)(2,1)} custom-call(s32[3]{0:T(128)S(1)} %pad_add_fusion.where_ref, s32[4]{0:T(128)S(1)} %bitcast.10, s32[4]{0:T(128)S(1)} %bitcast.12, bf16[16,320,128]{2,1,0:T(8,128)(2,1)} %bitcast.16), custom_call_target="tpu_custom_call" | custom-call | tf_op jit(solution)/shard_map/rotate/pallas_call | solution.py:71
  23.5 3.7 %all-to-all-start.1 = ((bf16[16,320,128]{2,1,0:T(8,128)(2,1)}), bf16[16,320,128]{2,1,0:T(8,128)(2,1)S(1)}, u32[]{:S(2)}, u32[]{:S(2)}) async-start(bf16[16,320,128]{2,1,0:T(8,128)(2,1)} %rotate.1), calls=%async_computation.1 | async-start | bytes 2621440 | tf_op jit(solution)/shard_map/all_to_all | solution.py:275
  27.3 32.0 %all_gather.3 = bf16[640,640]{1,0:T(8,128)(2,1)S(1)} all-gather(bf16[40,640]{1,0:T(8,128)(2,1)S(1)} %reshape.9), channel_id=1, replica_groups=mesh['z'=16,'y_hi'=2,'core'=2,'bal_hi'=2,'bal_lo'=2,'tensor'=4] {'z'}, dimensions={0}, use_global_device_ids=true | all-gather | bytes 870400 | tf_op jit(solution)/shard_map/all_gather | solution.py:276
  59.3 3.5 %collective-permute-start.5 = (bf16[320,640]{1,0:T(8,128)(2,1)S(1)}, bf16[320,640]{1,0:T(8,128)(2,1)S(1)}, u32[]{:S(2)}, u32[]{:S(2)}) collective-permute-start(bf16[320,640]{1,0:T(8,128)(2,1)S(1)} %get-tuple-element.18.refs_0_), channel_id=1, source_target_pairs={{0,1},{1,2},{2,3},{3,32},{32,33},{33,34},{34,35},{35,0},{4,5},{5,6... | collective-permute-start | bytes 1228808 | tf_op jit(solution)/shard_map/ppermute | solution.py:250
  62.8 3.6 %collective-permute-start.3 = (bf16[320,640]{1,0:T(8,128)(2,1)S(1)}, bf16[320,640]{1,0:T(8,128)(2,1)S(1)}, u32[]{:S(2)}, u32[]{:S(2)}) collective-permute-start(bf16[320,640]{1,0:T(8,128)(2,1)S(1)} %get-tuple-element.17.refs_1_), channel_id=1, source_target_pairs={{0,35},{1,0},{2,1},{3,2},{32,3},{33,32},{34,33},{35,34},{4,39},{5,... | collective-permute-start | bytes 1228808 | tf_op jit(solution)/shard_map/ppermute | solution.py:253
  66.4 1.9 %collective-permute-start.7 = (bf16[320,640]{1,0:T(8,128)(2,1)S(1)}, bf16[320,640]{1,0:T(8,128)(2,1)S(1)}, u32[]{:S(2)}, u32[]{:S(2)}) collective-permute-start(bf16[320,640]{1,0:T(8,128)(2,1)S(1)} %get-tuple-element.17.refs_1_), channel_id=1, source_target_pairs={{0,1},{1,2},{2,3},{3,32},{32,33},{33,34},{34,35},{35,0},{4,5},{5,6... | collective-permute-start | bytes 1228808 | tf_op jit(solution)/shard_map/ppermute | solution.py:250
  68.3 4.6 %collective-permute-start.1 = (bf16[320,640]{1,0:T(8,128)(2,1)S(1)}, bf16[320,640]{1,0:T(8,128)(2,1)}, u32[]{:S(2)}, u32[]{:S(2)}) collective-permute-start(bf16[320,640]{1,0:T(8,128)(2,1)S(1)} %get-tuple-element.18.refs_0_), channel_id=1, source_target_pairs={{0,35},{1,0},{2,1},{3,2},{32,3},{33,32},{34,33},{35,34},{4,39},{5,... | collective-permute-start | bytes 1228808 | tf_op jit(solution)/shard_map/ppermute | solution.py:253
  72.9 1.9 %collective-permute-start.6 = (bf16[320,640]{1,0:T(8,128)(2,1)S(1)}, bf16[320,640]{1,0:T(8,128)(2,1)}, u32[]{:S(2)}, u32[]{:S(2)}) collective-permute-start(bf16[320,640]{1,0:T(8,128)(2,1)S(1)} %collective-permute-done.5.refs_10_), channel_id=1, source_target_pairs={{0,1},{1,2},{2,3},{3,32},{32,33},{33,34},{34,35},{35,0},{4,5},{5,6... | collective-permute-start | bytes 1228808 | tf_op jit(solution)/shard_map/ppermute | solution.py:250
  74.9 4.6 %collective-permute-start.4 = (bf16[320,640]{1,0:T(8,128)(2,1)S(1)}, bf16[320,640]{1,0:T(8,128)(2,1)}, u32[]{:S(2)}, u32[]{:S(2)}) collective-permute-start(bf16[320,640]{1,0:T(8,128)(2,1)S(1)} %collective-permute-done.3.refs_5_), channel_id=1, source_target_pairs={{0,35},{1,0},{2,1},{3,2},{32,3},{33,32},{34,33},{35,34},{4,39},{5,... | collective-permute-start | bytes 1228808 | tf_op jit(solution)/shard_map/ppermute | solution.py:253
  81.0 1.9 %collective-permute-start.8 = (bf16[320,640]{1,0:T(8,128)(2,1)S(1)}, bf16[320,640]{1,0:T(8,128)(2,1)}, u32[]{:S(2)}, u32[]{:S(2)}) collective-permute-start(bf16[320,640]{1,0:T(8,128)(2,1)S(1)} %collective-permute-done.7.refs_11_), channel_id=1, source_target_pairs={{0,1},{1,2},{2,3},{3,32},{32,33},{33,34},{34,35},{35,0},{4,5},{5,6... | collective-permute-start | bytes 1228808 | tf_op jit(solution)/shard_map/ppermute | solution.py:250
  82.9 4.6 %collective-permute-start.2 = (bf16[320,640]{1,0:T(8,128)(2,1)}, bf16[320,640]{1,0:T(8,128)(2,1)}, u32[]{:S(2)}, u32[]{:S(2)}) collective-permute-start(bf16[320,640]{1,0:T(8,128)(2,1)} %collective-permute-done.1.refs_4_), channel_id=1, source_target_pairs={{0,35},{1,0},{2,1},{3,2},{32,3},{33,32},{34,33},{35,34},{4,39},{5,... | collective-permute-start | bytes 1228808 | tf_op jit(solution)/shard_map/ppermute | solution.py:253
  89.3 11.5 %collective-permute-start = (bf16[2,128,1280]{2,1,0:T(8,128)(2,1)S(1)}, bf16[2,128,1280]{2,1,0:T(8,128)(2,1)S(1)}, u32[]{:S(2)}, u32[]{:S(2)}) collective-permute-start(bf16[2,128,1280]{2,1,0:T(8,128)(2,1)S(1)} %get-tuple-element.13.own_ref), channel_id=1, source_target_pairs={{0,16},{16,0},{1,17},{17,1},{2,18},{18,2},{3,19},{19,3},{4,20},{20... | collective-permute-start | bytes 1966088 | tf_op jit(solution)/shard_map/ppermute | solution.py:279
  100.8 1.9 %collective-permute-start.9 = (bf16[320,640]{1,0:T(8,128)(2,1)}, bf16[320,640]{1,0:T(8,128)(2,1)S(1)}, u32[]{:S(2)}, u32[]{:S(2)}) collective-permute-start(bf16[320,640]{1,0:T(8,128)(2,1)} %collective-permute-done.6.refs_2_), channel_id=1, source_target_pairs={{0,1},{1,2},{2,3},{3,32},{32,33},{33,34},{34,35},{35,0},{4,5},{5,6... | collective-permute-start | bytes 1228808 | tf_op jit(solution)/shard_map/ppermute | solution.py:250
  102.7 4.6 %collective-permute-start.12 = (bf16[320,640]{1,0:T(8,128)(2,1)}, bf16[320,640]{1,0:T(8,128)(2,1)S(1)}, u32[]{:S(2)}, u32[]{:S(2)}) collective-permute-start(bf16[320,640]{1,0:T(8,128)(2,1)} %collective-permute-done.4.refs_1_), channel_id=1, source_target_pairs={{0,35},{1,0},{2,1},{3,2},{32,3},{33,32},{34,33},{35,34},{4,39},{5,... | collective-permute-start | bytes 1228808 | tf_op jit(solution)/shard_map/ppermute | solution.py:253
  107.3 1.9 %collective-permute-start.10 = (bf16[320,640]{1,0:T(8,128)(2,1)}, bf16[320,640]{1,0:T(8,128)(2,1)S(1)}, u32[]{:S(2)}, u32[]{:S(2)}) collective-permute-start(bf16[320,640]{1,0:T(8,128)(2,1)} %collective-permute-done.8.refs_3_), channel_id=1, source_target_pairs={{0,1},{1,2},{2,3},{3,32},{32,33},{33,34},{34,35},{35,0},{4,5},{5,6... | collective-permute-start | bytes 1228808 | tf_op jit(solution)/shard_map/ppermute | solution.py:250
  109.3 4.6 %collective-permute-start.11 = (bf16[320,640]{1,0:T(8,128)(2,1)}, bf16[320,640]{1,0:T(8,128)(2,1)S(1)}, u32[]{:S(2)}, u32[]{:S(2)}) collective-permute-start(bf16[320,640]{1,0:T(8,128)(2,1)} %collective-permute-done.2.refs_0_), channel_id=1, source_target_pairs={{0,35},{1,0},{2,1},{3,2},{32,3},{33,32},{34,33},{35,34},{4,39},{5,... | collective-permute-start | bytes 1228808 | tf_op jit(solution)/shard_map/ppermute | solution.py:253
  115.2 1.9 %collective-permute-start.13 = (bf16[320,640]{1,0:T(8,128)(2,1)S(1)}, bf16[320,640]{1,0:T(8,128)(2,1)S(1)}, u32[]{:S(2)}, u32[]{:S(2)}) collective-permute-start(bf16[320,640]{1,0:T(8,128)(2,1)S(1)} %collective-permute-done.9.refs_6_), channel_id=1, source_target_pairs={{0,1},{1,2},{2,3},{3,32},{32,33},{33,34},{34,35},{35,0},{4,5},{5,6... | collective-permute-start | bytes 1228808 | tf_op jit(solution)/shard_map/ppermute | solution.py:250
  117.1 4.6 %collective-permute-start.14 = (bf16[320,640]{1,0:T(8,128)(2,1)S(1)}, bf16[320,640]{1,0:T(8,128)(2,1)S(1)}, u32[]{:S(2)}, u32[]{:S(2)}) collective-permute-start(bf16[320,640]{1,0:T(8,128)(2,1)S(1)} %collective-permute-done.12.refs_9_), channel_id=1, source_target_pairs={{0,35},{1,0},{2,1},{3,2},{32,3},{33,32},{34,33},{35,34},{4,39},{5,... | collective-permute-start | bytes 1228808 | tf_op jit(solution)/shard_map/ppermute | solution.py:253
  121.7 2.3 %collective-permute-done.10.refs_7_ = bf16[320,640]{1,0:T(8,128)(2,1)S(1)} collective-permute-done((bf16[320,640]{1,0:T(8,128)(2,1)}, bf16[320,640]{1,0:T(8,128)(2,1)S(1)}, u32[]{:S(2)}, u32[]{:S(2)}) %collective-permute-start.10) | collective-permute-done | bytes 409632 | tf_op jit(solution)/shard_map/ppermute | solution.py:250
  125.7 6.9 %early_body.1.early_ref = f32[1280,512]{1,0:T(8,128)S(1)} custom-call(s32[3]{0:T(128)S(1)} %pad_add_fusion.where_ref, bf16[2,128,1280]{2,1,0:T(8,128)(2,1)S(1)} %get-tuple-element.13.own_ref, bf16[2,128,1280]{2,1,0:T(8,128)(2,1)S(1)} %collective-permute-done.other_ref, bf16[320,640]{1,0:T(8,128)(2,1)} %collective-permute-done.2.refs_0_, ...), custom_call_target="tpu_custom_call" | custom-call | flops 2516582400 | bytes 4915200 | tf_op jit(solution)/shard_map/early_body/pallas_call | solution.py:219
  133.6 3.3 %late_body.1 = (bf16[2,1280,128]{2,1,0:T(8,128)(2,1)S(1)}, bf16[2,1280,128]{2,1,0:T(8,128)(2,1)S(1)}) custom-call(s32[3]{0:T(128)S(1)} %pad_add_fusion.where_ref, bf16[2,128,1280]{2,1,0:T(8,128)(2,1)S(1)} %get-tuple-element.13.own_ref, bf16[2,128,1280]{2,1,0:T(8,128)(2,1)S(1)} %collective-permute-done.other_ref, f32[1280,512]{1,0:T(8,128)S(1)} %early_body.1.early_ref, ...), custom_call_target="tpu_custom_call" | custom-call | flops 838860800 | bytes 1638400 | tf_op jit(solution)/shard_map/late_body/pallas_call | solution.py:219
  136.9 3.0 %collective-permute-start.15 = (bf16[2,1280,128]{2,1,0:T(8,128)(2,1)S(1)}, bf16[2,1280,128]{2,1,0:T(8,128)(2,1)S(1)}, u32[]{:S(2)}, u32[]{:S(2)}) collective-permute-start(bf16[2,1280,128]{2,1,0:T(8,128)(2,1)S(1)} %get-tuple-element.16), channel_id=1, source_target_pairs={{0,16},{16,0},{1,17},{17,1},{2,18},{18,2},{3,19},{19,3},{4,20},{20... | collective-permute-start | bytes 1966088 | tf_op jit(solution)/shard_map/ppermute | solution.py:287
  141.9 26.3 %all_to_all.15 = bf16[8,320,128]{2,1,0:T(8,128)(2,1)S(1)} all-to-all(bf16[8,320,128]{2,1,0:T(8,128)(2,1)S(1)} %bitcast.14), channel_id=1, replica_groups=mesh['z'=16,'y_hi'=2,'core'=2,'bal_hi'=2,'bal_lo'=2,'tensor'=4] {'bal_hi..., dimensions={0} | all-to-all | bytes 1310720 | tf_op jit(solution)/shard_map/all_to_all | solution.py:291
  (46 shorter events, 13.2 us)
Async XLA Ops:
  1.5 22.0 %all-to-all-start = ((bf16[2,20,640]{2,1,0:T(8,128)(2,1)}), bf16[2,20,640]{2,1,0:T(8,128)(2,1)S(1)}, u32[]{:S(2)}, u32[]{:S(2)}) async-start(bf16[2,20,640]{2,1,0:T(8,128)(2,1)} %cut.1), calls=%async_computation | async-start | bytes 122880 | tf_op jit(solution)/shard_map/all_to_all | solution.py:271
  23.5 63.9 %all-to-all-start.1 = ((bf16[16,320,128]{2,1,0:T(8,128)(2,1)}), bf16[16,320,128]{2,1,0:T(8,128)(2,1)S(1)}, u32[]{:S(2)}, u32[]{:S(2)}) async-start(bf16[16,320,128]{2,1,0:T(8,128)(2,1)} %rotate.1), calls=%async_computation.1 | async-start | bytes 2621440 | tf_op jit(solution)/shard_map/all_to_all | solution.py:275
  27.3 60.2 %copy-start.1 = (s32[1,4]{1,0:T(1,128)S(1)}, s32[1,4]{1,0:T(1,128)}, u32[]{:S(2)}) copy-start(s32[1,4]{1,0:T(1,128)} %param.6) | copy-start | bytes 52
  27.3 60.2 %copy-start.3 = (s32[1,4]{1,0:T(1,128)S(1)}, s32[1,4]{1,0:T(1,128)}, u32[]{:S(2)}) copy-start(s32[1,4]{1,0:T(1,128)} %param.7) | copy-start | bytes 52
  59.3 13.6 %collective-permute-start.5 = (bf16[320,640]{1,0:T(8,128)(2,1)S(1)}, bf16[320,640]{1,0:T(8,128)(2,1)S(1)}, u32[]{:S(2)}, u32[]{:S(2)}) collective-permute-start(bf16[320,640]{1,0:T(8,128)(2,1)S(1)} %get-tuple-element.18.refs_0_), channel_id=1, source_target_pairs={{0,1},{1,2},{2,3},{3,32},{32,33},{33,34},{34,35},{35,0},{4,5},{5,6... | collective-permute-start | bytes 1228808 | tf_op jit(solution)/shard_map/ppermute | solution.py:250
  62.8 12.1 %collective-permute-start.3 = (bf16[320,640]{1,0:T(8,128)(2,1)S(1)}, bf16[320,640]{1,0:T(8,128)(2,1)S(1)}, u32[]{:S(2)}, u32[]{:S(2)}) collective-permute-start(bf16[320,640]{1,0:T(8,128)(2,1)S(1)} %get-tuple-element.17.refs_1_), channel_id=1, source_target_pairs={{0,35},{1,0},{2,1},{3,2},{32,3},{33,32},{34,33},{35,34},{4,39},{5,... | collective-permute-start | bytes 1228808 | tf_op jit(solution)/shard_map/ppermute | solution.py:253
  66.4 14.6 %collective-permute-start.7 = (bf16[320,640]{1,0:T(8,128)(2,1)S(1)}, bf16[320,640]{1,0:T(8,128)(2,1)S(1)}, u32[]{:S(2)}, u32[]{:S(2)}) collective-permute-start(bf16[320,640]{1,0:T(8,128)(2,1)S(1)} %get-tuple-element.17.refs_1_), channel_id=1, source_target_pairs={{0,1},{1,2},{2,3},{3,32},{32,33},{33,34},{34,35},{35,0},{4,5},{5,6... | collective-permute-start | bytes 1228808 | tf_op jit(solution)/shard_map/ppermute | solution.py:250
  68.3 14.6 %collective-permute-start.1 = (bf16[320,640]{1,0:T(8,128)(2,1)S(1)}, bf16[320,640]{1,0:T(8,128)(2,1)}, u32[]{:S(2)}, u32[]{:S(2)}) collective-permute-start(bf16[320,640]{1,0:T(8,128)(2,1)S(1)} %get-tuple-element.18.refs_0_), channel_id=1, source_target_pairs={{0,35},{1,0},{2,1},{3,2},{32,3},{33,32},{34,33},{35,34},{4,39},{5,... | collective-permute-start | bytes 1228808 | tf_op jit(solution)/shard_map/ppermute | solution.py:253
  72.9 52.1 %copy-start.4 = (bf16[320,640]{1,0:T(8,128)(2,1)}, bf16[320,640]{1,0:T(8,128)(2,1)S(1)}, u32[]{:S(2)}) copy-start(bf16[320,640]{1,0:T(8,128)(2,1)S(1)} %collective-permute-done.5.refs_10_) | copy-start | bytes 1228804
  72.9 27.9 %collective-permute-start.6 = (bf16[320,640]{1,0:T(8,128)(2,1)S(1)}, bf16[320,640]{1,0:T(8,128)(2,1)}, u32[]{:S(2)}, u32[]{:S(2)}) collective-permute-start(bf16[320,640]{1,0:T(8,128)(2,1)S(1)} %collective-permute-done.5.refs_10_), channel_id=1, source_target_pairs={{0,1},{1,2},{2,3},{3,32},{32,33},{33,34},{34,35},{35,0},{4,5},{5,6... | collective-permute-start | bytes 1228808 | tf_op jit(solution)/shard_map/ppermute | solution.py:250
  74.8 50.1 %copy-start.5 = (bf16[320,640]{1,0:T(8,128)(2,1)}, bf16[320,640]{1,0:T(8,128)(2,1)S(1)}, u32[]{:S(2)}) copy-start(bf16[320,640]{1,0:T(8,128)(2,1)S(1)} %collective-permute-done.3.refs_5_) | copy-start | bytes 1228804
  74.9 27.9 %collective-permute-start.4 = (bf16[320,640]{1,0:T(8,128)(2,1)S(1)}, bf16[320,640]{1,0:T(8,128)(2,1)}, u32[]{:S(2)}, u32[]{:S(2)}) collective-permute-start(bf16[320,640]{1,0:T(8,128)(2,1)S(1)} %collective-permute-done.3.refs_5_), channel_id=1, source_target_pairs={{0,35},{1,0},{2,1},{3,2},{32,3},{33,32},{34,33},{35,34},{4,39},{5,... | collective-permute-start | bytes 1228808 | tf_op jit(solution)/shard_map/ppermute | solution.py:253
  81.0 44.0 %copy-start.6 = (bf16[320,640]{1,0:T(8,128)(2,1)}, bf16[320,640]{1,0:T(8,128)(2,1)S(1)}, u32[]{:S(2)}) copy-start(bf16[320,640]{1,0:T(8,128)(2,1)S(1)} %collective-permute-done.7.refs_11_) | copy-start | bytes 1228804
  81.0 26.3 %collective-permute-start.8 = (bf16[320,640]{1,0:T(8,128)(2,1)S(1)}, bf16[320,640]{1,0:T(8,128)(2,1)}, u32[]{:S(2)}, u32[]{:S(2)}) collective-permute-start(bf16[320,640]{1,0:T(8,128)(2,1)S(1)} %collective-permute-done.7.refs_11_), channel_id=1, source_target_pairs={{0,1},{1,2},{2,3},{3,32},{32,33},{33,34},{34,35},{35,0},{4,5},{5,6... | collective-permute-start | bytes 1228808 | tf_op jit(solution)/shard_map/ppermute | solution.py:250
  82.9 26.3 %collective-permute-start.2 = (bf16[320,640]{1,0:T(8,128)(2,1)}, bf16[320,640]{1,0:T(8,128)(2,1)}, u32[]{:S(2)}, u32[]{:S(2)}) collective-permute-start(bf16[320,640]{1,0:T(8,128)(2,1)} %collective-permute-done.1.refs_4_), channel_id=1, source_target_pairs={{0,35},{1,0},{2,1},{3,2},{32,3},{33,32},{34,33},{35,34},{4,39},{5,... | collective-permute-start | bytes 1228808 | tf_op jit(solution)/shard_map/ppermute | solution.py:253
  89.3 35.7 %collective-permute-start = (bf16[2,128,1280]{2,1,0:T(8,128)(2,1)S(1)}, bf16[2,128,1280]{2,1,0:T(8,128)(2,1)S(1)}, u32[]{:S(2)}, u32[]{:S(2)}) collective-permute-start(bf16[2,128,1280]{2,1,0:T(8,128)(2,1)S(1)} %get-tuple-element.13.own_ref), channel_id=1, source_target_pairs={{0,16},{16,0},{1,17},{17,1},{2,18},{18,2},{3,19},{19,3},{4,20},{20... | collective-permute-start | bytes 1966088 | tf_op jit(solution)/shard_map/ppermute | solution.py:279
  100.8 14.4 %collective-permute-start.9 = (bf16[320,640]{1,0:T(8,128)(2,1)}, bf16[320,640]{1,0:T(8,128)(2,1)S(1)}, u32[]{:S(2)}, u32[]{:S(2)}) collective-permute-start(bf16[320,640]{1,0:T(8,128)(2,1)} %collective-permute-done.6.refs_2_), channel_id=1, source_target_pairs={{0,1},{1,2},{2,3},{3,32},{32,33},{33,34},{34,35},{35,0},{4,5},{5,6... | collective-permute-start | bytes 1228808 | tf_op jit(solution)/shard_map/ppermute | solution.py:250
  102.7 14.4 %collective-permute-start.12 = (bf16[320,640]{1,0:T(8,128)(2,1)}, bf16[320,640]{1,0:T(8,128)(2,1)S(1)}, u32[]{:S(2)}, u32[]{:S(2)}) collective-permute-start(bf16[320,640]{1,0:T(8,128)(2,1)} %collective-permute-done.4.refs_1_), channel_id=1, source_target_pairs={{0,35},{1,0},{2,1},{3,2},{32,3},{33,32},{34,33},{35,34},{4,39},{5,... | collective-permute-start | bytes 1228808 | tf_op jit(solution)/shard_map/ppermute | solution.py:253
  107.3 16.6 %collective-permute-start.10 = (bf16[320,640]{1,0:T(8,128)(2,1)}, bf16[320,640]{1,0:T(8,128)(2,1)S(1)}, u32[]{:S(2)}, u32[]{:S(2)}) collective-permute-start(bf16[320,640]{1,0:T(8,128)(2,1)} %collective-permute-done.8.refs_3_), channel_id=1, source_target_pairs={{0,1},{1,2},{2,3},{3,32},{32,33},{33,34},{34,35},{35,0},{4,5},{5,6... | collective-permute-start | bytes 1228808 | tf_op jit(solution)/shard_map/ppermute | solution.py:250
  109.3 15.7 %collective-permute-start.11 = (bf16[320,640]{1,0:T(8,128)(2,1)}, bf16[320,640]{1,0:T(8,128)(2,1)S(1)}, u32[]{:S(2)}, u32[]{:S(2)}) collective-permute-start(bf16[320,640]{1,0:T(8,128)(2,1)} %collective-permute-done.2.refs_0_), channel_id=1, source_target_pairs={{0,35},{1,0},{2,1},{3,2},{32,3},{33,32},{34,33},{35,34},{4,39},{5,... | collective-permute-start | bytes 1228808 | tf_op jit(solution)/shard_map/ppermute | solution.py:253
  115.2 9.8 %copy-start.7 = (bf16[320,640]{1,0:T(8,128)(2,1)}, bf16[320,640]{1,0:T(8,128)(2,1)S(1)}, u32[]{:S(2)}) copy-start(bf16[320,640]{1,0:T(8,128)(2,1)S(1)} %collective-permute-done.9.refs_6_) | copy-start | bytes 1228804
  115.2 17.6 %collective-permute-start.13 = (bf16[320,640]{1,0:T(8,128)(2,1)S(1)}, bf16[320,640]{1,0:T(8,128)(2,1)S(1)}, u32[]{:S(2)}, u32[]{:S(2)}) collective-permute-start(bf16[320,640]{1,0:T(8,128)(2,1)S(1)} %collective-permute-done.9.refs_6_), channel_id=1, source_target_pairs={{0,1},{1,2},{2,3},{3,32},{32,33},{33,34},{34,35},{35,0},{4,5},{5,6... | collective-permute-start | bytes 1228808 | tf_op jit(solution)/shard_map/ppermute | solution.py:250
  117.1 16.5 %collective-permute-start.14 = (bf16[320,640]{1,0:T(8,128)(2,1)S(1)}, bf16[320,640]{1,0:T(8,128)(2,1)S(1)}, u32[]{:S(2)}, u32[]{:S(2)}) collective-permute-start(bf16[320,640]{1,0:T(8,128)(2,1)S(1)} %collective-permute-done.12.refs_9_), channel_id=1, source_target_pairs={{0,35},{1,0},{2,1},{3,2},{32,3},{33,32},{34,33},{35,34},{4,39},{5,... | collective-permute-start | bytes 1228808 | tf_op jit(solution)/shard_map/ppermute | solution.py:253
  136.9 4.7 %collective-permute-start.15 = (bf16[2,1280,128]{2,1,0:T(8,128)(2,1)S(1)}, bf16[2,1280,128]{2,1,0:T(8,128)(2,1)S(1)}, u32[]{:S(2)}, u32[]{:S(2)}) collective-permute-start(bf16[2,1280,128]{2,1,0:T(8,128)(2,1)S(1)} %get-tuple-element.16), channel_id=1, source_target_pairs={{0,16},{16,0},{1,17},{17,1},{2,18},{18,2},{3,19},{19,3},{4,20},{20... | collective-permute-start | bytes 1966088 | tf_op jit(solution)/shard_map/ppermute | solution.py:287
  (5 other events, 11.0 us)

commit v6 on v5

--- a/solution.py
+++ b/solution.py
@@ -12,7 +12,7 @@
 DOCS = 4
 ZS = 16
 GROUPS = 4
-PIECES = 4
+PIECES = 3
 EARLY, LATE = (2, 1, 3), (0,)
 LOCAL = 2
 WIDTH = LOCAL * HDIM
@@ -160,26 +160,30 @@
 
 
 def group_contexts(groups, where_ref, own_ref, other_ref, pieces, weight_ref, sems):
-    def copies(n, group):
-        made = []
-        for k in range(PIECES):
-            y_hi = ((where_ref[2] + group + k // 2 * GROUPS) >> 2) & 1
-            made.append(
-                pltpu.make_async_copy(
-                    pieces[n * PIECES + k], weight_ref.at[n, y_hi, k % 2], sems.at[n, k]
-                )
-            )
-        return made
-
+    half = D // 4
+    taken = iter(pieces)
+    copies = []
     for n, group in enumerate(groups):
-        for copy in copies(n, group):
+        parts = []
+        for k in range(2):
+            y_hi = ((where_ref[2] + where_ref[3] * (group + k * GROUPS)) >> 2) & 1
+            target = weight_ref.at[n, y_hi]
+            if group + k * GROUPS == GROUPS:
+                targets = [target.at[pl.ds(0, half)], target.at[pl.ds(half, half)]]
+            else:
+                targets = [target]
+            for t in targets:
+                parts.append(pltpu.make_async_copy(next(taken), t, sems.at[n, len(parts)]))
+        copies.append(parts)
+    for parts in copies:
+        for copy in parts:
             copy.start()
     normed = jnp.concatenate(
         [ref[...].reshape(2 * PATCH, D) for ref in (own_ref, other_ref)], axis=0
     )
     contexts, outs = [], []
-    for n, group in enumerate(groups):
-        for copy in copies(n, group):
+    for n, parts in enumerate(copies):
+        for copy in parts:
             copy.wait()
         weight = weight_ref[n].reshape(D, 4 * WIDTH)
         projected = jnp.dot(normed, weight[:, : 3 * WIDTH], preferred_element_type=jnp.float32)
@@ -193,26 +197,27 @@
 
 
 def early_body(where_ref, own_ref, other_ref, *refs):
-    count = len(EARLY) * PIECES
-    total_ref, weight_ref, sems = refs[count:]
+    total_ref, weight_ref, sems = refs[-3:]
     total_ref[...] = group_contexts(
-        EARLY, where_ref, own_ref, other_ref, refs[:count], weight_ref, sems
+        EARLY, where_ref, own_ref, other_ref, refs[:-3], weight_ref, sems
     )
 
 
 def late_body(where_ref, own_ref, other_ref, early_ref, *refs):
-    count = len(LATE) * PIECES
-    own_out_ref, other_out_ref, weight_ref, sems = refs[count:]
-    total = group_contexts(LATE, where_ref, own_ref, other_ref, refs[:count], weight_ref, sems)
+    outs, (weight_ref, sems) = refs[-4:-2], refs[-2:]
+    total = group_contexts(LATE, where_ref, own_ref, other_ref, refs[:-4], weight_ref, sems)
     total = by_z(total + early_ref[...])
     for tile in range(4):
-        target = (own_out_ref, other_out_ref)[tile // 2]
-        target[tile % 2] = total[:, tile * PATCH : (tile + 1) * PATCH].astype(jnp.bfloat16)
+        block = total[:, tile * PATCH : (tile + 1) * PATCH]
+        outs[tile // 2][tile % 2] = block.astype(jnp.bfloat16)
 
 
 def encode(body, groups, out_shape, where, arrays, pieces):
     in_vmem = pl.BlockSpec(memory_space=pltpu.VMEM)
-    taken = [pieces[group * PIECES + k] for group in groups for k in range(PIECES)]
+    keys = [group + k * GROUPS for group in groups for k in range(2)]
+    taken = [pieces[key] for key in keys if key != GROUPS]
+    if GROUPS in keys:
+        taken += [pieces[GROUPS, 0], pieces[GROUPS, 1]]
     if groups == EARLY:
         taken = [pltpu.with_memory_space_constraint(t, pltpu.HBM) for t in taken]
     flops = 2 * 4 * PATCH * D * 4 * WIDTH * len(groups)
@@ -224,7 +229,7 @@
         + [pl.BlockSpec(memory_space=pl.ANY)] * len(taken),
         out_specs=jax.tree.map(lambda _: in_vmem, out_shape),
         scratch_shapes=[
-            pltpu.VMEM((len(groups), 2, 2, D // 4, 4 * WIDTH), jnp.bfloat16),
+            pltpu.VMEM((len(groups), 2, D // 2, 4 * WIDTH), jnp.bfloat16),
             pltpu.SemaphoreType.DMA((len(groups), PIECES)),
         ],
         compiler_params=vmem_params(),
@@ -237,24 +242,25 @@
 
 def around_y(block):
     length = 2 * GROUPS
-    half = block.shape[0] // 2
-    up = [(i, (i + 1) % length) for i in range(length)]
-    down = [(i, (i - 1) % length) for i in range(length)]
-    halves = [block[:half], block[half:]]
-    rising, falling = list(halves), list(halves)
-    found = {(0, 0): halves[0], (0, 1): halves[1]}
+
+    def ways(chain):
+        pairs = []
+        for y in range(length):
+            for core in range(2):
+                to = (y + (1 if core == chain else -1)) % length
+                pairs.append(tuple(p // 4 * 8 + core * 4 + p % 4 for p in (y, to)))
+        return pairs
+
+    held = [block, block]
+    found = {0: block}
     for hop in range(1, length // 2 + 1):
-        last = 2 * hop == length
-        for k in range(2):
-            if not last or k == 0:
-                rising[k] = lax.ppermute(rising[k], ("y_hi", "tensor"), up)
-                found[length - hop, k] = rising[k]
-            if not last or k == 1:
-                falling[k] = lax.ppermute(falling[k], ("y_hi", "tensor"), down)
-                found[hop, k] = falling[k]
-    return [
-        found[group + k // 2 * GROUPS, k % 2] for group in range(GROUPS) for k in range(PIECES)
-    ]
+        for chain in range(2):
+            if 2 * hop == length:
+                half = block.shape[0] // 2
+                held[chain] = held[chain][chain * half : (chain + 1) * half]
+            held[chain] = lax.ppermute(held[chain], ("y_hi", "core", "tensor"), ways(chain))
+            found[(hop if chain else -hop) % length if 2 * hop < length else (hop, chain)] = held[chain]
+    return found
 
 
 def local(tiles, tile_counts, doc_order, qkv_weight, out_weight):
@@ -264,7 +270,8 @@
 
     place = bal_lo * 8 + bal_hi * 4 + tensor
     y = lax.axis_index("y_hi") * 4 + tensor
-    where = jnp.stack([bal_hi * 2 + bal_lo, place, y]).astype(jnp.int32)
+    along = 1 - 2 * lax.axis_index("core")
+    where = jnp.stack([bal_hi * 2 + bal_lo, place, y, along]).astype(jnp.int32)
     counts, order = tile_counts[0], doc_order[0]
 
     halves = cut(qkv_weight, out_weight)
@@ -285,13 +292,9 @@
         late_body, LATE, (part, part), where, (normed, other, total), pieces
     )
     back_part = lax.ppermute(other_part, "core", swap)
-    encoded = (
-        source.astype(jnp.float32) + own_part.astype(jnp.float32) + back_part.astype(jnp.float32)
-    ).astype(jnp.bfloat16)
-    returned = lax.all_to_all(
-        encoded.reshape(8, D // 4, PATCH), ("bal_hi", "tensor"), 0, 0, tiled=True
-    )
-    return returned[None]
+    encoded = sum(a.astype(jnp.float32) for a in (source, own_part, back_part))
+    encoded = encoded.astype(jnp.bfloat16).reshape(8, D // 4, PATCH)
+    return lax.all_to_all(encoded, ("bal_hi", "tensor"), 0, 0, tiled=True)[None]
 
 
 def solution(mesh):

time: 170 us -> 179 us (1.053)
  waiting for transfers between devices: 8.87 us -> 35.2 us
  starting transfers between devices: 81.6 us -> 66.2 us
    ppermute x14 -> x8, waiting for transfers between devices: 7.16 us -> 33.5 us  [around_y(): lax.ppermute(held[chain], ('y_hi', 'core', 'tensor'), ways(chain))]
    ppermute x14 -> x8, starting transfers between devices: 46 us -> 24.6 us  [around_y(): lax.ppermute(held[chain], ('y_hi', 'core', 'tensor'), ways(chain))]
    ppermute x1, starting transfers between devices: 3.02 us -> 8.84 us  [local(): back_part = lax.ppermute(other_part, 'core', swap)]
  transfers between devices with their start and end apart: 18 -> 12, of which waited for: 7 -> 7; matrix products, arithmetic and copies ran while one was open for 0% -> 1% of each run, Pallas kernels for 7% -> 7%
where the time goes in v6:
time: 179 us; the launch traced here: 178 us
  starting transfers between devices  66.2 us (37%)
  blocking collectives  56.5 us (32%)
  waiting for transfers between devices  35.2 us (20%)
  Pallas kernels  16.3 us (9%)
  local copies, waits for them, and re-layouts  3.26 us (2%)
    ppermute x8, waiting for transfers between devices, around_y(): lax.ppermute(held[chain], ('y_hi', 'core', 'tensor'), ways(chain))  33.5 us
    all_gather x1, blocking collectives, local(): block = lax.all_gather(both, 'z', axis=0, tiled=True)  32 us
    ppermute x8, starting transfers between devices, around_y(): lax.ppermute(held[chain], ('y_hi', 'core', 'tensor'), ways(chain))  24.6 us
    all_to_all x1, blocking collectives, local(): return lax.all_to_all(encoded, ('bal_hi', 'tensor'), 0, 0, tiled=True)[None]  24.5 us
    all_to_all x1, starting transfers between devices, local(): lax.all_to_all(halves, 'core', 0, 0, tiled=True).reshape(-1, 4 * WIDTH)  17.4 us
    ppermute x1, starting transfers between devices, local(): other = lax.ppermute(normed, 'core', swap)  11.6 us
    pallas_call x2, Pallas kernels, encode(): pl.pallas_call(body, out_shape=out_shape, in_specs=[pl.BlockSpec(memory_s...  9.82 us
    ppermute x1, starting transfers between devices, local(): back_part = lax.ppermute(other_part, 'core', swap)  8.84 us
  transfers between devices with their start and end apart: 12, of which 7 were waited for; matrix products, arithmetic and copies ran while one was open for 1% of the time, Pallas kernels for 7%

profile of v6, /device:TPU:1, one launch (start us, length us, event | category | flops | bytes accessed | tf_op | source)
XLA Modules:
  0.0 178.0 jit_solution(7240857929910792193)
XLA Ops:
  1.5 17.4 %all-to-all-start = ((bf16[2,20,640]{2,1,0:T(8,128)(2,1)}), bf16[2,20,640]{2,1,0:T(8,128)(2,1)S(1)}, u32[]{:S(2)}, u32[]{:S(2)}) async-start(bf16[2,20,640]{2,1,0:T(8,128)(2,1)} %cut.1), calls=%async_computation | async-start | bytes 122880 | tf_op jit(solution)/shard_map/all_to_all | solution.py:278
  20.4 3.1 %rotate.1 = bf16[16,320,128]{2,1,0:T(8,128)(2,1)} custom-call(s32[4]{0:T(128)S(1)} %pad_add_fusion.where_ref, s32[4]{0:T(128)S(1)} %bitcast.11, s32[4]{0:T(128)S(1)} %bitcast.13, bf16[16,320,128]{2,1,0:T(8,128)(2,1)} %bitcast.17), custom_call_target="tpu_custom_call" | custom-call | tf_op jit(solution)/shard_map/rotate/pallas_call | solution.py:71
  23.6 3.7 %all-to-all-start.1 = ((bf16[16,320,128]{2,1,0:T(8,128)(2,1)}), bf16[16,320,128]{2,1,0:T(8,128)(2,1)S(1)}, u32[]{:S(2)}, u32[]{:S(2)}) async-start(bf16[16,320,128]{2,1,0:T(8,128)(2,1)} %rotate.1), calls=%async_computation.1 | async-start | bytes 2621440 | tf_op jit(solution)/shard_map/all_to_all | solution.py:282
  27.3 32.0 %all_gather.3.refs_0_ = bf16[640,640]{1,0:T(8,128)(2,1)S(1)} all-gather(bf16[40,640]{1,0:T(8,128)(2,1)S(1)} %reshape.9), channel_id=1, replica_groups=mesh['z'=16,'y_hi'=2,'core'=2,'bal_hi'=2,'bal_lo'=2,'tensor'=4] {'z'}, dimensions={0}, use_global_device_ids=true | all-gather | bytes 870400 | tf_op jit(solution)/shard_map/all_gather | solution.py:283
  59.3 5.1 %collective-permute-start.3 = (bf16[640,640]{1,0:T(8,128)(2,1)S(1)}, bf16[640,640]{1,0:T(8,128)(2,1)S(1)}, u32[]{:S(2)}, u32[]{:S(2)}) collective-permute-start(bf16[640,640]{1,0:T(8,128)(2,1)S(1)} %all_gather.3.refs_0_), channel_id=1, source_target_pairs={{0,1},{16,51},{1,2},{17,16},{2,3},{18,17},{3,32},{19,18},{32,33},{... | collective-permute-start | bytes 2457608 | tf_op jit(solution)/shard_map/ppermute | solution.py:261
  64.4 1.9 %collective-permute-start.1 = (bf16[640,640]{1,0:T(8,128)(2,1)S(1)}, bf16[640,640]{1,0:T(8,128)(2,1)S(1)}, u32[]{:S(2)}, u32[]{:S(2)}) collective-permute-start(bf16[640,640]{1,0:T(8,128)(2,1)S(1)} %all_gather.3.refs_0_), channel_id=1, source_target_pairs={{0,35},{16,17},{1,0},{17,18},{2,1},{18,19},{3,2},{19,48},{32,3},{4... | collective-permute-start | bytes 2457608 | tf_op jit(solution)/shard_map/ppermute | solution.py:261
  66.3 7.6 %collective-permute-done.3.refs_5_ = bf16[640,640]{1,0:T(8,128)(2,1)S(1)} collective-permute-done((bf16[640,640]{1,0:T(8,128)(2,1)S(1)}, bf16[640,640]{1,0:T(8,128)(2,1)S(1)}, u32[]{:S(2)}, u32[]{:S(2)}) %collective-permute-start.3) | collective-permute-done | bytes 819232 | tf_op jit(solution)/shard_map/ppermute | solution.py:261
  73.9 5.3 %collective-permute-start.4 = (bf16[640,640]{1,0:T(8,128)(2,1)S(1)}, bf16[640,640]{1,0:T(8,128)(2,1)}, u32[]{:S(2)}, u32[]{:S(2)}) collective-permute-start(bf16[640,640]{1,0:T(8,128)(2,1)S(1)} %collective-permute-done.3.refs_5_), channel_id=1, source_target_pairs={{0,1},{16,51},{1,2},{17,16},{2,3},{18,17},{3,32},{19,18},{32,33},{... | collective-permute-start | bytes 2457608 | tf_op jit(solution)/shard_map/ppermute | solution.py:261
  79.2 6.8 %collective-permute-done.1.refs_2_ = bf16[640,640]{1,0:T(8,128)(2,1)S(1)} collective-permute-done((bf16[640,640]{1,0:T(8,128)(2,1)S(1)}, bf16[640,640]{1,0:T(8,128)(2,1)S(1)}, u32[]{:S(2)}, u32[]{:S(2)}) %collective-permute-start.1) | collective-permute-done | bytes 819232 | tf_op jit(solution)/shard_map/ppermute | solution.py:261
  86.0 1.9 %collective-permute-start.2 = (bf16[640,640]{1,0:T(8,128)(2,1)S(1)}, bf16[640,640]{1,0:T(8,128)(2,1)}, u32[]{:S(2)}, u32[]{:S(2)}) collective-permute-start(bf16[640,640]{1,0:T(8,128)(2,1)S(1)} %collective-permute-done.1.refs_2_), channel_id=1, source_target_pairs={{0,35},{16,17},{1,0},{17,18},{2,1},{18,19},{3,2},{19,48},{32,3},{4... | collective-permute-start | bytes 2457608 | tf_op jit(solution)/shard_map/ppermute | solution.py:261
  87.9 3.7 %collective-permute-done.4.refs_1_ = bf16[640,640]{1,0:T(8,128)(2,1)} collective-permute-done((bf16[640,640]{1,0:T(8,128)(2,1)S(1)}, bf16[640,640]{1,0:T(8,128)(2,1)}, u32[]{:S(2)}, u32[]{:S(2)}) %collective-permute-start.4) | collective-permute-done | bytes 819232 | tf_op jit(solution)/shard_map/ppermute | solution.py:261
  91.6 4.7 %collective-permute-start.5 = (bf16[640,640]{1,0:T(8,128)(2,1)}, bf16[640,640]{1,0:T(8,128)(2,1)S(1)}, u32[]{:S(2)}, u32[]{:S(2)}) collective-permute-start(bf16[640,640]{1,0:T(8,128)(2,1)} %collective-permute-done.4.refs_1_), channel_id=1, source_target_pairs={{0,1},{16,51},{1,2},{17,16},{2,3},{18,17},{3,32},{19,18},{32,33},{... | collective-permute-start | bytes 2457608 | tf_op jit(solution)/shard_map/ppermute | solution.py:261
  96.3 10.5 %collective-permute-done.2.refs_0_ = bf16[640,640]{1,0:T(8,128)(2,1)} collective-permute-done((bf16[640,640]{1,0:T(8,128)(2,1)S(1)}, bf16[640,640]{1,0:T(8,128)(2,1)}, u32[]{:S(2)}, u32[]{:S(2)}) %collective-permute-start.2) | collective-permute-done | bytes 819232 | tf_op jit(solution)/shard_map/ppermute | solution.py:261
  106.8 1.9 %collective-permute-start.6 = (bf16[640,640]{1,0:T(8,128)(2,1)}, bf16[640,640]{1,0:T(8,128)(2,1)}, u32[]{:S(2)}, u32[]{:S(2)}) collective-permute-start(bf16[640,640]{1,0:T(8,128)(2,1)} %collective-permute-done.2.refs_0_), channel_id=1, source_target_pairs={{0,35},{16,17},{1,0},{17,18},{2,1},{18,19},{3,2},{19,48},{32,3},{4... | collective-permute-start | bytes 2457608 | tf_op jit(solution)/shard_map/ppermute | solution.py:261
  108.7 1.8 normalise.1
  110.5 11.6 %collective-permute-start = (bf16[2,128,1280]{2,1,0:T(8,128)(2,1)S(1)}, bf16[2,128,1280]{2,1,0:T(8,128)(2,1)S(1)}, u32[]{:S(2)}, u32[]{:S(2)}) collective-permute-start(bf16[2,128,1280]{2,1,0:T(8,128)(2,1)S(1)} %get-tuple-element.13.own_ref), channel_id=1, source_target_pairs={{0,16},{16,0},{1,17},{17,1},{2,18},{18,2},{3,19},{19,3},{4,20},{20... | collective-permute-start | bytes 1966088 | tf_op jit(solution)/shard_map/ppermute | solution.py:286
  122.2 1.9 %collective-permute-start.7 = (bf16[320,640]{1,0:T(8,128)(2,1)S(1)}, bf16[320,640]{1,0:T(8,128)(2,1)S(1)}, u32[]{:S(2)}, u32[]{:S(2)}) collective-permute-start(bf16[320,640]{1,0:T(8,128)(2,1)S(1)} %slice.8), channel_id=1, source_target_pairs={{0,1},{16,51},{1,2},{17,16},{2,3},{18,17},{3,32},{19,18},{32,33},{... | collective-permute-start | bytes 1228808 | tf_op jit(solution)/shard_map/ppermute | solution.py:261
  124.1 2.7 %collective-permute-done.6.refs_4_ = bf16[640,640]{1,0:T(8,128)(2,1)} collective-permute-done((bf16[640,640]{1,0:T(8,128)(2,1)}, bf16[640,640]{1,0:T(8,128)(2,1)}, u32[]{:S(2)}, u32[]{:S(2)}) %collective-permute-start.6) | collective-permute-done | bytes 819232 | tf_op jit(solution)/shard_map/ppermute | solution.py:261
  127.8 1.9 %collective-permute-start.8 = (bf16[320,640]{1,0:T(8,128)(2,1)S(1)}, bf16[320,640]{1,0:T(8,128)(2,1)S(1)}, u32[]{:S(2)}, u32[]{:S(2)}) collective-permute-start(bf16[320,640]{1,0:T(8,128)(2,1)S(1)} %slice.9), channel_id=1, source_target_pairs={{0,35},{16,17},{1,0},{17,18},{2,1},{18,19},{3,2},{19,48},{32,3},{4... | collective-permute-start | bytes 1228808 | tf_op jit(solution)/shard_map/ppermute | solution.py:261
  129.7 6.8 %early_body.1.early_ref = f32[1280,512]{1,0:T(8,128)S(1)} custom-call(s32[4]{0:T(128)S(1)} %pad_add_fusion.where_ref, bf16[2,128,1280]{2,1,0:T(8,128)(2,1)S(1)} %get-tuple-element.13.own_ref, bf16[2,128,1280]{2,1,0:T(8,128)(2,1)S(1)} %collective-permute-done.other_ref, bf16[640,640]{1,0:T(8,128)(2,1)} %collective-permute-done.2.refs_0_, ...), custom_call_target="tpu_custom_call" | custom-call | flops 2516582400 | bytes 4915200 | tf_op jit(solution)/shard_map/early_body/pallas_call | solution.py:224
  136.6 2.3 %collective-permute-done.8.refs_2_ = bf16[320,640]{1,0:T(8,128)(2,1)S(1)} collective-permute-done((bf16[320,640]{1,0:T(8,128)(2,1)S(1)}, bf16[320,640]{1,0:T(8,128)(2,1)S(1)}, u32[]{:S(2)}, u32[]{:S(2)}) %collective-permute-start.8) | collective-permute-done | bytes 409632 | tf_op jit(solution)/shard_map/ppermute | solution.py:261
  138.9 3.0 %late_body.1 = (bf16[2,1280,128]{2,1,0:T(8,128)(2,1)S(1)}, bf16[2,1280,128]{2,1,0:T(8,128)(2,1)S(1)}) custom-call(s32[4]{0:T(128)S(1)} %pad_add_fusion.where_ref, bf16[2,128,1280]{2,1,0:T(8,128)(2,1)S(1)} %get-tuple-element.13.own_ref, bf16[2,128,1280]{2,1,0:T(8,128)(2,1)S(1)} %collective-permute-done.other_ref, f32[1280,512]{1,0:T(8,128)S(1)} %early_body.1.early_ref, ...), custom_call_target="tpu_custom_call" | custom-call | flops 838860800 | bytes 1638400 | tf_op jit(solution)/shard_map/late_body/pallas_call | solution.py:224
  141.9 8.8 %collective-permute-start.9 = (bf16[2,1280,128]{2,1,0:T(8,128)(2,1)S(1)}, bf16[2,1280,128]{2,1,0:T(8,128)(2,1)S(1)}, u32[]{:S(2)}, u32[]{:S(2)}) collective-permute-start(bf16[2,1280,128]{2,1,0:T(8,128)(2,1)S(1)} %get-tuple-element.16), channel_id=1, source_target_pairs={{0,16},{16,0},{1,17},{17,1},{2,18},{18,2},{3,19},{19,3},{4,20},{20... | collective-permute-start | bytes 1966088 | tf_op jit(solution)/shard_map/ppermute | solution.py:294
  152.7 24.5 %all_to_all.15 = bf16[8,320,128]{2,1,0:T(8,128)(2,1)S(1)} all-to-all(bf16[8,320,128]{2,1,0:T(8,128)(2,1)S(1)} %bitcast.15), channel_id=1, replica_groups=mesh['z'=16,'y_hi'=2,'core'=2,'bal_hi'=2,'bal_lo'=2,'tensor'=4] {'bal_hi..., dimensions={0} | all-to-all | bytes 1310720 | tf_op jit(solution)/shard_map/all_to_all | solution.py:297
  (27 shorter events, 6.8 us)
Async XLA Ops:
  1.5 22.0 %all-to-all-start = ((bf16[2,20,640]{2,1,0:T(8,128)(2,1)}), bf16[2,20,640]{2,1,0:T(8,128)(2,1)S(1)}, u32[]{:S(2)}, u32[]{:S(2)}) async-start(bf16[2,20,640]{2,1,0:T(8,128)(2,1)} %cut.1), calls=%async_computation | async-start | bytes 122880 | tf_op jit(solution)/shard_map/all_to_all | solution.py:278
  19.0 0.7 copy-start
  19.7 0.7 copy-start.2
  23.5 85.2 %copy-start.1 = (s32[1,4]{1,0:T(1,128)S(1)}, s32[1,4]{1,0:T(1,128)}, u32[]{:S(2)}) copy-start(s32[1,4]{1,0:T(1,128)} %param.6) | copy-start | bytes 52
  23.6 85.2 %copy-start.3 = (s32[1,4]{1,0:T(1,128)S(1)}, s32[1,4]{1,0:T(1,128)}, u32[]{:S(2)}) copy-start(s32[1,4]{1,0:T(1,128)} %param.7) | copy-start | bytes 52
  23.6 85.1 %all-to-all-start.1 = ((bf16[16,320,128]{2,1,0:T(8,128)(2,1)}), bf16[16,320,128]{2,1,0:T(8,128)(2,1)S(1)}, u32[]{:S(2)}, u32[]{:S(2)}) async-start(bf16[16,320,128]{2,1,0:T(8,128)(2,1)} %rotate.1), calls=%async_computation.1 | async-start | bytes 2621440 | tf_op jit(solution)/shard_map/all_to_all | solution.py:282
  59.3 14.6 %collective-permute-start.3 = (bf16[640,640]{1,0:T(8,128)(2,1)S(1)}, bf16[640,640]{1,0:T(8,128)(2,1)S(1)}, u32[]{:S(2)}, u32[]{:S(2)}) collective-permute-start(bf16[640,640]{1,0:T(8,128)(2,1)S(1)} %all_gather.3.refs_0_), channel_id=1, source_target_pairs={{0,1},{16,51},{1,2},{17,16},{2,3},{18,17},{3,32},{19,18},{32,33},{... | collective-permute-start | bytes 2457608 | tf_op jit(solution)/shard_map/ppermute | solution.py:261
  64.4 21.6 %collective-permute-start.1 = (bf16[640,640]{1,0:T(8,128)(2,1)S(1)}, bf16[640,640]{1,0:T(8,128)(2,1)S(1)}, u32[]{:S(2)}, u32[]{:S(2)}) collective-permute-start(bf16[640,640]{1,0:T(8,128)(2,1)S(1)} %all_gather.3.refs_0_), channel_id=1, source_target_pairs={{0,35},{16,17},{1,0},{17,18},{2,1},{18,19},{3,2},{19,48},{32,3},{4... | collective-permute-start | bytes 2457608 | tf_op jit(solution)/shard_map/ppermute | solution.py:261
  73.9 32.9 %copy-start.5 = (bf16[640,640]{1,0:T(8,128)(2,1)}, bf16[640,640]{1,0:T(8,128)(2,1)S(1)}, u32[]{:S(2)}) copy-start(bf16[640,640]{1,0:T(8,128)(2,1)S(1)} %collective-permute-done.3.refs_5_) | copy-start | bytes 2457604
  73.9 17.8 %collective-permute-start.4 = (bf16[640,640]{1,0:T(8,128)(2,1)S(1)}, bf16[640,640]{1,0:T(8,128)(2,1)}, u32[]{:S(2)}, u32[]{:S(2)}) collective-permute-start(bf16[640,640]{1,0:T(8,128)(2,1)S(1)} %collective-permute-done.3.refs_5_), channel_id=1, source_target_pairs={{0,1},{16,51},{1,2},{17,16},{2,3},{18,17},{3,32},{19,18},{32,33},{... | collective-permute-start | bytes 2457608 | tf_op jit(solution)/shard_map/ppermute | solution.py:261
  86.0 20.8 %copy-start.6 = (bf16[640,640]{1,0:T(8,128)(2,1)}, bf16[640,640]{1,0:T(8,128)(2,1)S(1)}, u32[]{:S(2)}) copy-start(bf16[640,640]{1,0:T(8,128)(2,1)S(1)} %collective-permute-done.1.refs_2_) | copy-start | bytes 2457604
  86.0 20.8 %collective-permute-start.2 = (bf16[640,640]{1,0:T(8,128)(2,1)S(1)}, bf16[640,640]{1,0:T(8,128)(2,1)}, u32[]{:S(2)}, u32[]{:S(2)}) collective-permute-start(bf16[640,640]{1,0:T(8,128)(2,1)S(1)} %collective-permute-done.1.refs_2_), channel_id=1, source_target_pairs={{0,35},{16,17},{1,0},{17,18},{2,1},{18,19},{3,2},{19,48},{32,3},{4... | collective-permute-start | bytes 2457608 | tf_op jit(solution)/shard_map/ppermute | solution.py:261
  91.6 30.5 %collective-permute-start.5 = (bf16[640,640]{1,0:T(8,128)(2,1)}, bf16[640,640]{1,0:T(8,128)(2,1)S(1)}, u32[]{:S(2)}, u32[]{:S(2)}) collective-permute-start(bf16[640,640]{1,0:T(8,128)(2,1)} %collective-permute-done.4.refs_1_), channel_id=1, source_target_pairs={{0,1},{16,51},{1,2},{17,16},{2,3},{18,17},{3,32},{19,18},{32,33},{... | collective-permute-start | bytes 2457608 | tf_op jit(solution)/shard_map/ppermute | solution.py:261
  106.8 20.0 %collective-permute-start.6 = (bf16[640,640]{1,0:T(8,128)(2,1)}, bf16[640,640]{1,0:T(8,128)(2,1)}, u32[]{:S(2)}, u32[]{:S(2)}) collective-permute-start(bf16[640,640]{1,0:T(8,128)(2,1)} %collective-permute-done.2.refs_0_), channel_id=1, source_target_pairs={{0,35},{16,17},{1,0},{17,18},{2,1},{18,19},{3,2},{19,48},{32,3},{4... | collective-permute-start | bytes 2457608 | tf_op jit(solution)/shard_map/ppermute | solution.py:261
  110.5 19.2 %collective-permute-start = (bf16[2,128,1280]{2,1,0:T(8,128)(2,1)S(1)}, bf16[2,128,1280]{2,1,0:T(8,128)(2,1)S(1)}, u32[]{:S(2)}, u32[]{:S(2)}) collective-permute-start(bf16[2,128,1280]{2,1,0:T(8,128)(2,1)S(1)} %get-tuple-element.13.own_ref), channel_id=1, source_target_pairs={{0,16},{16,0},{1,17},{17,1},{2,18},{18,2},{3,19},{19,3},{4,20},{20... | collective-permute-start | bytes 1966088 | tf_op jit(solution)/shard_map/ppermute | solution.py:286
  122.1 7.6 %copy-start.4 = (bf16[640,640]{1,0:T(8,128)(2,1)}, bf16[640,640]{1,0:T(8,128)(2,1)S(1)}, u32[]{:S(2)}) copy-start(bf16[640,640]{1,0:T(8,128)(2,1)S(1)} %collective-permute-done.5.refs_3_) | copy-start | bytes 2457604
  122.2 14.4 %collective-permute-start.7 = (bf16[320,640]{1,0:T(8,128)(2,1)S(1)}, bf16[320,640]{1,0:T(8,128)(2,1)S(1)}, u32[]{:S(2)}, u32[]{:S(2)}) collective-permute-start(bf16[320,640]{1,0:T(8,128)(2,1)S(1)} %slice.8), channel_id=1, source_target_pairs={{0,1},{16,51},{1,2},{17,16},{2,3},{18,17},{3,32},{19,18},{32,33},{... | collective-permute-start | bytes 1228808 | tf_op jit(solution)/shard_map/ppermute | solution.py:261
  127.8 11.1 %collective-permute-start.8 = (bf16[320,640]{1,0:T(8,128)(2,1)S(1)}, bf16[320,640]{1,0:T(8,128)(2,1)S(1)}, u32[]{:S(2)}, u32[]{:S(2)}) collective-permute-start(bf16[320,640]{1,0:T(8,128)(2,1)S(1)} %slice.9), channel_id=1, source_target_pairs={{0,35},{16,17},{1,0},{17,18},{2,1},{18,19},{3,2},{19,48},{32,3},{4... | collective-permute-start | bytes 1228808 | tf_op jit(solution)/shard_map/ppermute | solution.py:261
  141.9 10.5 %collective-permute-start.9 = (bf16[2,1280,128]{2,1,0:T(8,128)(2,1)S(1)}, bf16[2,1280,128]{2,1,0:T(8,128)(2,1)S(1)}, u32[]{:S(2)}, u32[]{:S(2)}) collective-permute-start(bf16[2,1280,128]{2,1,0:T(8,128)(2,1)S(1)} %get-tuple-element.16), channel_id=1, source_target_pairs={{0,16},{16,0},{1,17},{17,1},{2,18},{18,2},{3,19},{19,3},{4,20},{20... | collective-permute-start | bytes 1966088 | tf_op jit(solution)/shard_map/ppermute | solution.py:294

commit v7 on v4

--- a/solution.py
+++ b/solution.py
@@ -10,6 +10,7 @@
 PATCH = 128
 SLOTS = 16
 DOCS = 4
+BAL, PLACE, RING, CORE, COUNTS, ORDER = 0, 1, 2, 3, 4, 4 + DOCS
 ZS = 16
 GROUPS = 4
 PIECES = 4
@@ -25,58 +26,81 @@
     return pltpu.CompilerParams(vmem_limit_bytes=VMEM)
 
 
-def cut_body(qkv_ref, out_ref, halves_ref):
+def cut_body(facts_ref, qkv_ref, out_ref, keep_ref, send_ref):
+    halves = []
     for core in range(2):
         low = core * WIDTH
         kinds = [qkv_ref[k, :, low : low + WIDTH] for k in range(3)] + [out_ref[:, low : low + WIDTH]]
-        halves_ref[core] = jnp.concatenate(kinds, axis=1)
-
-
-def cut(qkv_weight, out_weight):
+        halves.append(jnp.concatenate(kinds, axis=1))
+
+    def put(keep, send):
+        keep_ref[...] = halves[keep]
+        send_ref[...] = halves[send]
+
+    pl.when(facts_ref[CORE] == 0)(lambda: put(0, 1))
+    pl.when(facts_ref[CORE] != 0)(lambda: put(1, 0))
+
+
+def cut(facts, qkv_weight, out_weight):
+    in_vmem = pl.BlockSpec(memory_space=pltpu.VMEM)
+    half = jax.ShapeDtypeStruct((out_weight.shape[0], 4 * WIDTH), jnp.bfloat16)
     return pl.pallas_call(
         cut_body,
-        out_shape=jax.ShapeDtypeStruct((2, out_weight.shape[0], 4 * WIDTH), jnp.bfloat16),
+        out_shape=(half, half),
+        in_specs=[pl.BlockSpec(memory_space=pltpu.SMEM), in_vmem, in_vmem],
+        out_specs=(in_vmem, in_vmem),
         compiler_params=vmem_params(),
         name="cut",
-    )(qkv_weight, out_weight)
-
-
-def in_turn(counts_ref, order_ref):
+    )(facts, *[pltpu.with_memory_space_constraint(w, pltpu.HBM) for w in (qkv_weight, out_weight)])
+
+
+def in_turn(facts_ref):
     first, turns = 0, []
     for turn in range(DOCS):
-        doc = order_ref[turn]
-        turns.append((doc, first, counts_ref[doc]))
-        first = first + counts_ref[doc]
+        doc = facts_ref[ORDER + turn]
+        count = facts_ref[COUNTS + doc]
+        turns.append((doc, first, count))
+        first = first + count
     return turns
 
 
-def rotate_body(where_ref, counts_ref, order_ref, tiles_ref, out_ref, sems):
+def rotate_body(facts_ref, tiles_ref, out_ref, held_ref, in_sems, out_sems):
     start = 0
-    for doc, first, _ in in_turn(counts_ref, order_ref):
-        start = jnp.where(doc == where_ref[0], first, start)
-    copies = [
+    for doc, first, _ in in_turn(facts_ref):
+        start = jnp.where(doc == facts_ref[BAL], first, start)
+    arriving = [
+        pltpu.make_async_copy(tiles_ref.at[slot], held_ref.at[slot], in_sems.at[slot])
+        for slot in range(SLOTS)
+    ]
+    leaving = [
         pltpu.make_async_copy(
-            tiles_ref.at[slot], out_ref.at[(slot + start) & (SLOTS - 1)], sems.at[slot]
+            held_ref.at[slot], out_ref.at[(slot + start) & (SLOTS - 1)], out_sems.at[slot]
         )
         for slot in range(SLOTS)
     ]
-    for copy in copies:
+    for copy in arriving:
         copy.start()
-    for copy in copies:
+    for slot in range(SLOTS):
+        arriving[slot].wait()
+        leaving[slot].start()
+    for copy in leaving:
         copy.wait()
 
 
-def rotate(where, counts, order, tiles):
-    in_smem = pl.BlockSpec(memory_space=pltpu.SMEM)
+def rotate(facts, tiles):
     return pl.pallas_call(
         rotate_body,
         out_shape=jax.ShapeDtypeStruct(tiles.shape, tiles.dtype),
-        in_specs=[in_smem, in_smem, in_smem, pl.BlockSpec(memory_space=pl.ANY)],
+        in_specs=[pl.BlockSpec(memory_space=pltpu.SMEM), pl.BlockSpec(memory_space=pl.ANY)],
         out_specs=pl.BlockSpec(memory_space=pl.ANY),
-        scratch_shapes=[pltpu.SemaphoreType.DMA((SLOTS,))],
+        scratch_shapes=[
+            pltpu.VMEM(tiles.shape, tiles.dtype),
+            pltpu.SemaphoreType.DMA((SLOTS,)),
+            pltpu.SemaphoreType.DMA((SLOTS,)),
+        ],
         compiler_params=vmem_params(),
         name="rotate",
-    )(where, counts, order, pltpu.with_memory_space_constraint(tiles, pltpu.HBM))
+    )(facts, pltpu.with_memory_space_constraint(tiles, pltpu.HBM))
 
 
 def by_half(rows):
@@ -89,7 +113,7 @@
     return jnp.concatenate([parts[0], parts[1]], axis=1).reshape(D, rows.shape[-1])
 
 
-def normalise_body(where_ref, counts_ref, order_ref, tile_ref, source_ref, normed_ref):
+def normalise_body(facts_ref, tile_ref, source_ref, normed_ref):
     tile = tile_ref[0]
     source_ref[0] = tile
     values = tile.astype(jnp.float32)
@@ -99,11 +123,11 @@
     normed_ref[0] = normed.T.astype(jnp.bfloat16)
 
 
-def normalise(where, counts, order, arrived):
-    def pick(j, where_ref, counts_ref, order_ref):
-        packed = where_ref[1] + j * SLOTS
+def normalise(facts, arrived):
+    def pick(j, facts_ref):
+        packed = facts_ref[PLACE] + j * SLOTS
         owner = 0
-        for doc, first, count in in_turn(counts_ref, order_ref):
+        for doc, first, count in in_turn(facts_ref):
             owner = jnp.where((first <= packed) & (packed < first + count), doc, owner)
         return (owner & 1) * 2 + (owner >> 1), 0, 0
 
@@ -117,14 +141,14 @@
             jax.ShapeDtypeStruct((2, PATCH, D), jnp.bfloat16),
         ),
         grid_spec=pltpu.PrefetchScalarGridSpec(
-            num_scalar_prefetch=3,
+            num_scalar_prefetch=1,
             grid=(2,),
             in_specs=[pl.BlockSpec((1, D, PATCH), pick)],
             out_specs=(pl.BlockSpec((1, D, PATCH), same), pl.BlockSpec((1, PATCH, D), same)),
         ),
         compiler_params=vmem_params(),
         name="normalise",
-    )(where, counts, order, arrived)
+    )(facts, arrived)
 
 
 def attend(qkv):
@@ -159,11 +183,11 @@
     )
 
 
-def group_contexts(groups, where_ref, own_ref, other_ref, pieces, weight_ref, sems):
+def group_contexts(groups, facts_ref, own_ref, other_ref, pieces, weight_ref, sems):
     def copies(n, group):
         made = []
         for k in range(PIECES):
-            y_hi = ((where_ref[2] + group + k // 2 * GROUPS) >> 2) & 1
+            y_hi = ((facts_ref[RING] + group + k // 2 * GROUPS) >> 2) & 1
             made.append(
                 pltpu.make_async_copy(
                     pieces[n * PIECES + k], weight_ref.at[n, y_hi, k % 2], sems.at[n, k]
@@ -192,25 +216,25 @@
     )
 
 
-def early_body(where_ref, own_ref, other_ref, *refs):
+def early_body(facts_ref, own_ref, other_ref, *refs):
     count = len(EARLY) * PIECES
     total_ref, weight_ref, sems = refs[count:]
     total_ref[...] = group_contexts(
-        EARLY, where_ref, own_ref, other_ref, refs[:count], weight_ref, sems
-    )
-
-
-def late_body(where_ref, own_ref, other_ref, early_ref, *refs):
+        EARLY, facts_ref, own_ref, other_ref, refs[:count], weight_ref, sems
+    )
+
+
+def late_body(facts_ref, own_ref, other_ref, early_ref, *refs):
     count = len(LATE) * PIECES
     own_out_ref, other_out_ref, weight_ref, sems = refs[count:]
-    total = group_contexts(LATE, where_ref, own_ref, other_ref, refs[:count], weight_ref, sems)
+    total = group_contexts(LATE, facts_ref, own_ref, other_ref, refs[:count], weight_ref, sems)
     total = by_z(total + early_ref[...])
     for tile in range(4):
         target = (own_out_ref, other_out_ref)[tile // 2]
         target[tile % 2] = total[:, tile * PATCH : (tile + 1) * PATCH].astype(jnp.bfloat16)
 
 
-def encode(body, groups, out_shape, where, arrays, pieces):
+def encode(body, groups, out_shape, facts, arrays, pieces):
     in_vmem = pl.BlockSpec(memory_space=pltpu.VMEM)
     taken = [pieces[group * PIECES + k] for group in groups for k in range(PIECES)]
     if groups == EARLY:
@@ -232,7 +256,7 @@
             flops=flops, bytes_accessed=len(groups) * D * 8 * WIDTH, transcendentals=0
         ),
         name=body.__name__,
-    )(where, *arrays, *taken)
+    )(facts, *arrays, *taken)
 
 
 def around_y(block):
@@ -264,25 +288,28 @@
 
     place = bal_lo * 8 + bal_hi * 4 + tensor
     y = lax.axis_index("y_hi") * 4 + tensor
-    where = jnp.stack([bal_hi * 2 + bal_lo, place, y]).astype(jnp.int32)
-    counts, order = tile_counts[0], doc_order[0]
-
-    halves = cut(qkv_weight, out_weight)
-    both = lax.all_to_all(halves, "core", 0, 0, tiled=True).reshape(-1, 4 * WIDTH)
-
-    outbound = rotate(where, counts, order, tiles[0, 0])
-    outbound, both = lax.optimization_barrier((outbound, both))
+    core = lax.axis_index("core")
+    here = jnp.stack([bal_hi * 2 + bal_lo, place, y, core]).astype(jnp.int32)
+    facts = jnp.concatenate([here, tile_counts[0], doc_order[0]])
+
+    outbound = rotate(facts, tiles[0, 0])
+    outbound, qkv_weight, out_weight = lax.optimization_barrier((outbound, qkv_weight, out_weight))
     arrived = lax.all_to_all(outbound, ("bal_lo", "bal_hi", "tensor"), 0, 0, tiled=True)
+
+    keep, send = cut(facts, qkv_weight, out_weight)
+    got = lax.ppermute(send, "core", swap)
+    first, second = jnp.where(core == 0, keep, got), jnp.where(core == 0, got, keep)
+    both = jnp.concatenate([first, second])
     block = lax.all_gather(both, "z", axis=0, tiled=True)
     pieces = around_y(block)
-    source, normed = normalise(where, counts, order, arrived.reshape(4, D, PATCH))
+    source, normed = normalise(facts, arrived.reshape(4, D, PATCH))
     other = lax.ppermute(normed, "core", swap)
 
     early = jax.ShapeDtypeStruct((D, 4 * PATCH), jnp.float32)
     part = jax.ShapeDtypeStruct((2, D, PATCH), jnp.bfloat16)
-    total = encode(early_body, EARLY, early, where, (normed, other), pieces)
+    total = encode(early_body, EARLY, early, facts, (normed, other), pieces)
     own_part, other_part = encode(
-        late_body, LATE, (part, part), where, (normed, other, total), pieces
+        late_body, LATE, (part, part), facts, (normed, other, total), pieces
     )
     back_part = lax.ppermute(other_part, "core", swap)
     encoded = (

time: 209 us -> 168 us (0.80)
  Pallas kernels: 54.2 us -> 15.7 us
  local copies, waits for them, and re-layouts: 4.51 us -> 2.38 us
    pallas_call x1, Pallas kernels: 41.5 us -> 2.85 us  [rotate(): pl.pallas_call(rotate_body, out_shape=jax.ShapeDtypeStruct(tiles.shape, t...]
    all_to_all x1 -> x0, starting transfers between devices: 17.4 us -> none  [local(): lax.all_to_all(halves, 'core', 0, 0, tiled=True).reshape(-1, 4 * WIDTH)]
    ppermute x0 -> x1, starting transfers between devices: none -> 11.8 us  [local(): got = lax.ppermute(send, 'core', swap)]
    all_to_all x1, starting transfers between devices: 3.71 us -> 8.02 us  [local(): lax.all_to_all(outbound, ('bal_lo', 'bal_hi', 'tensor'), 0, 0, tiled=True)]
    unnamed x27 -> x15, local copies, waits for them, and re-layouts: 4.42 us -> 1.56 us
  transfers between devices with their start and end apart: 18 -> 18, of which waited for: 7 -> 8; matrix products, arithmetic and copies ran while one was open for 0% -> 0% of each run, Pallas kernels for 24% -> 6%
where the time goes in v7:
time: 168 us; the launch traced here: 167 us
  starting transfers between devices  81 us (48%)
  blocking collectives  58.1 us (35%)
  Pallas kernels  15.7 us (9%)
  waiting for transfers between devices  9.52 us (6%)
  local copies, waits for them, and re-layouts  2.38 us (1%)
    all_gather x1, blocking collectives, local(): block = lax.all_gather(both, 'z', axis=0, tiled=True)  31.8 us
    ppermute x7, starting transfers between devices, around_y(): falling[k] = lax.ppermute(falling[k], ('y_hi', 'tensor'), down)  31.5 us
    all_to_all x1, blocking collectives, local(): lax.all_to_all(encoded.reshape(8, D // 4, PATCH), ('bal_hi', 'tensor'), 0...  26.2 us
    ppermute x7, starting transfers between devices, around_y(): rising[k] = lax.ppermute(rising[k], ('y_hi', 'tensor'), up)  14.6 us
    ppermute x1, starting transfers between devices, local(): other = lax.ppermute(normed, 'core', swap)  12.1 us
    ppermute x1, starting transfers between devices, local(): got = lax.ppermute(send, 'core', swap)  11.8 us
    pallas_call x2, Pallas kernels, encode(): pl.pallas_call(body, out_shape=out_shape, in_specs=[pl.BlockSpec(memory_s...  10.2 us
    all_to_all x1, starting transfers between devices, local(): lax.all_to_all(outbound, ('bal_lo', 'bal_hi', 'tensor'), 0, 0, tiled=True)  8.02 us
  transfers between devices with their start and end apart: 18, of which 8 were waited for; matrix products, arithmetic and copies ran while one was open for 0% of the time, Pallas kernels for 6%

profile of v7, /device:TPU:1, one launch (start us, length us, event | category | flops | bytes accessed | tf_op | source)
XLA Modules:
  0.0 167.3 jit_solution(11923489679046832207)
XLA Ops:
  0.7 2.9 %rotate.1 = bf16[16,320,128]{2,1,0:T(8,128)(2,1)} custom-call(s32[12]{0:T(128)S(1)} %concatenate.6.facts_ref, bf16[16,320,128]{2,1,0:T(8,128)(2,1)} %bitcast.13), custom_call_target="tpu_custom_call" | custom-call | tf_op jit(solution)/shard_map/rotate/pallas_call | solution.py:91
  3.6 8.0 %all-to-all-start = ((bf16[16,320,128]{2,1,0:T(8,128)(2,1)}), bf16[16,320,128]{2,1,0:T(8,128)(2,1)S(1)}, u32[]{:S(2)}, u32[]{:S(2)}) async-start(bf16[16,320,128]{2,1,0:T(8,128)(2,1)} %rotate.1), calls=%async_computation | async-start | bytes 2621440 | tf_op jit(solution)/shard_map/all_to_all | solution.py:297
  12.6 11.8 %collective-permute-start.1 = (bf16[20,640]{1,0:T(8,128)(2,1)S(1)}, bf16[20,640]{1,0:T(8,128)(2,1)S(1)}, u32[]{:S(2)}, u32[]{:S(2)}) collective-permute-start(bf16[20,640]{1,0:T(8,128)(2,1)S(1)} %get-tuple-element.20), channel_id=1, source_target_pairs={{0,16},{16,0},{1,17},{17,1},{2,18},{18,2},{3,19},{19,3},{4,20},{20... | collective-permute-start | bytes 76808 | tf_op jit(solution)/shard_map/ppermute | solution.py:300
  25.2 31.8 %all_gather.3 = bf16[640,640]{1,0:T(8,128)(2,1)S(1)} all-gather(bf16[40,640]{1,0:T(8,128)(2,1)S(1)} %pad_maximum_fusion), channel_id=1, replica_groups=mesh['z'=16,'y_hi'=2,'core'=2,'bal_hi'=2,'bal_lo'=2,'tensor'=4] {'z'}, dimensions={0}, use_global_device_ids=true | all-gather | bytes 870400 | tf_op jit(solution)/shard_map/all_gather | solution.py:303
  57.1 3.1 %collective-permute-start.6 = (bf16[320,640]{1,0:T(8,128)(2,1)S(1)}, bf16[320,640]{1,0:T(8,128)(2,1)S(1)}, u32[]{:S(2)}, u32[]{:S(2)}) collective-permute-start(bf16[320,640]{1,0:T(8,128)(2,1)S(1)} %get-tuple-element.24.refs_0_), channel_id=1, source_target_pairs={{0,1},{1,2},{2,3},{3,32},{32,33},{33,34},{34,35},{35,0},{4,5},{5,6... | collective-permute-start | bytes 1228808 | tf_op jit(solution)/shard_map/ppermute | solution.py:274
  60.2 4.1 %collective-permute-start.4 = (bf16[320,640]{1,0:T(8,128)(2,1)S(1)}, bf16[320,640]{1,0:T(8,128)(2,1)S(1)}, u32[]{:S(2)}, u32[]{:S(2)}) collective-permute-start(bf16[320,640]{1,0:T(8,128)(2,1)S(1)} %get-tuple-element.23.refs_1_), channel_id=1, source_target_pairs={{0,35},{1,0},{2,1},{3,2},{32,3},{33,32},{34,33},{35,34},{4,39},{5,... | collective-permute-start | bytes 1228808 | tf_op jit(solution)/shard_map/ppermute | solution.py:277
  64.3 1.9 %collective-permute-start.8 = (bf16[320,640]{1,0:T(8,128)(2,1)S(1)}, bf16[320,640]{1,0:T(8,128)(2,1)S(1)}, u32[]{:S(2)}, u32[]{:S(2)}) collective-permute-start(bf16[320,640]{1,0:T(8,128)(2,1)S(1)} %get-tuple-element.23.refs_1_), channel_id=1, source_target_pairs={{0,1},{1,2},{2,3},{3,32},{32,33},{33,34},{34,35},{35,0},{4,5},{5,6... | collective-permute-start | bytes 1228808 | tf_op jit(solution)/shard_map/ppermute | solution.py:274
  66.2 4.6 %collective-permute-start.2 = (bf16[320,640]{1,0:T(8,128)(2,1)S(1)}, bf16[320,640]{1,0:T(8,128)(2,1)}, u32[]{:S(2)}, u32[]{:S(2)}) collective-permute-start(bf16[320,640]{1,0:T(8,128)(2,1)S(1)} %get-tuple-element.24.refs_0_), channel_id=1, source_target_pairs={{0,35},{1,0},{2,1},{3,2},{32,3},{33,32},{34,33},{35,34},{4,39},{5,... | collective-permute-start | bytes 1228808 | tf_op jit(solution)/shard_map/ppermute | solution.py:277
  70.8 1.9 %collective-permute-start.7 = (bf16[320,640]{1,0:T(8,128)(2,1)S(1)}, bf16[320,640]{1,0:T(8,128)(2,1)}, u32[]{:S(2)}, u32[]{:S(2)}) collective-permute-start(bf16[320,640]{1,0:T(8,128)(2,1)S(1)} %collective-permute-done.6.refs_10_), channel_id=1, source_target_pairs={{0,1},{1,2},{2,3},{3,32},{32,33},{33,34},{34,35},{35,0},{4,5},{5,6... | collective-permute-start | bytes 1228808 | tf_op jit(solution)/shard_map/ppermute | solution.py:274
  72.8 4.6 %collective-permute-start.5 = (bf16[320,640]{1,0:T(8,128)(2,1)S(1)}, bf16[320,640]{1,0:T(8,128)(2,1)}, u32[]{:S(2)}, u32[]{:S(2)}) collective-permute-start(bf16[320,640]{1,0:T(8,128)(2,1)S(1)} %collective-permute-done.4.refs_5_), channel_id=1, source_target_pairs={{0,35},{1,0},{2,1},{3,2},{32,3},{33,32},{34,33},{35,34},{4,39},{5,... | collective-permute-start | bytes 1228808 | tf_op jit(solution)/shard_map/ppermute | solution.py:277
  78.7 1.9 %collective-permute-start.9 = (bf16[320,640]{1,0:T(8,128)(2,1)S(1)}, bf16[320,640]{1,0:T(8,128)(2,1)}, u32[]{:S(2)}, u32[]{:S(2)}) collective-permute-start(bf16[320,640]{1,0:T(8,128)(2,1)S(1)} %collective-permute-done.8.refs_11_), channel_id=1, source_target_pairs={{0,1},{1,2},{2,3},{3,32},{32,33},{33,34},{34,35},{35,0},{4,5},{5,6... | collective-permute-start | bytes 1228808 | tf_op jit(solution)/shard_map/ppermute | solution.py:274
  80.6 4.6 %collective-permute-start.3 = (bf16[320,640]{1,0:T(8,128)(2,1)}, bf16[320,640]{1,0:T(8,128)(2,1)}, u32[]{:S(2)}, u32[]{:S(2)}) collective-permute-start(bf16[320,640]{1,0:T(8,128)(2,1)} %collective-permute-done.2.refs_4_), channel_id=1, source_target_pairs={{0,35},{1,0},{2,1},{3,2},{32,3},{33,32},{34,33},{35,34},{4,39},{5,... | collective-permute-start | bytes 1228808 | tf_op jit(solution)/shard_map/ppermute | solution.py:277
  87.0 12.1 %collective-permute-start = (bf16[2,128,1280]{2,1,0:T(8,128)(2,1)S(1)}, bf16[2,128,1280]{2,1,0:T(8,128)(2,1)S(1)}, u32[]{:S(2)}, u32[]{:S(2)}) collective-permute-start(bf16[2,128,1280]{2,1,0:T(8,128)(2,1)S(1)} %get-tuple-element.16.own_ref), channel_id=1, source_target_pairs={{0,16},{16,0},{1,17},{17,1},{2,18},{18,2},{3,19},{19,3},{4,20},{20... | collective-permute-start | bytes 1966088 | tf_op jit(solution)/shard_map/ppermute | solution.py:306
  99.1 1.9 %collective-permute-start.10 = (bf16[320,640]{1,0:T(8,128)(2,1)}, bf16[320,640]{1,0:T(8,128)(2,1)S(1)}, u32[]{:S(2)}, u32[]{:S(2)}) collective-permute-start(bf16[320,640]{1,0:T(8,128)(2,1)} %collective-permute-done.7.refs_2_), channel_id=1, source_target_pairs={{0,1},{1,2},{2,3},{3,32},{32,33},{33,34},{34,35},{35,0},{4,5},{5,6... | collective-permute-start | bytes 1228808 | tf_op jit(solution)/shard_map/ppermute | solution.py:274
  101.0 4.6 %collective-permute-start.13 = (bf16[320,640]{1,0:T(8,128)(2,1)}, bf16[320,640]{1,0:T(8,128)(2,1)S(1)}, u32[]{:S(2)}, u32[]{:S(2)}) collective-permute-start(bf16[320,640]{1,0:T(8,128)(2,1)} %collective-permute-done.5.refs_1_), channel_id=1, source_target_pairs={{0,35},{1,0},{2,1},{3,2},{32,3},{33,32},{34,33},{35,34},{4,39},{5,... | collective-permute-start | bytes 1228808 | tf_op jit(solution)/shard_map/ppermute | solution.py:277
  105.6 1.9 %collective-permute-start.11 = (bf16[320,640]{1,0:T(8,128)(2,1)}, bf16[320,640]{1,0:T(8,128)(2,1)S(1)}, u32[]{:S(2)}, u32[]{:S(2)}) collective-permute-start(bf16[320,640]{1,0:T(8,128)(2,1)} %collective-permute-done.9.refs_3_), channel_id=1, source_target_pairs={{0,1},{1,2},{2,3},{3,32},{32,33},{33,34},{34,35},{35,0},{4,5},{5,6... | collective-permute-start | bytes 1228808 | tf_op jit(solution)/shard_map/ppermute | solution.py:274
  107.5 4.6 %collective-permute-start.12 = (bf16[320,640]{1,0:T(8,128)(2,1)}, bf16[320,640]{1,0:T(8,128)(2,1)S(1)}, u32[]{:S(2)}, u32[]{:S(2)}) collective-permute-start(bf16[320,640]{1,0:T(8,128)(2,1)} %collective-permute-done.3.refs_0_), channel_id=1, source_target_pairs={{0,35},{1,0},{2,1},{3,2},{32,3},{33,32},{34,33},{35,34},{4,39},{5,... | collective-permute-start | bytes 1228808 | tf_op jit(solution)/shard_map/ppermute | solution.py:277
  113.5 1.9 %collective-permute-start.14 = (bf16[320,640]{1,0:T(8,128)(2,1)S(1)}, bf16[320,640]{1,0:T(8,128)(2,1)S(1)}, u32[]{:S(2)}, u32[]{:S(2)}) collective-permute-start(bf16[320,640]{1,0:T(8,128)(2,1)S(1)} %collective-permute-done.10.refs_6_), channel_id=1, source_target_pairs={{0,1},{1,2},{2,3},{3,32},{32,33},{33,34},{34,35},{35,0},{4,5},{5,6... | collective-permute-start | bytes 1228808 | tf_op jit(solution)/shard_map/ppermute | solution.py:274
  115.4 4.6 %collective-permute-start.15 = (bf16[320,640]{1,0:T(8,128)(2,1)S(1)}, bf16[320,640]{1,0:T(8,128)(2,1)S(1)}, u32[]{:S(2)}, u32[]{:S(2)}) collective-permute-start(bf16[320,640]{1,0:T(8,128)(2,1)S(1)} %collective-permute-done.13.refs_9_), channel_id=1, source_target_pairs={{0,35},{1,0},{2,1},{3,2},{32,3},{33,32},{34,33},{35,34},{4,39},{5,... | collective-permute-start | bytes 1228808 | tf_op jit(solution)/shard_map/ppermute | solution.py:277
  120.0 2.3 %collective-permute-done.11.refs_7_ = bf16[320,640]{1,0:T(8,128)(2,1)S(1)} collective-permute-done((bf16[320,640]{1,0:T(8,128)(2,1)}, bf16[320,640]{1,0:T(8,128)(2,1)S(1)}, u32[]{:S(2)}, u32[]{:S(2)}) %collective-permute-start.11) | collective-permute-done | bytes 409632 | tf_op jit(solution)/shard_map/ppermute | solution.py:274
  124.0 6.9 %early_body.1.early_ref = f32[1280,512]{1,0:T(8,128)S(1)} custom-call(s32[12]{0:T(128)S(1)} %concatenate.6.facts_ref, bf16[2,128,1280]{2,1,0:T(8,128)(2,1)S(1)} %get-tuple-element.16.own_ref, bf16[2,128,1280]{2,1,0:T(8,128)(2,1)S(1)} %collective-permute-done.other_ref, bf16[320,640]{1,0:T(8,128)(2,1)} %collective-permute-done.3.refs_0_, ...), custom_call_target="tpu_custom_call" | custom-call | flops 2516582400 | bytes 4915200 | tf_op jit(solution)/shard_map/early_body/pallas_call | solution.py:243
  131.9 3.3 %late_body.1 = (bf16[2,1280,128]{2,1,0:T(8,128)(2,1)S(1)}, bf16[2,1280,128]{2,1,0:T(8,128)(2,1)S(1)}) custom-call(s32[12]{0:T(128)S(1)} %concatenate.6.facts_ref, bf16[2,128,1280]{2,1,0:T(8,128)(2,1)S(1)} %get-tuple-element.16.own_ref, bf16[2,128,1280]{2,1,0:T(8,128)(2,1)S(1)} %collective-permute-done.other_ref, f32[1280,512]{1,0:T(8,128)S(1)} %early_body.1.early_ref, ...), custom_call_target="tpu_custom_call" | custom-call | flops 838860800 | bytes 1638400 | tf_op jit(solution)/shard_map/late_body/pallas_call | solution.py:243
  135.2 3.0 %collective-permute-start.16 = (bf16[2,1280,128]{2,1,0:T(8,128)(2,1)S(1)}, bf16[2,1280,128]{2,1,0:T(8,128)(2,1)S(1)}, u32[]{:S(2)}, u32[]{:S(2)}) collective-permute-start(bf16[2,1280,128]{2,1,0:T(8,128)(2,1)S(1)} %get-tuple-element.22), channel_id=1, source_target_pairs={{0,16},{16,0},{1,17},{17,1},{2,18},{18,2},{3,19},{19,3},{4,20},{20... | collective-permute-start | bytes 1966088 | tf_op jit(solution)/shard_map/ppermute | solution.py:314
  140.2 26.2 %all_to_all.10 = bf16[8,320,128]{2,1,0:T(8,128)(2,1)S(1)} all-to-all(bf16[8,320,128]{2,1,0:T(8,128)(2,1)S(1)} %bitcast.11), channel_id=1, replica_groups=mesh['z'=16,'y_hi'=2,'core'=2,'bal_hi'=2,'bal_lo'=2,'tensor'=4] {'bal_hi..., dimensions={0} | all-to-all | bytes 1310720 | tf_op jit(solution)/shard_map/all_to_all | solution.py:318
  (39 shorter events, 12.6 us)
Async XLA Ops:
  3.6 81.6 %all-to-all-start = ((bf16[16,320,128]{2,1,0:T(8,128)(2,1)}), bf16[16,320,128]{2,1,0:T(8,128)(2,1)S(1)}, u32[]{:S(2)}, u32[]{:S(2)}) async-start(bf16[16,320,128]{2,1,0:T(8,128)(2,1)} %rotate.1), calls=%async_computation | async-start | bytes 2621440 | tf_op jit(solution)/shard_map/all_to_all | solution.py:297
  12.6 12.6 %collective-permute-start.1 = (bf16[20,640]{1,0:T(8,128)(2,1)S(1)}, bf16[20,640]{1,0:T(8,128)(2,1)S(1)}, u32[]{:S(2)}, u32[]{:S(2)}) collective-permute-start(bf16[20,640]{1,0:T(8,128)(2,1)S(1)} %get-tuple-element.20), channel_id=1, source_target_pairs={{0,16},{16,0},{1,17},{17,1},{2,18},{18,2},{3,19},{19,3},{4,20},{20... | collective-permute-start | bytes 76808 | tf_op jit(solution)/shard_map/ppermute | solution.py:300
  57.1 13.7 %collective-permute-start.6 = (bf16[320,640]{1,0:T(8,128)(2,1)S(1)}, bf16[320,640]{1,0:T(8,128)(2,1)S(1)}, u32[]{:S(2)}, u32[]{:S(2)}) collective-permute-start(bf16[320,640]{1,0:T(8,128)(2,1)S(1)} %get-tuple-element.24.refs_0_), channel_id=1, source_target_pairs={{0,1},{1,2},{2,3},{3,32},{32,33},{33,34},{34,35},{35,0},{4,5},{5,6... | collective-permute-start | bytes 1228808 | tf_op jit(solution)/shard_map/ppermute | solution.py:274
  60.2 12.5 %collective-permute-start.4 = (bf16[320,640]{1,0:T(8,128)(2,1)S(1)}, bf16[320,640]{1,0:T(8,128)(2,1)S(1)}, u32[]{:S(2)}, u32[]{:S(2)}) collective-permute-start(bf16[320,640]{1,0:T(8,128)(2,1)S(1)} %get-tuple-element.23.refs_1_), channel_id=1, source_target_pairs={{0,35},{1,0},{2,1},{3,2},{32,3},{33,32},{34,33},{35,34},{4,39},{5,... | collective-permute-start | bytes 1228808 | tf_op jit(solution)/shard_map/ppermute | solution.py:277
  64.3 14.4 %collective-permute-start.8 = (bf16[320,640]{1,0:T(8,128)(2,1)S(1)}, bf16[320,640]{1,0:T(8,128)(2,1)S(1)}, u32[]{:S(2)}, u32[]{:S(2)}) collective-permute-start(bf16[320,640]{1,0:T(8,128)(2,1)S(1)} %get-tuple-element.23.refs_1_), channel_id=1, source_target_pairs={{0,1},{1,2},{2,3},{3,32},{32,33},{33,34},{34,35},{35,0},{4,5},{5,6... | collective-permute-start | bytes 1228808 | tf_op jit(solution)/shard_map/ppermute | solution.py:274
  66.2 14.4 %collective-permute-start.2 = (bf16[320,640]{1,0:T(8,128)(2,1)S(1)}, bf16[320,640]{1,0:T(8,128)(2,1)}, u32[]{:S(2)}, u32[]{:S(2)}) collective-permute-start(bf16[320,640]{1,0:T(8,128)(2,1)S(1)} %get-tuple-element.24.refs_0_), channel_id=1, source_target_pairs={{0,35},{1,0},{2,1},{3,2},{32,3},{33,32},{34,33},{35,34},{4,39},{5,... | collective-permute-start | bytes 1228808 | tf_op jit(solution)/shard_map/ppermute | solution.py:277
  70.8 52.4 %copy-start = (bf16[320,640]{1,0:T(8,128)(2,1)}, bf16[320,640]{1,0:T(8,128)(2,1)S(1)}, u32[]{:S(2)}) copy-start(bf16[320,640]{1,0:T(8,128)(2,1)S(1)} %collective-permute-done.6.refs_10_) | copy-start | bytes 1228804
  70.8 28.2 %collective-permute-start.7 = (bf16[320,640]{1,0:T(8,128)(2,1)S(1)}, bf16[320,640]{1,0:T(8,128)(2,1)}, u32[]{:S(2)}, u32[]{:S(2)}) collective-permute-start(bf16[320,640]{1,0:T(8,128)(2,1)S(1)} %collective-permute-done.6.refs_10_), channel_id=1, source_target_pairs={{0,1},{1,2},{2,3},{3,32},{32,33},{33,34},{34,35},{35,0},{4,5},{5,6... | collective-permute-start | bytes 1228808 | tf_op jit(solution)/shard_map/ppermute | solution.py:274
  72.8 50.5 %copy-start.1 = (bf16[320,640]{1,0:T(8,128)(2,1)}, bf16[320,640]{1,0:T(8,128)(2,1)S(1)}, u32[]{:S(2)}) copy-start(bf16[320,640]{1,0:T(8,128)(2,1)S(1)} %collective-permute-done.4.refs_5_) | copy-start | bytes 1228804
  72.8 28.2 %collective-permute-start.5 = (bf16[320,640]{1,0:T(8,128)(2,1)S(1)}, bf16[320,640]{1,0:T(8,128)(2,1)}, u32[]{:S(2)}, u32[]{:S(2)}) collective-permute-start(bf16[320,640]{1,0:T(8,128)(2,1)S(1)} %collective-permute-done.4.refs_5_), channel_id=1, source_target_pairs={{0,35},{1,0},{2,1},{3,2},{32,3},{33,32},{34,33},{35,34},{4,39},{5,... | collective-permute-start | bytes 1228808 | tf_op jit(solution)/shard_map/ppermute | solution.py:277
  78.7 44.5 %copy-start.2 = (bf16[320,640]{1,0:T(8,128)(2,1)}, bf16[320,640]{1,0:T(8,128)(2,1)S(1)}, u32[]{:S(2)}) copy-start(bf16[320,640]{1,0:T(8,128)(2,1)S(1)} %collective-permute-done.8.refs_11_) | copy-start | bytes 1228804
  78.7 26.9 %collective-permute-start.9 = (bf16[320,640]{1,0:T(8,128)(2,1)S(1)}, bf16[320,640]{1,0:T(8,128)(2,1)}, u32[]{:S(2)}, u32[]{:S(2)}) collective-permute-start(bf16[320,640]{1,0:T(8,128)(2,1)S(1)} %collective-permute-done.8.refs_11_), channel_id=1, source_target_pairs={{0,1},{1,2},{2,3},{3,32},{32,33},{33,34},{34,35},{35,0},{4,5},{5,6... | collective-permute-start | bytes 1228808 | tf_op jit(solution)/shard_map/ppermute | solution.py:274
  80.6 26.9 %collective-permute-start.3 = (bf16[320,640]{1,0:T(8,128)(2,1)}, bf16[320,640]{1,0:T(8,128)(2,1)}, u32[]{:S(2)}, u32[]{:S(2)}) collective-permute-start(bf16[320,640]{1,0:T(8,128)(2,1)} %collective-permute-done.2.refs_4_), channel_id=1, source_target_pairs={{0,35},{1,0},{2,1},{3,2},{32,3},{33,32},{34,33},{35,34},{4,39},{5,... | collective-permute-start | bytes 1228808 | tf_op jit(solution)/shard_map/ppermute | solution.py:277
  87.0 36.2 %collective-permute-start = (bf16[2,128,1280]{2,1,0:T(8,128)(2,1)S(1)}, bf16[2,128,1280]{2,1,0:T(8,128)(2,1)S(1)}, u32[]{:S(2)}, u32[]{:S(2)}) collective-permute-start(bf16[2,128,1280]{2,1,0:T(8,128)(2,1)S(1)} %get-tuple-element.16.own_ref), channel_id=1, source_target_pairs={{0,16},{16,0},{1,17},{17,1},{2,18},{18,2},{3,19},{19,3},{4,20},{20... | collective-permute-start | bytes 1966088 | tf_op jit(solution)/shard_map/ppermute | solution.py:306
  99.1 14.4 %collective-permute-start.10 = (bf16[320,640]{1,0:T(8,128)(2,1)}, bf16[320,640]{1,0:T(8,128)(2,1)S(1)}, u32[]{:S(2)}, u32[]{:S(2)}) collective-permute-start(bf16[320,640]{1,0:T(8,128)(2,1)} %collective-permute-done.7.refs_2_), channel_id=1, source_target_pairs={{0,1},{1,2},{2,3},{3,32},{32,33},{33,34},{34,35},{35,0},{4,5},{5,6... | collective-permute-start | bytes 1228808 | tf_op jit(solution)/shard_map/ppermute | solution.py:274
  101.0 14.4 %collective-permute-start.13 = (bf16[320,640]{1,0:T(8,128)(2,1)}, bf16[320,640]{1,0:T(8,128)(2,1)S(1)}, u32[]{:S(2)}, u32[]{:S(2)}) collective-permute-start(bf16[320,640]{1,0:T(8,128)(2,1)} %collective-permute-done.5.refs_1_), channel_id=1, source_target_pairs={{0,35},{1,0},{2,1},{3,2},{32,3},{33,32},{34,33},{35,34},{4,39},{5,... | collective-permute-start | bytes 1228808 | tf_op jit(solution)/shard_map/ppermute | solution.py:277
  105.6 16.6 %collective-permute-start.11 = (bf16[320,640]{1,0:T(8,128)(2,1)}, bf16[320,640]{1,0:T(8,128)(2,1)S(1)}, u32[]{:S(2)}, u32[]{:S(2)}) collective-permute-start(bf16[320,640]{1,0:T(8,128)(2,1)} %collective-permute-done.9.refs_3_), channel_id=1, source_target_pairs={{0,1},{1,2},{2,3},{3,32},{32,33},{33,34},{34,35},{35,0},{4,5},{5,6... | collective-permute-start | bytes 1228808 | tf_op jit(solution)/shard_map/ppermute | solution.py:274
  107.5 15.7 %collective-permute-start.12 = (bf16[320,640]{1,0:T(8,128)(2,1)}, bf16[320,640]{1,0:T(8,128)(2,1)S(1)}, u32[]{:S(2)}, u32[]{:S(2)}) collective-permute-start(bf16[320,640]{1,0:T(8,128)(2,1)} %collective-permute-done.3.refs_0_), channel_id=1, source_target_pairs={{0,35},{1,0},{2,1},{3,2},{32,3},{33,32},{34,33},{35,34},{4,39},{5,... | collective-permute-start | bytes 1228808 | tf_op jit(solution)/shard_map/ppermute | solution.py:277
  113.5 9.8 %copy-start.3 = (bf16[320,640]{1,0:T(8,128)(2,1)}, bf16[320,640]{1,0:T(8,128)(2,1)S(1)}, u32[]{:S(2)}) copy-start(bf16[320,640]{1,0:T(8,128)(2,1)S(1)} %collective-permute-done.10.refs_6_) | copy-start | bytes 1228804
  113.5 17.6 %collective-permute-start.14 = (bf16[320,640]{1,0:T(8,128)(2,1)S(1)}, bf16[320,640]{1,0:T(8,128)(2,1)S(1)}, u32[]{:S(2)}, u32[]{:S(2)}) collective-permute-start(bf16[320,640]{1,0:T(8,128)(2,1)S(1)} %collective-permute-done.10.refs_6_), channel_id=1, source_target_pairs={{0,1},{1,2},{2,3},{3,32},{32,33},{33,34},{34,35},{35,0},{4,5},{5,6... | collective-permute-start | bytes 1228808 | tf_op jit(solution)/shard_map/ppermute | solution.py:274
  115.4 7.9 %copy-start.4 = (bf16[320,640]{1,0:T(8,128)(2,1)}, bf16[320,640]{1,0:T(8,128)(2,1)S(1)}, u32[]{:S(2)}) copy-start(bf16[320,640]{1,0:T(8,128)(2,1)S(1)} %collective-permute-done.13.refs_9_) | copy-start | bytes 1228804
  115.4 16.5 %collective-permute-start.15 = (bf16[320,640]{1,0:T(8,128)(2,1)S(1)}, bf16[320,640]{1,0:T(8,128)(2,1)S(1)}, u32[]{:S(2)}, u32[]{:S(2)}) collective-permute-start(bf16[320,640]{1,0:T(8,128)(2,1)S(1)} %collective-permute-done.13.refs_9_), channel_id=1, source_target_pairs={{0,35},{1,0},{2,1},{3,2},{32,3},{33,32},{34,33},{35,34},{4,39},{5,... | collective-permute-start | bytes 1228808 | tf_op jit(solution)/shard_map/ppermute | solution.py:277
  122.2 1.0 copy-start.5
  135.2 4.7 %collective-permute-start.16 = (bf16[2,1280,128]{2,1,0:T(8,128)(2,1)S(1)}, bf16[2,1280,128]{2,1,0:T(8,128)(2,1)S(1)}, u32[]{:S(2)}, u32[]{:S(2)}) collective-permute-start(bf16[2,1280,128]{2,1,0:T(8,128)(2,1)S(1)} %get-tuple-element.22), channel_id=1, source_target_pairs={{0,16},{16,0},{1,17},{17,1},{2,18},{18,2},{3,19},{19,3},{4,20},{20... | collective-permute-start | bytes 1966088 | tf_op jit(solution)/shard_map/ppermute | solution.py:314
  (1 other events, 0.8 us)

commit v8 on v7

--- a/solution.py
+++ b/solution.py
@@ -187,7 +187,8 @@
     def copies(n, group):
         made = []
         for k in range(PIECES):
-            y_hi = ((facts_ref[RING] + group + k // 2 * GROUPS) >> 2) & 1
+            away = (1 - 2 * facts_ref[CORE]) * (group + k // 2 * GROUPS)
+            y_hi = ((facts_ref[RING] + away) >> 2) & 1
             made.append(
                 pltpu.make_async_copy(
                     pieces[n * PIECES + k], weight_ref.at[n, y_hi, k % 2], sems.at[n, k]
@@ -262,8 +263,15 @@
 def around_y(block):
     length = 2 * GROUPS
     half = block.shape[0] // 2
-    up = [(i, (i + 1) % length) for i in range(length)]
-    down = [(i, (i - 1) % length) for i in range(length)]
+
+    def ways(sign):
+        pairs = []
+        for y in range(length):
+            for core in range(2):
+                to = (y + (sign if core == 0 else -sign)) % length
+                pairs.append(tuple(p // 4 * 8 + core * 4 + p % 4 for p in (y, to)))
+        return pairs
+
     halves = [block[:half], block[half:]]
     rising, falling = list(halves), list(halves)
     found = {(0, 0): halves[0], (0, 1): halves[1]}
@@ -271,10 +279,10 @@
         last = 2 * hop == length
         for k in range(2):
             if not last or k == 0:
-                rising[k] = lax.ppermute(rising[k], ("y_hi", "tensor"), up)
+                rising[k] = lax.ppermute(rising[k], ("y_hi", "core", "tensor"), ways(1))
                 found[length - hop, k] = rising[k]
             if not last or k == 1:
-                falling[k] = lax.ppermute(falling[k], ("y_hi", "tensor"), down)
+                falling[k] = lax.ppermute(falling[k], ("y_hi", "core", "tensor"), ways(-1))
                 found[hop, k] = falling[k]
     return [
         found[group + k // 2 * GROUPS, k % 2] for group in range(GROUPS) for k in range(PIECES)

time: 168 us -> 166 us (0.988)
  starting transfers between devices: 81 us -> 76.6 us
  waiting for transfers between devices: 9.52 us -> 13.6 us
  blocking collectives: 58.1 us -> 55.8 us
    ppermute x14, waiting for transfers between devices: 6.98 us -> 10.7 us  [the longest x7 9.04 us: around_y(): falling[k] = lax.ppermute(falling[k], ('y_hi', 'core', 'tensor'), ways(-1))]
    ppermute x14, starting transfers between devices: 46.1 us -> 42.9 us  [the longest x7 27.8 us: around_y(): rising[k] = lax.ppermute(rising[k], ('y_hi', 'core', 'tensor'), ways(1))]
    all_to_all x1, blocking collectives: 26.2 us -> 23.9 us  [local(): lax.all_to_all(encoded.reshape(8, D // 4, PATCH), ('bal_hi', 'tensor'), 0...]
  transfers between devices with their start and end apart: 18 -> 18, of which waited for: 8 -> 7; matrix products, arithmetic and copies ran while one was open for 0% -> 0% of each run, Pallas kernels for 6% -> 6%
where the time goes in v8:
time: 166 us; the launch traced here: 165 us
  starting transfers between devices  76.6 us (46%)
  blocking collectives  55.8 us (34%)
  Pallas kernels  15.7 us (9%)
  waiting for transfers between devices  13.6 us (8%)
  local copies, waits for them, and re-layouts  2.38 us (1%)
    all_gather x1, blocking collectives, local(): block = lax.all_gather(both, 'z', axis=0, tiled=True)  31.9 us
    ppermute x7, starting transfers between devices, around_y(): rising[k] = lax.ppermute(rising[k], ('y_hi', 'core', 'tensor'), ways(1))  27.8 us
    all_to_all x1, blocking collectives, local(): lax.all_to_all(encoded.reshape(8, D // 4, PATCH), ('bal_hi', 'tensor'), 0...  23.9 us
    ppermute x7, starting transfers between devices, around_y(): falling[k] = lax.ppermute(falling[k], ('y_hi', 'core', 'tensor'), ways(-1))  15.1 us
    ppermute x1, starting transfers between devices, local(): other = lax.ppermute(normed, 'core', swap)  11.9 us
    ppermute x1, starting transfers between devices, local(): got = lax.ppermute(send, 'core', swap)  11.8 us
    pallas_call x2, Pallas kernels, encode(): pl.pallas_call(body, out_shape=out_shape, in_specs=[pl.BlockSpec(memory_s...  10.2 us
    ppermute x7, waiting for transfers between devices, around_y(): falling[k] = lax.ppermute(falling[k], ('y_hi', 'core', 'tensor'), ways(-1))  9.04 us
  transfers between devices with their start and end apart: 18, of which 7 were waited for; matrix products, arithmetic and copies ran while one was open for 0% of the time, Pallas kernels for 6%

profile of v8, /device:TPU:1, one launch (start us, length us, event | category | flops | bytes accessed | tf_op | source)
XLA Modules:
  0.0 164.7 jit_solution(4788080744905549964)
XLA Ops:
  0.7 2.9 %rotate.1 = bf16[16,320,128]{2,1,0:T(8,128)(2,1)} custom-call(s32[12]{0:T(128)S(1)} %concatenate.6.facts_ref, bf16[16,320,128]{2,1,0:T(8,128)(2,1)} %bitcast.13), custom_call_target="tpu_custom_call" | custom-call | tf_op jit(solution)/shard_map/rotate/pallas_call | solution.py:91
  3.6 8.0 %all-to-all-start = ((bf16[16,320,128]{2,1,0:T(8,128)(2,1)}), bf16[16,320,128]{2,1,0:T(8,128)(2,1)S(1)}, u32[]{:S(2)}, u32[]{:S(2)}) async-start(bf16[16,320,128]{2,1,0:T(8,128)(2,1)} %rotate.1), calls=%async_computation | async-start | bytes 2621440 | tf_op jit(solution)/shard_map/all_to_all | solution.py:305
  12.6 11.8 %collective-permute-start.1 = (bf16[20,640]{1,0:T(8,128)(2,1)S(1)}, bf16[20,640]{1,0:T(8,128)(2,1)S(1)}, u32[]{:S(2)}, u32[]{:S(2)}) collective-permute-start(bf16[20,640]{1,0:T(8,128)(2,1)S(1)} %get-tuple-element.20), channel_id=1, source_target_pairs={{0,16},{16,0},{1,17},{17,1},{2,18},{18,2},{3,19},{19,3},{4,20},{20... | collective-permute-start | bytes 76808 | tf_op jit(solution)/shard_map/ppermute | solution.py:308
  25.2 31.9 %all_gather.3 = bf16[640,640]{1,0:T(8,128)(2,1)S(1)} all-gather(bf16[40,640]{1,0:T(8,128)(2,1)S(1)} %pad_maximum_fusion), channel_id=1, replica_groups=mesh['z'=16,'y_hi'=2,'core'=2,'bal_hi'=2,'bal_lo'=2,'tensor'=4] {'z'}, dimensions={0}, use_global_device_ids=true | all-gather | bytes 870400 | tf_op jit(solution)/shard_map/all_gather | solution.py:311
  57.2 5.2 %collective-permute-start.6 = (bf16[320,640]{1,0:T(8,128)(2,1)S(1)}, bf16[320,640]{1,0:T(8,128)(2,1)S(1)}, u32[]{:S(2)}, u32[]{:S(2)}) collective-permute-start(bf16[320,640]{1,0:T(8,128)(2,1)S(1)} %get-tuple-element.24.refs_0_), channel_id=1, source_target_pairs={{0,1},{16,51},{1,2},{17,16},{2,3},{18,17},{3,32},{19,18},{32,33},{... | collective-permute-start | bytes 1228808 | tf_op jit(solution)/shard_map/ppermute | solution.py:282
  62.4 1.9 %collective-permute-start.4 = (bf16[320,640]{1,0:T(8,128)(2,1)S(1)}, bf16[320,640]{1,0:T(8,128)(2,1)S(1)}, u32[]{:S(2)}, u32[]{:S(2)}) collective-permute-start(bf16[320,640]{1,0:T(8,128)(2,1)S(1)} %get-tuple-element.23.refs_1_), channel_id=1, source_target_pairs={{0,35},{16,17},{1,0},{17,18},{2,1},{18,19},{3,2},{19,48},{32,3},{4... | collective-permute-start | bytes 1228808 | tf_op jit(solution)/shard_map/ppermute | solution.py:285
  64.3 4.6 %collective-permute-start.8 = (bf16[320,640]{1,0:T(8,128)(2,1)S(1)}, bf16[320,640]{1,0:T(8,128)(2,1)S(1)}, u32[]{:S(2)}, u32[]{:S(2)}) collective-permute-start(bf16[320,640]{1,0:T(8,128)(2,1)S(1)} %get-tuple-element.23.refs_1_), channel_id=1, source_target_pairs={{0,1},{16,51},{1,2},{17,16},{2,3},{18,17},{3,32},{19,18},{32,33},{... | collective-permute-start | bytes 1228808 | tf_op jit(solution)/shard_map/ppermute | solution.py:282
  68.9 1.9 %collective-permute-start.2 = (bf16[320,640]{1,0:T(8,128)(2,1)S(1)}, bf16[320,640]{1,0:T(8,128)(2,1)}, u32[]{:S(2)}, u32[]{:S(2)}) collective-permute-start(bf16[320,640]{1,0:T(8,128)(2,1)S(1)} %get-tuple-element.24.refs_0_), channel_id=1, source_target_pairs={{0,35},{16,17},{1,0},{17,18},{2,1},{18,19},{3,2},{19,48},{32,3},{4... | collective-permute-start | bytes 1228808 | tf_op jit(solution)/shard_map/ppermute | solution.py:285
  70.8 4.6 %collective-permute-start.7 = (bf16[320,640]{1,0:T(8,128)(2,1)S(1)}, bf16[320,640]{1,0:T(8,128)(2,1)}, u32[]{:S(2)}, u32[]{:S(2)}) collective-permute-start(bf16[320,640]{1,0:T(8,128)(2,1)S(1)} %collective-permute-done.6.refs_10_), channel_id=1, source_target_pairs={{0,1},{16,51},{1,2},{17,16},{2,3},{18,17},{3,32},{19,18},{32,33},{... | collective-permute-start | bytes 1228808 | tf_op jit(solution)/shard_map/ppermute | solution.py:282
  75.4 1.9 %collective-permute-start.5 = (bf16[320,640]{1,0:T(8,128)(2,1)S(1)}, bf16[320,640]{1,0:T(8,128)(2,1)}, u32[]{:S(2)}, u32[]{:S(2)}) collective-permute-start(bf16[320,640]{1,0:T(8,128)(2,1)S(1)} %collective-permute-done.4.refs_5_), channel_id=1, source_target_pairs={{0,35},{16,17},{1,0},{17,18},{2,1},{18,19},{3,2},{19,48},{32,3},{4... | collective-permute-start | bytes 1228808 | tf_op jit(solution)/shard_map/ppermute | solution.py:285
  77.4 4.6 %collective-permute-start.9 = (bf16[320,640]{1,0:T(8,128)(2,1)S(1)}, bf16[320,640]{1,0:T(8,128)(2,1)}, u32[]{:S(2)}, u32[]{:S(2)}) collective-permute-start(bf16[320,640]{1,0:T(8,128)(2,1)S(1)} %collective-permute-done.8.refs_11_), channel_id=1, source_target_pairs={{0,1},{16,51},{1,2},{17,16},{2,3},{18,17},{3,32},{19,18},{32,33},{... | collective-permute-start | bytes 1228808 | tf_op jit(solution)/shard_map/ppermute | solution.py:282
  83.5 1.9 %collective-permute-start.3 = (bf16[320,640]{1,0:T(8,128)(2,1)}, bf16[320,640]{1,0:T(8,128)(2,1)}, u32[]{:S(2)}, u32[]{:S(2)}) collective-permute-start(bf16[320,640]{1,0:T(8,128)(2,1)} %collective-permute-done.2.refs_4_), channel_id=1, source_target_pairs={{0,35},{16,17},{1,0},{17,18},{2,1},{18,19},{3,2},{19,48},{32,3},{4... | collective-permute-start | bytes 1228808 | tf_op jit(solution)/shard_map/ppermute | solution.py:285
  87.2 11.9 %collective-permute-start = (bf16[2,128,1280]{2,1,0:T(8,128)(2,1)S(1)}, bf16[2,128,1280]{2,1,0:T(8,128)(2,1)S(1)}, u32[]{:S(2)}, u32[]{:S(2)}) collective-permute-start(bf16[2,128,1280]{2,1,0:T(8,128)(2,1)S(1)} %get-tuple-element.16.own_ref), channel_id=1, source_target_pairs={{0,16},{16,0},{1,17},{17,1},{2,18},{18,2},{3,19},{19,3},{4,20},{20... | collective-permute-start | bytes 1966088 | tf_op jit(solution)/shard_map/ppermute | solution.py:314
  99.1 1.9 %collective-permute-start.10 = (bf16[320,640]{1,0:T(8,128)(2,1)}, bf16[320,640]{1,0:T(8,128)(2,1)S(1)}, u32[]{:S(2)}, u32[]{:S(2)}) collective-permute-start(bf16[320,640]{1,0:T(8,128)(2,1)} %collective-permute-done.7.refs_2_), channel_id=1, source_target_pairs={{0,1},{16,51},{1,2},{17,16},{2,3},{18,17},{3,32},{19,18},{32,33},{... | collective-permute-start | bytes 1228808 | tf_op jit(solution)/shard_map/ppermute | solution.py:282
  101.1 3.4 %collective-permute-start.13 = (bf16[320,640]{1,0:T(8,128)(2,1)}, bf16[320,640]{1,0:T(8,128)(2,1)S(1)}, u32[]{:S(2)}, u32[]{:S(2)}) collective-permute-start(bf16[320,640]{1,0:T(8,128)(2,1)} %collective-permute-done.5.refs_1_), channel_id=1, source_target_pairs={{0,35},{16,17},{1,0},{17,18},{2,1},{18,19},{3,2},{19,48},{32,3},{4... | collective-permute-start | bytes 1228808 | tf_op jit(solution)/shard_map/ppermute | solution.py:285
  104.5 3.1 %collective-permute-start.11 = (bf16[320,640]{1,0:T(8,128)(2,1)}, bf16[320,640]{1,0:T(8,128)(2,1)S(1)}, u32[]{:S(2)}, u32[]{:S(2)}) collective-permute-start(bf16[320,640]{1,0:T(8,128)(2,1)} %collective-permute-done.9.refs_3_), channel_id=1, source_target_pairs={{0,1},{16,51},{1,2},{17,16},{2,3},{18,17},{3,32},{19,18},{32,33},{... | collective-permute-start | bytes 1228808 | tf_op jit(solution)/shard_map/ppermute | solution.py:282
  107.6 2.2 %collective-permute-start.12 = (bf16[320,640]{1,0:T(8,128)(2,1)}, bf16[320,640]{1,0:T(8,128)(2,1)S(1)}, u32[]{:S(2)}, u32[]{:S(2)}) collective-permute-start(bf16[320,640]{1,0:T(8,128)(2,1)} %collective-permute-done.3.refs_0_), channel_id=1, source_target_pairs={{0,35},{16,17},{1,0},{17,18},{2,1},{18,19},{3,2},{19,48},{32,3},{4... | collective-permute-start | bytes 1228808 | tf_op jit(solution)/shard_map/ppermute | solution.py:285
  110.3 3.9 %collective-permute-start.14 = (bf16[320,640]{1,0:T(8,128)(2,1)S(1)}, bf16[320,640]{1,0:T(8,128)(2,1)S(1)}, u32[]{:S(2)}, u32[]{:S(2)}) collective-permute-start(bf16[320,640]{1,0:T(8,128)(2,1)S(1)} %collective-permute-done.10.refs_6_), channel_id=1, source_target_pairs={{0,1},{16,51},{1,2},{17,16},{2,3},{18,17},{3,32},{19,18},{32,33},{... | collective-permute-start | bytes 1228808 | tf_op jit(solution)/shard_map/ppermute | solution.py:282
  119.0 5.7 %collective-permute-done.12.refs_8_ = bf16[320,640]{1,0:T(8,128)(2,1)S(1)} collective-permute-done((bf16[320,640]{1,0:T(8,128)(2,1)}, bf16[320,640]{1,0:T(8,128)(2,1)S(1)}, u32[]{:S(2)}, u32[]{:S(2)}) %collective-permute-start.12) | collective-permute-done | bytes 409632 | tf_op jit(solution)/shard_map/ppermute | solution.py:285
  125.5 6.9 %early_body.1.early_ref = f32[1280,512]{1,0:T(8,128)S(1)} custom-call(s32[12]{0:T(128)S(1)} %concatenate.6.facts_ref, bf16[2,128,1280]{2,1,0:T(8,128)(2,1)S(1)} %get-tuple-element.16.own_ref, bf16[2,128,1280]{2,1,0:T(8,128)(2,1)S(1)} %collective-permute-done.other_ref, bf16[320,640]{1,0:T(8,128)(2,1)} %collective-permute-done.3.refs_0_, ...), custom_call_target="tpu_custom_call" | custom-call | flops 2516582400 | bytes 4915200 | tf_op jit(solution)/shard_map/early_body/pallas_call | solution.py:244
  132.4 3.3 %late_body.1 = (bf16[2,1280,128]{2,1,0:T(8,128)(2,1)S(1)}, bf16[2,1280,128]{2,1,0:T(8,128)(2,1)S(1)}) custom-call(s32[12]{0:T(128)S(1)} %concatenate.6.facts_ref, bf16[2,128,1280]{2,1,0:T(8,128)(2,1)S(1)} %get-tuple-element.16.own_ref, bf16[2,128,1280]{2,1,0:T(8,128)(2,1)S(1)} %collective-permute-done.other_ref, f32[1280,512]{1,0:T(8,128)S(1)} %early_body.1.early_ref, ...), custom_call_target="tpu_custom_call" | custom-call | flops 838860800 | bytes 1638400 | tf_op jit(solution)/shard_map/late_body/pallas_call | solution.py:244
  135.7 1.9 %collective-permute-start.16 = (bf16[2,1280,128]{2,1,0:T(8,128)(2,1)S(1)}, bf16[2,1280,128]{2,1,0:T(8,128)(2,1)S(1)}, u32[]{:S(2)}, u32[]{:S(2)}) collective-permute-start(bf16[2,1280,128]{2,1,0:T(8,128)(2,1)S(1)} %get-tuple-element.22), channel_id=1, source_target_pairs={{0,16},{16,0},{1,17},{17,1},{2,18},{18,2},{3,19},{19,3},{4,20},{20... | collective-permute-start | bytes 1966088 | tf_op jit(solution)/shard_map/ppermute | solution.py:322
  137.6 2.1 %collective-permute-done.16 = bf16[2,1280,128]{2,1,0:T(8,128)(2,1)S(1)} collective-permute-done((bf16[2,1280,128]{2,1,0:T(8,128)(2,1)S(1)}, bf16[2,1280,128]{2,1,0:T(8,128)(2,1)S(1)}, u32[]{:S(2)}, u32[]{:S(2)}) %collective-permute-start.16) | collective-permute-done | bytes 655392 | tf_op jit(solution)/shard_map/ppermute | solution.py:322
  139.9 23.9 %all_to_all.10 = bf16[8,320,128]{2,1,0:T(8,128)(2,1)S(1)} all-to-all(bf16[8,320,128]{2,1,0:T(8,128)(2,1)S(1)} %bitcast.11), channel_id=1, replica_groups=mesh['z'=16,'y_hi'=2,'core'=2,'bal_hi'=2,'bal_lo'=2,'tensor'=4] {'bal_hi..., dimensions={0} | all-to-all | bytes 1310720 | tf_op jit(solution)/shard_map/all_to_all | solution.py:326
  (39 shorter events, 13.1 us)
Async XLA Ops:
  3.6 81.8 %all-to-all-start = ((bf16[16,320,128]{2,1,0:T(8,128)(2,1)}), bf16[16,320,128]{2,1,0:T(8,128)(2,1)S(1)}, u32[]{:S(2)}, u32[]{:S(2)}) async-start(bf16[16,320,128]{2,1,0:T(8,128)(2,1)} %rotate.1), calls=%async_computation | async-start | bytes 2621440 | tf_op jit(solution)/shard_map/all_to_all | solution.py:305
  12.6 12.6 %collective-permute-start.1 = (bf16[20,640]{1,0:T(8,128)(2,1)S(1)}, bf16[20,640]{1,0:T(8,128)(2,1)S(1)}, u32[]{:S(2)}, u32[]{:S(2)}) collective-permute-start(bf16[20,640]{1,0:T(8,128)(2,1)S(1)} %get-tuple-element.20), channel_id=1, source_target_pairs={{0,16},{16,0},{1,17},{17,1},{2,18},{18,2},{3,19},{19,3},{4,20},{20... | collective-permute-start | bytes 76808 | tf_op jit(solution)/shard_map/ppermute | solution.py:308
  57.2 13.7 %collective-permute-start.6 = (bf16[320,640]{1,0:T(8,128)(2,1)S(1)}, bf16[320,640]{1,0:T(8,128)(2,1)S(1)}, u32[]{:S(2)}, u32[]{:S(2)}) collective-permute-start(bf16[320,640]{1,0:T(8,128)(2,1)S(1)} %get-tuple-element.24.refs_0_), channel_id=1, source_target_pairs={{0,1},{16,51},{1,2},{17,16},{2,3},{18,17},{3,32},{19,18},{32,33},{... | collective-permute-start | bytes 1228808 | tf_op jit(solution)/shard_map/ppermute | solution.py:282
  62.4 13.0 %collective-permute-start.4 = (bf16[320,640]{1,0:T(8,128)(2,1)S(1)}, bf16[320,640]{1,0:T(8,128)(2,1)S(1)}, u32[]{:S(2)}, u32[]{:S(2)}) collective-permute-start(bf16[320,640]{1,0:T(8,128)(2,1)S(1)} %get-tuple-element.23.refs_1_), channel_id=1, source_target_pairs={{0,35},{16,17},{1,0},{17,18},{2,1},{18,19},{3,2},{19,48},{32,3},{4... | collective-permute-start | bytes 1228808 | tf_op jit(solution)/shard_map/ppermute | solution.py:285
  64.3 13.1 %collective-permute-start.8 = (bf16[320,640]{1,0:T(8,128)(2,1)S(1)}, bf16[320,640]{1,0:T(8,128)(2,1)S(1)}, u32[]{:S(2)}, u32[]{:S(2)}) collective-permute-start(bf16[320,640]{1,0:T(8,128)(2,1)S(1)} %get-tuple-element.23.refs_1_), channel_id=1, source_target_pairs={{0,1},{16,51},{1,2},{17,16},{2,3},{18,17},{3,32},{19,18},{32,33},{... | collective-permute-start | bytes 1228808 | tf_op jit(solution)/shard_map/ppermute | solution.py:282
  68.9 14.6 %collective-permute-start.2 = (bf16[320,640]{1,0:T(8,128)(2,1)S(1)}, bf16[320,640]{1,0:T(8,128)(2,1)}, u32[]{:S(2)}, u32[]{:S(2)}) collective-permute-start(bf16[320,640]{1,0:T(8,128)(2,1)S(1)} %get-tuple-element.24.refs_0_), channel_id=1, source_target_pairs={{0,35},{16,17},{1,0},{17,18},{2,1},{18,19},{3,2},{19,48},{32,3},{4... | collective-permute-start | bytes 1228808 | tf_op jit(solution)/shard_map/ppermute | solution.py:285
  70.8 53.9 %copy-start = (bf16[320,640]{1,0:T(8,128)(2,1)}, bf16[320,640]{1,0:T(8,128)(2,1)S(1)}, u32[]{:S(2)}) copy-start(bf16[320,640]{1,0:T(8,128)(2,1)S(1)} %collective-permute-done.6.refs_10_) | copy-start | bytes 1228804
  70.8 28.3 %collective-permute-start.7 = (bf16[320,640]{1,0:T(8,128)(2,1)S(1)}, bf16[320,640]{1,0:T(8,128)(2,1)}, u32[]{:S(2)}, u32[]{:S(2)}) collective-permute-start(bf16[320,640]{1,0:T(8,128)(2,1)S(1)} %collective-permute-done.6.refs_10_), channel_id=1, source_target_pairs={{0,1},{16,51},{1,2},{17,16},{2,3},{18,17},{3,32},{19,18},{32,33},{... | collective-permute-start | bytes 1228808 | tf_op jit(solution)/shard_map/ppermute | solution.py:282
  75.4 49.3 %copy-start.1 = (bf16[320,640]{1,0:T(8,128)(2,1)}, bf16[320,640]{1,0:T(8,128)(2,1)S(1)}, u32[]{:S(2)}) copy-start(bf16[320,640]{1,0:T(8,128)(2,1)S(1)} %collective-permute-done.4.refs_5_) | copy-start | bytes 1228804
  75.4 25.6 %collective-permute-start.5 = (bf16[320,640]{1,0:T(8,128)(2,1)S(1)}, bf16[320,640]{1,0:T(8,128)(2,1)}, u32[]{:S(2)}, u32[]{:S(2)}) collective-permute-start(bf16[320,640]{1,0:T(8,128)(2,1)S(1)} %collective-permute-done.4.refs_5_), channel_id=1, source_target_pairs={{0,35},{16,17},{1,0},{17,18},{2,1},{18,19},{3,2},{19,48},{32,3},{4... | collective-permute-start | bytes 1228808 | tf_op jit(solution)/shard_map/ppermute | solution.py:285
  77.4 47.4 %copy-start.2 = (bf16[320,640]{1,0:T(8,128)(2,1)}, bf16[320,640]{1,0:T(8,128)(2,1)S(1)}, u32[]{:S(2)}) copy-start(bf16[320,640]{1,0:T(8,128)(2,1)S(1)} %collective-permute-done.8.refs_11_) | copy-start | bytes 1228804
  77.4 27.1 %collective-permute-start.9 = (bf16[320,640]{1,0:T(8,128)(2,1)S(1)}, bf16[320,640]{1,0:T(8,128)(2,1)}, u32[]{:S(2)}, u32[]{:S(2)}) collective-permute-start(bf16[320,640]{1,0:T(8,128)(2,1)S(1)} %collective-permute-done.8.refs_11_), channel_id=1, source_target_pairs={{0,1},{16,51},{1,2},{17,16},{2,3},{18,17},{3,32},{19,18},{32,33},{... | collective-permute-start | bytes 1228808 | tf_op jit(solution)/shard_map/ppermute | solution.py:282
  83.5 24.1 %collective-permute-start.3 = (bf16[320,640]{1,0:T(8,128)(2,1)}, bf16[320,640]{1,0:T(8,128)(2,1)}, u32[]{:S(2)}, u32[]{:S(2)}) collective-permute-start(bf16[320,640]{1,0:T(8,128)(2,1)} %collective-permute-done.2.refs_4_), channel_id=1, source_target_pairs={{0,35},{16,17},{1,0},{17,18},{2,1},{18,19},{3,2},{19,48},{32,3},{4... | collective-permute-start | bytes 1228808 | tf_op jit(solution)/shard_map/ppermute | solution.py:285
  87.2 37.5 %collective-permute-start = (bf16[2,128,1280]{2,1,0:T(8,128)(2,1)S(1)}, bf16[2,128,1280]{2,1,0:T(8,128)(2,1)S(1)}, u32[]{:S(2)}, u32[]{:S(2)}) collective-permute-start(bf16[2,128,1280]{2,1,0:T(8,128)(2,1)S(1)} %get-tuple-element.16.own_ref), channel_id=1, source_target_pairs={{0,16},{16,0},{1,17},{17,1},{2,18},{18,2},{3,19},{19,3},{4,20},{20... | collective-permute-start | bytes 1966088 | tf_op jit(solution)/shard_map/ppermute | solution.py:314
  99.1 11.1 %collective-permute-start.10 = (bf16[320,640]{1,0:T(8,128)(2,1)}, bf16[320,640]{1,0:T(8,128)(2,1)S(1)}, u32[]{:S(2)}, u32[]{:S(2)}) collective-permute-start(bf16[320,640]{1,0:T(8,128)(2,1)} %collective-permute-done.7.refs_2_), channel_id=1, source_target_pairs={{0,1},{16,51},{1,2},{17,16},{2,3},{18,17},{3,32},{19,18},{32,33},{... | collective-permute-start | bytes 1228808 | tf_op jit(solution)/shard_map/ppermute | solution.py:282
  101.1 14.9 %collective-permute-start.13 = (bf16[320,640]{1,0:T(8,128)(2,1)}, bf16[320,640]{1,0:T(8,128)(2,1)S(1)}, u32[]{:S(2)}, u32[]{:S(2)}) collective-permute-start(bf16[320,640]{1,0:T(8,128)(2,1)} %collective-permute-done.5.refs_1_), channel_id=1, source_target_pairs={{0,35},{16,17},{1,0},{17,18},{2,1},{18,19},{3,2},{19,48},{32,3},{4... | collective-permute-start | bytes 1228808 | tf_op jit(solution)/shard_map/ppermute | solution.py:285
  104.5 14.6 %collective-permute-start.11 = (bf16[320,640]{1,0:T(8,128)(2,1)}, bf16[320,640]{1,0:T(8,128)(2,1)S(1)}, u32[]{:S(2)}, u32[]{:S(2)}) collective-permute-start(bf16[320,640]{1,0:T(8,128)(2,1)} %collective-permute-done.9.refs_3_), channel_id=1, source_target_pairs={{0,1},{16,51},{1,2},{17,16},{2,3},{18,17},{3,32},{19,18},{32,33},{... | collective-permute-start | bytes 1228808 | tf_op jit(solution)/shard_map/ppermute | solution.py:282
  107.6 17.1 %collective-permute-start.12 = (bf16[320,640]{1,0:T(8,128)(2,1)}, bf16[320,640]{1,0:T(8,128)(2,1)S(1)}, u32[]{:S(2)}, u32[]{:S(2)}) collective-permute-start(bf16[320,640]{1,0:T(8,128)(2,1)} %collective-permute-done.3.refs_0_), channel_id=1, source_target_pairs={{0,35},{16,17},{1,0},{17,18},{2,1},{18,19},{3,2},{19,48},{32,3},{4... | collective-permute-start | bytes 1228808 | tf_op jit(solution)/shard_map/ppermute | solution.py:285
  110.2 14.5 %copy-start.3 = (bf16[320,640]{1,0:T(8,128)(2,1)}, bf16[320,640]{1,0:T(8,128)(2,1)S(1)}, u32[]{:S(2)}) copy-start(bf16[320,640]{1,0:T(8,128)(2,1)S(1)} %collective-permute-done.10.refs_6_) | copy-start | bytes 1228804
  110.3 22.1 %collective-permute-start.14 = (bf16[320,640]{1,0:T(8,128)(2,1)S(1)}, bf16[320,640]{1,0:T(8,128)(2,1)S(1)}, u32[]{:S(2)}, u32[]{:S(2)}) collective-permute-start(bf16[320,640]{1,0:T(8,128)(2,1)S(1)} %collective-permute-done.10.refs_6_), channel_id=1, source_target_pairs={{0,1},{16,51},{1,2},{17,16},{2,3},{18,17},{3,32},{19,18},{32,33},{... | collective-permute-start | bytes 1228808 | tf_op jit(solution)/shard_map/ppermute | solution.py:282
  115.9 8.8 %copy-start.4 = (bf16[320,640]{1,0:T(8,128)(2,1)}, bf16[320,640]{1,0:T(8,128)(2,1)S(1)}, u32[]{:S(2)}) copy-start(bf16[320,640]{1,0:T(8,128)(2,1)S(1)} %collective-permute-done.13.refs_9_) | copy-start | bytes 1228804
  115.9 16.4 %collective-permute-start.15 = (bf16[320,640]{1,0:T(8,128)(2,1)S(1)}, bf16[320,640]{1,0:T(8,128)(2,1)S(1)}, u32[]{:S(2)}, u32[]{:S(2)}) collective-permute-start(bf16[320,640]{1,0:T(8,128)(2,1)S(1)} %collective-permute-done.13.refs_9_), channel_id=1, source_target_pairs={{0,35},{16,17},{1,0},{17,18},{2,1},{18,19},{3,2},{19,48},{32,3},{4... | collective-permute-start | bytes 1228808 | tf_op jit(solution)/shard_map/ppermute | solution.py:285
  119.0 5.7 %copy-start.5 = (bf16[320,640]{1,0:T(8,128)(2,1)}, bf16[320,640]{1,0:T(8,128)(2,1)S(1)}, u32[]{:S(2)}) copy-start(bf16[320,640]{1,0:T(8,128)(2,1)S(1)} %collective-permute-done.11.refs_7_) | copy-start | bytes 1228804
  135.7 4.0 %collective-permute-start.16 = (bf16[2,1280,128]{2,1,0:T(8,128)(2,1)S(1)}, bf16[2,1280,128]{2,1,0:T(8,128)(2,1)S(1)}, u32[]{:S(2)}, u32[]{:S(2)}) collective-permute-start(bf16[2,1280,128]{2,1,0:T(8,128)(2,1)S(1)} %get-tuple-element.22), channel_id=1, source_target_pairs={{0,16},{16,0},{1,17},{17,1},{2,18},{18,2},{3,19},{19,3},{4,20},{20... | collective-permute-start | bytes 1966088 | tf_op jit(solution)/shard_map/ppermute | solution.py:322
  (1 other events, 0.8 us)

commit v9 on v8

--- a/solution.py
+++ b/solution.py
@@ -14,7 +14,7 @@
 ZS = 16
 GROUPS = 4
 PIECES = 4
-EARLY, LATE = (2, 1, 3), (0,)
+ORDERED = (2, 1, 3, 0)
 LOCAL = 2
 WIDTH = LOCAL * HDIM
 EPSILON = 1e-06
@@ -217,47 +217,37 @@
     )
 
 
-def early_body(facts_ref, own_ref, other_ref, *refs):
-    count = len(EARLY) * PIECES
-    total_ref, weight_ref, sems = refs[count:]
-    total_ref[...] = group_contexts(
-        EARLY, facts_ref, own_ref, other_ref, refs[:count], weight_ref, sems
-    )
-
-
-def late_body(facts_ref, own_ref, other_ref, early_ref, *refs):
-    count = len(LATE) * PIECES
-    own_out_ref, other_out_ref, weight_ref, sems = refs[count:]
-    total = group_contexts(LATE, facts_ref, own_ref, other_ref, refs[:count], weight_ref, sems)
-    total = by_z(total + early_ref[...])
+def encode_body(facts_ref, own_ref, other_ref, *refs):
+    outs, (weight_ref, sems) = refs[-4:-2], refs[-2:]
+    total = group_contexts(ORDERED, facts_ref, own_ref, other_ref, refs[:-4], weight_ref, sems)
+    total = by_z(total)
     for tile in range(4):
-        target = (own_out_ref, other_out_ref)[tile // 2]
-        target[tile % 2] = total[:, tile * PATCH : (tile + 1) * PATCH].astype(jnp.bfloat16)
-
-
-def encode(body, groups, out_shape, facts, arrays, pieces):
+        block = total[:, tile * PATCH : (tile + 1) * PATCH]
+        outs[tile // 2][tile % 2] = block.astype(jnp.bfloat16)
+
+
+def encode(facts, own, other, pieces):
     in_vmem = pl.BlockSpec(memory_space=pltpu.VMEM)
-    taken = [pieces[group * PIECES + k] for group in groups for k in range(PIECES)]
-    if groups == EARLY:
-        taken = [pltpu.with_memory_space_constraint(t, pltpu.HBM) for t in taken]
-    flops = 2 * 4 * PATCH * D * 4 * WIDTH * len(groups)
+    part = jax.ShapeDtypeStruct((2, D, PATCH), jnp.bfloat16)
+    taken = [pieces[group * PIECES + k] for group in ORDERED for k in range(PIECES)]
+    settled = len(taken) - 2
+    taken = [
+        pltpu.with_memory_space_constraint(t, pltpu.HBM) if i < settled else t
+        for i, t in enumerate(taken)
+    ]
     return pl.pallas_call(
-        body,
-        out_shape=out_shape,
-        in_specs=[pl.BlockSpec(memory_space=pltpu.SMEM)]
-        + [in_vmem] * len(arrays)
+        encode_body,
+        out_shape=(part, part),
+        in_specs=[pl.BlockSpec(memory_space=pltpu.SMEM), in_vmem, in_vmem]
         + [pl.BlockSpec(memory_space=pl.ANY)] * len(taken),
-        out_specs=jax.tree.map(lambda _: in_vmem, out_shape),
+        out_specs=(in_vmem, in_vmem),
         scratch_shapes=[
-            pltpu.VMEM((len(groups), 2, 2, D // 4, 4 * WIDTH), jnp.bfloat16),
-            pltpu.SemaphoreType.DMA((len(groups), PIECES)),
+            pltpu.VMEM((GROUPS, 2, 2, D // 4, 4 * WIDTH), jnp.bfloat16),
+            pltpu.SemaphoreType.DMA((GROUPS, PIECES)),
         ],
         compiler_params=vmem_params(),
-        cost_estimate=pl.CostEstimate(
-            flops=flops, bytes_accessed=len(groups) * D * 8 * WIDTH, transcendentals=0
-        ),
-        name=body.__name__,
-    )(facts, *arrays, *taken)
+        name="encode",
+    )(facts, own, other, *taken)
 
 
 def around_y(block):
@@ -313,12 +303,7 @@
     source, normed = normalise(facts, arrived.reshape(4, D, PATCH))
     other = lax.ppermute(normed, "core", swap)
 
-    early = jax.ShapeDtypeStruct((D, 4 * PATCH), jnp.float32)
-    part = jax.ShapeDtypeStruct((2, D, PATCH), jnp.bfloat16)
-    total = encode(early_body, EARLY, early, facts, (normed, other), pieces)
-    own_part, other_part = encode(
-        late_body, LATE, (part, part), facts, (normed, other, total), pieces
-    )
+    own_part, other_part = encode(facts, normed, other, pieces)
     back_part = lax.ppermute(other_part, "core", swap)
     encoded = (
         source.astype(jnp.float32) + own_part.astype(jnp.float32) + back_part.astype(jnp.float32)

time: 166 us -> 172 us (1.036)
  waiting for transfers between devices: 13.6 us -> 21.2 us
  starting transfers between devices: 76.6 us -> 78.4 us
    ppermute x7, waiting for transfers between devices: 9.04 us -> 16.4 us  [around_y(): falling[k] = lax.ppermute(falling[k], ('y_hi', 'core', 'tensor'), ways(-1))]
    pallas_call x2 -> x1, Pallas kernels: 10.2 us -> 8.64 us  [encode(): pl.pallas_call(encode_body, out_shape=(part, part), in_specs=[pl.BlockSpe...]
  transfers between devices with their start and end apart: 18 -> 18, of which waited for: 7 -> 6; matrix products, arithmetic and copies ran while one was open for 0% -> 0% of each run, Pallas kernels for 6% -> 2%
where the time goes in v9:
time: 172 us; the launch traced here: 171 us
  starting transfers between devices  78.4 us (46%)
  blocking collectives  54.8 us (32%)
  waiting for transfers between devices  21.2 us (12%)
  Pallas kernels  14.2 us (8%)
    all_gather x1, blocking collectives, local(): block = lax.all_gather(both, 'z', axis=0, tiled=True)  31.9 us
    ppermute x7, starting transfers between devices, around_y(): rising[k] = lax.ppermute(rising[k], ('y_hi', 'core', 'tensor'), ways(1))  27.8 us
    all_to_all x1, blocking collectives, local(): lax.all_to_all(encoded.reshape(8, D // 4, PATCH), ('bal_hi', 'tensor'), 0...  22.9 us
    ppermute x7, waiting for transfers between devices, around_y(): falling[k] = lax.ppermute(falling[k], ('y_hi', 'core', 'tensor'), ways(-1))  16.4 us
    ppermute x7, starting transfers between devices, around_y(): falling[k] = lax.ppermute(falling[k], ('y_hi', 'core', 'tensor'), ways(-1))  15.5 us
    ppermute x1, starting transfers between devices, local(): other = lax.ppermute(normed, 'core', swap)  12.8 us
    ppermute x1, starting transfers between devices, local(): got = lax.ppermute(send, 'core', swap)  11.7 us
    pallas_call x1, Pallas kernels, encode(): pl.pallas_call(encode_body, out_shape=(part, part), in_specs=[pl.BlockSpe...  8.64 us
  transfers between devices with their start and end apart: 18, of which 6 were waited for; matrix products, arithmetic and copies ran while one was open for 0% of the time, Pallas kernels for 2%

profile of v9, /device:TPU:1, one launch (start us, length us, event | category | flops | bytes accessed | tf_op | source)
XLA Modules:
  0.0 170.9 jit_solution(1117080482977616332)
XLA Ops:
  0.7 2.9 %rotate.1 = bf16[16,320,128]{2,1,0:T(8,128)(2,1)} custom-call(s32[12]{0:T(128)S(1)} %concatenate.6.facts_ref, bf16[16,320,128]{2,1,0:T(8,128)(2,1)} %bitcast.13), custom_call_target="tpu_custom_call" | custom-call | tf_op jit(solution)/shard_map/rotate/pallas_call | solution.py:91
  3.6 8.0 %all-to-all-start = ((bf16[16,320,128]{2,1,0:T(8,128)(2,1)}), bf16[16,320,128]{2,1,0:T(8,128)(2,1)S(1)}, u32[]{:S(2)}, u32[]{:S(2)}) async-start(bf16[16,320,128]{2,1,0:T(8,128)(2,1)} %rotate.1), calls=%async_computation | async-start | bytes 2621440 | tf_op jit(solution)/shard_map/all_to_all | solution.py:295
  12.6 11.7 %collective-permute-start.1 = (bf16[20,640]{1,0:T(8,128)(2,1)S(1)}, bf16[20,640]{1,0:T(8,128)(2,1)S(1)}, u32[]{:S(2)}, u32[]{:S(2)}) collective-permute-start(bf16[20,640]{1,0:T(8,128)(2,1)S(1)} %get-tuple-element.20), channel_id=1, source_target_pairs={{0,16},{16,0},{1,17},{17,1},{2,18},{18,2},{3,19},{19,3},{4,20},{20... | collective-permute-start | bytes 76808 | tf_op jit(solution)/shard_map/ppermute | solution.py:298
  25.2 31.9 %all_gather.3 = bf16[640,640]{1,0:T(8,128)(2,1)S(1)} all-gather(bf16[40,640]{1,0:T(8,128)(2,1)S(1)} %pad_maximum_fusion), channel_id=1, replica_groups=mesh['z'=16,'y_hi'=2,'core'=2,'bal_hi'=2,'bal_lo'=2,'tensor'=4] {'z'}, dimensions={0}, use_global_device_ids=true | all-gather | bytes 870400 | tf_op jit(solution)/shard_map/all_gather | solution.py:301
  57.2 3.4 %collective-permute-start.4 = (bf16[320,640]{1,0:T(8,128)(2,1)S(1)}, bf16[320,640]{1,0:T(8,128)(2,1)S(1)}, u32[]{:S(2)}, u32[]{:S(2)}) collective-permute-start(bf16[320,640]{1,0:T(8,128)(2,1)S(1)} %get-tuple-element.23.refs_13_), channel_id=1, source_target_pairs={{0,35},{16,17},{1,0},{17,18},{2,1},{18,19},{3,2},{19,48},{32,3},{4... | collective-permute-start | bytes 1228808 | tf_op jit(solution)/shard_map/ppermute | solution.py:275
  60.7 3.7 %collective-permute-start.6 = (bf16[320,640]{1,0:T(8,128)(2,1)S(1)}, bf16[320,640]{1,0:T(8,128)(2,1)S(1)}, u32[]{:S(2)}, u32[]{:S(2)}) collective-permute-start(bf16[320,640]{1,0:T(8,128)(2,1)S(1)} %get-tuple-element.24.refs_12_), channel_id=1, source_target_pairs={{0,1},{16,51},{1,2},{17,16},{2,3},{18,17},{3,32},{19,18},{32,33},{... | collective-permute-start | bytes 1228808 | tf_op jit(solution)/shard_map/ppermute | solution.py:272
  64.4 3.4 %collective-permute-start.8 = (bf16[320,640]{1,0:T(8,128)(2,1)S(1)}, bf16[320,640]{1,0:T(8,128)(2,1)S(1)}, u32[]{:S(2)}, u32[]{:S(2)}) collective-permute-start(bf16[320,640]{1,0:T(8,128)(2,1)S(1)} %get-tuple-element.23.refs_13_), channel_id=1, source_target_pairs={{0,1},{16,51},{1,2},{17,16},{2,3},{18,17},{3,32},{19,18},{32,33},{... | collective-permute-start | bytes 1228808 | tf_op jit(solution)/shard_map/ppermute | solution.py:272
  67.7 1.9 %collective-permute-start.2 = (bf16[320,640]{1,0:T(8,128)(2,1)S(1)}, bf16[320,640]{1,0:T(8,128)(2,1)}, u32[]{:S(2)}, u32[]{:S(2)}) collective-permute-start(bf16[320,640]{1,0:T(8,128)(2,1)S(1)} %get-tuple-element.24.refs_12_), channel_id=1, source_target_pairs={{0,35},{16,17},{1,0},{17,18},{2,1},{18,19},{3,2},{19,48},{32,3},{4... | collective-permute-start | bytes 1228808 | tf_op jit(solution)/shard_map/ppermute | solution.py:275
  69.7 1.9 %collective-permute-start.5 = (bf16[320,640]{1,0:T(8,128)(2,1)S(1)}, bf16[320,640]{1,0:T(8,128)(2,1)}, u32[]{:S(2)}, u32[]{:S(2)}) collective-permute-start(bf16[320,640]{1,0:T(8,128)(2,1)S(1)} %collective-permute-done.4.refs_5_), channel_id=1, source_target_pairs={{0,35},{16,17},{1,0},{17,18},{2,1},{18,19},{3,2},{19,48},{32,3},{4... | collective-permute-start | bytes 1228808 | tf_op jit(solution)/shard_map/ppermute | solution.py:275
  71.6 4.6 %collective-permute-start.7 = (bf16[320,640]{1,0:T(8,128)(2,1)S(1)}, bf16[320,640]{1,0:T(8,128)(2,1)}, u32[]{:S(2)}, u32[]{:S(2)}) collective-permute-start(bf16[320,640]{1,0:T(8,128)(2,1)S(1)} %collective-permute-done.6.refs_10_), channel_id=1, source_target_pairs={{0,1},{16,51},{1,2},{17,16},{2,3},{18,17},{3,32},{19,18},{32,33},{... | collective-permute-start | bytes 1228808 | tf_op jit(solution)/shard_map/ppermute | solution.py:272
  76.2 2.2 %collective-permute-done.8.refs_11_ = bf16[320,640]{1,0:T(8,128)(2,1)S(1)} collective-permute-done((bf16[320,640]{1,0:T(8,128)(2,1)S(1)}, bf16[320,640]{1,0:T(8,128)(2,1)S(1)}, u32[]{:S(2)}, u32[]{:S(2)}) %collective-permute-start.8) | collective-permute-done | bytes 409632 | tf_op jit(solution)/shard_map/ppermute | solution.py:272
  78.4 4.1 %collective-permute-start.9 = (bf16[320,640]{1,0:T(8,128)(2,1)S(1)}, bf16[320,640]{1,0:T(8,128)(2,1)}, u32[]{:S(2)}, u32[]{:S(2)}) collective-permute-start(bf16[320,640]{1,0:T(8,128)(2,1)S(1)} %collective-permute-done.8.refs_11_), channel_id=1, source_target_pairs={{0,1},{16,51},{1,2},{17,16},{2,3},{18,17},{3,32},{19,18},{32,33},{... | collective-permute-start | bytes 1228808 | tf_op jit(solution)/shard_map/ppermute | solution.py:272
  82.6 1.9 %collective-permute-start.3 = (bf16[320,640]{1,0:T(8,128)(2,1)}, bf16[320,640]{1,0:T(8,128)(2,1)}, u32[]{:S(2)}, u32[]{:S(2)}) collective-permute-start(bf16[320,640]{1,0:T(8,128)(2,1)} %collective-permute-done.2.refs_4_), channel_id=1, source_target_pairs={{0,35},{16,17},{1,0},{17,18},{2,1},{18,19},{3,2},{19,48},{32,3},{4... | collective-permute-start | bytes 1228808 | tf_op jit(solution)/shard_map/ppermute | solution.py:275
  84.5 4.5 %collective-permute-done.5.refs_1_ = bf16[320,640]{1,0:T(8,128)(2,1)} collective-permute-done((bf16[320,640]{1,0:T(8,128)(2,1)S(1)}, bf16[320,640]{1,0:T(8,128)(2,1)}, u32[]{:S(2)}, u32[]{:S(2)}) %collective-permute-start.5) | collective-permute-done | bytes 409632 | tf_op jit(solution)/shard_map/ppermute | solution.py:275
  91.0 4.6 %collective-permute-start.10 = (bf16[320,640]{1,0:T(8,128)(2,1)}, bf16[320,640]{1,0:T(8,128)(2,1)}, u32[]{:S(2)}, u32[]{:S(2)}) collective-permute-start(bf16[320,640]{1,0:T(8,128)(2,1)} %collective-permute-done.7.refs_2_), channel_id=1, source_target_pairs={{0,1},{16,51},{1,2},{17,16},{2,3},{18,17},{3,32},{19,18},{32,33},{... | collective-permute-start | bytes 1228808 | tf_op jit(solution)/shard_map/ppermute | solution.py:272
  97.4 12.8 %collective-permute-start = (bf16[2,128,1280]{2,1,0:T(8,128)(2,1)S(1)}, bf16[2,128,1280]{2,1,0:T(8,128)(2,1)S(1)}, u32[]{:S(2)}, u32[]{:S(2)}) collective-permute-start(bf16[2,128,1280]{2,1,0:T(8,128)(2,1)S(1)} %get-tuple-element.16.own_ref), channel_id=1, source_target_pairs={{0,16},{16,0},{1,17},{17,1},{2,18},{18,2},{3,19},{19,3},{4,20},{20... | collective-permute-start | bytes 1966088 | tf_op jit(solution)/shard_map/ppermute | solution.py:304
  110.2 2.9 %collective-permute-start.11 = (bf16[320,640]{1,0:T(8,128)(2,1)}, bf16[320,640]{1,0:T(8,128)(2,1)S(1)}, u32[]{:S(2)}, u32[]{:S(2)}) collective-permute-start(bf16[320,640]{1,0:T(8,128)(2,1)} %collective-permute-done.9.refs_3_), channel_id=1, source_target_pairs={{0,1},{16,51},{1,2},{17,16},{2,3},{18,17},{3,32},{19,18},{32,33},{... | collective-permute-start | bytes 1228808 | tf_op jit(solution)/shard_map/ppermute | solution.py:272
  113.0 2.4 %collective-permute-start.12 = (bf16[320,640]{1,0:T(8,128)(2,1)}, bf16[320,640]{1,0:T(8,128)(2,1)S(1)}, u32[]{:S(2)}, u32[]{:S(2)}) collective-permute-start(bf16[320,640]{1,0:T(8,128)(2,1)} %collective-permute-done.3.refs_0_), channel_id=1, source_target_pairs={{0,35},{16,17},{1,0},{17,18},{2,1},{18,19},{3,2},{19,48},{32,3},{4... | collective-permute-start | bytes 1228808 | tf_op jit(solution)/shard_map/ppermute | solution.py:275
  117.4 4.6 %collective-permute-start.14 = (bf16[320,640]{1,0:T(8,128)(2,1)}, bf16[320,640]{1,0:T(8,128)(2,1)S(1)}, u32[]{:S(2)}, u32[]{:S(2)}) collective-permute-start(bf16[320,640]{1,0:T(8,128)(2,1)} %collective-permute-done.10.refs_6_), channel_id=1, source_target_pairs={{0,1},{16,51},{1,2},{17,16},{2,3},{18,17},{3,32},{19,18},{32,33},{... | collective-permute-start | bytes 1228808 | tf_op jit(solution)/shard_map/ppermute | solution.py:272
  122.0 3.1 %collective-permute-done.12.refs_8_ = bf16[320,640]{1,0:T(8,128)(2,1)S(1)} collective-permute-done((bf16[320,640]{1,0:T(8,128)(2,1)}, bf16[320,640]{1,0:T(8,128)(2,1)S(1)}, u32[]{:S(2)}, u32[]{:S(2)}) %collective-permute-start.12) | collective-permute-done | bytes 409632 | tf_op jit(solution)/shard_map/ppermute | solution.py:275
  125.2 8.8 %collective-permute-done.15.refs_15_ = bf16[320,640]{1,0:T(8,128)(2,1)S(1)} collective-permute-done((bf16[320,640]{1,0:T(8,128)(2,1)}, bf16[320,640]{1,0:T(8,128)(2,1)S(1)}, u32[]{:S(2)}, u32[]{:S(2)}) %collective-permute-start.15) | collective-permute-done | bytes 409632 | tf_op jit(solution)/shard_map/ppermute | solution.py:275
  134.0 8.6 %encode.1 = (bf16[2,1280,128]{2,1,0:T(8,128)(2,1)S(1)}, bf16[2,1280,128]{2,1,0:T(8,128)(2,1)S(1)}) custom-call(s32[12]{0:T(128)S(1)} %concatenate.6.facts_ref, bf16[2,128,1280]{2,1,0:T(8,128)(2,1)S(1)} %get-tuple-element.16.own_ref, bf16[2,128,1280]{2,1,0:T(8,128)(2,1)S(1)} %collective-permute-done.other_ref, ...), custom_call_target="tpu_custom_call" | custom-call | tf_op jit(solution)/shard_map/encode/pallas_call | solution.py:238
  142.6 2.6 %collective-permute-start.16 = (bf16[2,1280,128]{2,1,0:T(8,128)(2,1)S(1)}, bf16[2,1280,128]{2,1,0:T(8,128)(2,1)S(1)}, u32[]{:S(2)}, u32[]{:S(2)}) collective-permute-start(bf16[2,1280,128]{2,1,0:T(8,128)(2,1)S(1)} %get-tuple-element.22), channel_id=1, source_target_pairs={{0,16},{16,0},{1,17},{17,1},{2,18},{18,2},{3,19},{19,3},{4,20},{20... | collective-permute-start | bytes 1966088 | tf_op jit(solution)/shard_map/ppermute | solution.py:307
  147.2 22.9 %all_to_all.10 = bf16[8,320,128]{2,1,0:T(8,128)(2,1)S(1)} all-to-all(bf16[8,320,128]{2,1,0:T(8,128)(2,1)S(1)} %bitcast.11), channel_id=1, replica_groups=mesh['z'=16,'y_hi'=2,'core'=2,'bal_hi'=2,'bal_lo'=2,'tensor'=4] {'bal_hi..., dimensions={0} | all-to-all | bytes 1310720 | tf_op jit(solution)/shard_map/all_to_all | solution.py:311
  (38 shorter events, 11.1 us)
Async XLA Ops:
  3.6 91.9 %all-to-all-start = ((bf16[16,320,128]{2,1,0:T(8,128)(2,1)}), bf16[16,320,128]{2,1,0:T(8,128)(2,1)S(1)}, u32[]{:S(2)}, u32[]{:S(2)}) async-start(bf16[16,320,128]{2,1,0:T(8,128)(2,1)} %rotate.1), calls=%async_computation | async-start | bytes 2621440 | tf_op jit(solution)/shard_map/all_to_all | solution.py:295
  12.6 12.6 %collective-permute-start.1 = (bf16[20,640]{1,0:T(8,128)(2,1)S(1)}, bf16[20,640]{1,0:T(8,128)(2,1)S(1)}, u32[]{:S(2)}, u32[]{:S(2)}) collective-permute-start(bf16[20,640]{1,0:T(8,128)(2,1)S(1)} %get-tuple-element.20), channel_id=1, source_target_pairs={{0,16},{16,0},{1,17},{17,1},{2,18},{18,2},{3,19},{19,3},{4,20},{20... | collective-permute-start | bytes 76808 | tf_op jit(solution)/shard_map/ppermute | solution.py:298
  57.2 76.7 %copy-start = (bf16[320,640]{1,0:T(8,128)(2,1)}, bf16[320,640]{1,0:T(8,128)(2,1)S(1)}, u32[]{:S(2)}) copy-start(bf16[320,640]{1,0:T(8,128)(2,1)S(1)} %get-tuple-element.23.refs_13_) | copy-start | bytes 1228804
  57.2 76.7 %copy-start.1 = (bf16[320,640]{1,0:T(8,128)(2,1)}, bf16[320,640]{1,0:T(8,128)(2,1)S(1)}, u32[]{:S(2)}) copy-start(bf16[320,640]{1,0:T(8,128)(2,1)S(1)} %get-tuple-element.24.refs_12_) | copy-start | bytes 1228804
  57.2 12.4 %collective-permute-start.4 = (bf16[320,640]{1,0:T(8,128)(2,1)S(1)}, bf16[320,640]{1,0:T(8,128)(2,1)S(1)}, u32[]{:S(2)}, u32[]{:S(2)}) collective-permute-start(bf16[320,640]{1,0:T(8,128)(2,1)S(1)} %get-tuple-element.23.refs_13_), channel_id=1, source_target_pairs={{0,35},{16,17},{1,0},{17,18},{2,1},{18,19},{3,2},{19,48},{32,3},{4... | collective-permute-start | bytes 1228808 | tf_op jit(solution)/shard_map/ppermute | solution.py:275
  60.7 10.9 %collective-permute-start.6 = (bf16[320,640]{1,0:T(8,128)(2,1)S(1)}, bf16[320,640]{1,0:T(8,128)(2,1)S(1)}, u32[]{:S(2)}, u32[]{:S(2)}) collective-permute-start(bf16[320,640]{1,0:T(8,128)(2,1)S(1)} %get-tuple-element.24.refs_12_), channel_id=1, source_target_pairs={{0,1},{16,51},{1,2},{17,16},{2,3},{18,17},{3,32},{19,18},{32,33},{... | collective-permute-start | bytes 1228808 | tf_op jit(solution)/shard_map/ppermute | solution.py:272
  64.4 14.1 %collective-permute-start.8 = (bf16[320,640]{1,0:T(8,128)(2,1)S(1)}, bf16[320,640]{1,0:T(8,128)(2,1)S(1)}, u32[]{:S(2)}, u32[]{:S(2)}) collective-permute-start(bf16[320,640]{1,0:T(8,128)(2,1)S(1)} %get-tuple-element.23.refs_13_), channel_id=1, source_target_pairs={{0,1},{16,51},{1,2},{17,16},{2,3},{18,17},{3,32},{19,18},{32,33},{... | collective-permute-start | bytes 1228808 | tf_op jit(solution)/shard_map/ppermute | solution.py:272
  67.7 14.9 %collective-permute-start.2 = (bf16[320,640]{1,0:T(8,128)(2,1)S(1)}, bf16[320,640]{1,0:T(8,128)(2,1)}, u32[]{:S(2)}, u32[]{:S(2)}) collective-permute-start(bf16[320,640]{1,0:T(8,128)(2,1)S(1)} %get-tuple-element.24.refs_12_), channel_id=1, source_target_pairs={{0,35},{16,17},{1,0},{17,18},{2,1},{18,19},{3,2},{19,48},{32,3},{4... | collective-permute-start | bytes 1228808 | tf_op jit(solution)/shard_map/ppermute | solution.py:275
  69.7 64.3 %copy-start.2 = (bf16[320,640]{1,0:T(8,128)(2,1)}, bf16[320,640]{1,0:T(8,128)(2,1)S(1)}, u32[]{:S(2)}) copy-start(bf16[320,640]{1,0:T(8,128)(2,1)S(1)} %collective-permute-done.4.refs_5_) | copy-start | bytes 1228804
  69.7 19.4 %collective-permute-start.5 = (bf16[320,640]{1,0:T(8,128)(2,1)S(1)}, bf16[320,640]{1,0:T(8,128)(2,1)}, u32[]{:S(2)}, u32[]{:S(2)}) collective-permute-start(bf16[320,640]{1,0:T(8,128)(2,1)S(1)} %collective-permute-done.4.refs_5_), channel_id=1, source_target_pairs={{0,35},{16,17},{1,0},{17,18},{2,1},{18,19},{3,2},{19,48},{32,3},{4... | collective-permute-start | bytes 1228808 | tf_op jit(solution)/shard_map/ppermute | solution.py:275
  71.6 62.3 %copy-start.3 = (bf16[320,640]{1,0:T(8,128)(2,1)}, bf16[320,640]{1,0:T(8,128)(2,1)S(1)}, u32[]{:S(2)}) copy-start(bf16[320,640]{1,0:T(8,128)(2,1)S(1)} %collective-permute-done.6.refs_10_) | copy-start | bytes 1228804
  71.6 19.4 %collective-permute-start.7 = (bf16[320,640]{1,0:T(8,128)(2,1)S(1)}, bf16[320,640]{1,0:T(8,128)(2,1)}, u32[]{:S(2)}, u32[]{:S(2)}) collective-permute-start(bf16[320,640]{1,0:T(8,128)(2,1)S(1)} %collective-permute-done.6.refs_10_), channel_id=1, source_target_pairs={{0,1},{16,51},{1,2},{17,16},{2,3},{18,17},{3,32},{19,18},{32,33},{... | collective-permute-start | bytes 1228808 | tf_op jit(solution)/shard_map/ppermute | solution.py:272
  78.4 55.5 %copy-start.4 = (bf16[320,640]{1,0:T(8,128)(2,1)}, bf16[320,640]{1,0:T(8,128)(2,1)S(1)}, u32[]{:S(2)}) copy-start(bf16[320,640]{1,0:T(8,128)(2,1)S(1)} %collective-permute-done.8.refs_11_) | copy-start | bytes 1228804
  78.4 31.7 %collective-permute-start.9 = (bf16[320,640]{1,0:T(8,128)(2,1)S(1)}, bf16[320,640]{1,0:T(8,128)(2,1)}, u32[]{:S(2)}, u32[]{:S(2)}) collective-permute-start(bf16[320,640]{1,0:T(8,128)(2,1)S(1)} %collective-permute-done.8.refs_11_), channel_id=1, source_target_pairs={{0,1},{16,51},{1,2},{17,16},{2,3},{18,17},{3,32},{19,18},{32,33},{... | collective-permute-start | bytes 1228808 | tf_op jit(solution)/shard_map/ppermute | solution.py:272
  82.6 30.4 %collective-permute-start.3 = (bf16[320,640]{1,0:T(8,128)(2,1)}, bf16[320,640]{1,0:T(8,128)(2,1)}, u32[]{:S(2)}, u32[]{:S(2)}) collective-permute-start(bf16[320,640]{1,0:T(8,128)(2,1)} %collective-permute-done.2.refs_4_), channel_id=1, source_target_pairs={{0,35},{16,17},{1,0},{17,18},{2,1},{18,19},{3,2},{19,48},{32,3},{4... | collective-permute-start | bytes 1228808 | tf_op jit(solution)/shard_map/ppermute | solution.py:275
  89.1 26.4 %collective-permute-start.13 = (bf16[320,640]{1,0:T(8,128)(2,1)}, bf16[320,640]{1,0:T(8,128)(2,1)}, u32[]{:S(2)}, u32[]{:S(2)}) collective-permute-start(bf16[320,640]{1,0:T(8,128)(2,1)} %collective-permute-done.5.refs_1_), channel_id=1, source_target_pairs={{0,35},{16,17},{1,0},{17,18},{2,1},{18,19},{3,2},{19,48},{32,3},{4... | collective-permute-start | bytes 1228808 | tf_op jit(solution)/shard_map/ppermute | solution.py:275
  91.0 26.4 %collective-permute-start.10 = (bf16[320,640]{1,0:T(8,128)(2,1)}, bf16[320,640]{1,0:T(8,128)(2,1)}, u32[]{:S(2)}, u32[]{:S(2)}) collective-permute-start(bf16[320,640]{1,0:T(8,128)(2,1)} %collective-permute-done.7.refs_2_), channel_id=1, source_target_pairs={{0,1},{16,51},{1,2},{17,16},{2,3},{18,17},{3,32},{19,18},{32,33},{... | collective-permute-start | bytes 1228808 | tf_op jit(solution)/shard_map/ppermute | solution.py:272
  97.4 36.6 %collective-permute-start = (bf16[2,128,1280]{2,1,0:T(8,128)(2,1)S(1)}, bf16[2,128,1280]{2,1,0:T(8,128)(2,1)S(1)}, u32[]{:S(2)}, u32[]{:S(2)}) collective-permute-start(bf16[2,128,1280]{2,1,0:T(8,128)(2,1)S(1)} %get-tuple-element.16.own_ref), channel_id=1, source_target_pairs={{0,16},{16,0},{1,17},{17,1},{2,18},{18,2},{3,19},{19,3},{4,20},{20... | collective-permute-start | bytes 1966088 | tf_op jit(solution)/shard_map/ppermute | solution.py:304
  110.2 11.8 %collective-permute-start.11 = (bf16[320,640]{1,0:T(8,128)(2,1)}, bf16[320,640]{1,0:T(8,128)(2,1)S(1)}, u32[]{:S(2)}, u32[]{:S(2)}) collective-permute-start(bf16[320,640]{1,0:T(8,128)(2,1)} %collective-permute-done.9.refs_3_), channel_id=1, source_target_pairs={{0,1},{16,51},{1,2},{17,16},{2,3},{18,17},{3,32},{19,18},{32,33},{... | collective-permute-start | bytes 1228808 | tf_op jit(solution)/shard_map/ppermute | solution.py:272
  113.0 12.1 %collective-permute-start.12 = (bf16[320,640]{1,0:T(8,128)(2,1)}, bf16[320,640]{1,0:T(8,128)(2,1)S(1)}, u32[]{:S(2)}, u32[]{:S(2)}) collective-permute-start(bf16[320,640]{1,0:T(8,128)(2,1)} %collective-permute-done.3.refs_0_), channel_id=1, source_target_pairs={{0,35},{16,17},{1,0},{17,18},{2,1},{18,19},{3,2},{19,48},{32,3},{4... | collective-permute-start | bytes 1228808 | tf_op jit(solution)/shard_map/ppermute | solution.py:275
  115.5 18.4 %collective-permute-start.15 = (bf16[320,640]{1,0:T(8,128)(2,1)}, bf16[320,640]{1,0:T(8,128)(2,1)S(1)}, u32[]{:S(2)}, u32[]{:S(2)}) collective-permute-start(bf16[320,640]{1,0:T(8,128)(2,1)} %collective-permute-done.13.refs_9_), channel_id=1, source_target_pairs={{0,35},{16,17},{1,0},{17,18},{2,1},{18,19},{3,2},{19,48},{32,3},{4... | collective-permute-start | bytes 1228808 | tf_op jit(solution)/shard_map/ppermute | solution.py:275
  117.4 16.5 %collective-permute-start.14 = (bf16[320,640]{1,0:T(8,128)(2,1)}, bf16[320,640]{1,0:T(8,128)(2,1)S(1)}, u32[]{:S(2)}, u32[]{:S(2)}) collective-permute-start(bf16[320,640]{1,0:T(8,128)(2,1)} %collective-permute-done.10.refs_6_), channel_id=1, source_target_pairs={{0,1},{16,51},{1,2},{17,16},{2,3},{18,17},{3,32},{19,18},{32,33},{... | collective-permute-start | bytes 1228808 | tf_op jit(solution)/shard_map/ppermute | solution.py:272
  122.0 11.9 %copy-start.5 = (bf16[320,640]{1,0:T(8,128)(2,1)}, bf16[320,640]{1,0:T(8,128)(2,1)S(1)}, u32[]{:S(2)}) copy-start(bf16[320,640]{1,0:T(8,128)(2,1)S(1)} %collective-permute-done.11.refs_7_) | copy-start | bytes 1228804
  142.6 4.3 %collective-permute-start.16 = (bf16[2,1280,128]{2,1,0:T(8,128)(2,1)S(1)}, bf16[2,1280,128]{2,1,0:T(8,128)(2,1)S(1)}, u32[]{:S(2)}, u32[]{:S(2)}) collective-permute-start(bf16[2,1280,128]{2,1,0:T(8,128)(2,1)S(1)} %get-tuple-element.22), channel_id=1, source_target_pairs={{0,16},{16,0},{1,17},{17,1},{2,18},{18,2},{3,19},{19,3},{4,20},{20... | collective-permute-start | bytes 1966088 | tf_op jit(solution)/shard_map/ppermute | solution.py:307
  (1 other events, 8.8 us)

commit v10 on v8

--- a/solution.py
+++ b/solution.py
@@ -152,7 +152,8 @@
 
 
 def attend(qkv):
-    pairs = [(tile, head) for tile in range(4) for head in range(LOCAL)]
+    count = qkv.shape[1] // PATCH
+    pairs = [(tile, head) for tile in range(count) for head in range(LOCAL)]
 
     def part(kind, tile, head):
         low = kind * WIDTH + head * HDIM
@@ -177,13 +178,13 @@
     return jnp.concatenate(
         [
             jnp.concatenate(contexts[tile * LOCAL : (tile + 1) * LOCAL], axis=0)
-            for tile in range(4)
+            for tile in range(count)
         ],
         axis=1,
     )
 
 
-def group_contexts(groups, facts_ref, own_ref, other_ref, pieces, weight_ref, sems):
+def group_contexts(groups, facts_ref, normed_refs, pieces, weight_ref, sems):
     def copies(n, group):
         made = []
         for k in range(PIECES):
@@ -200,7 +201,7 @@
         for copy in copies(n, group):
             copy.start()
     normed = jnp.concatenate(
-        [ref[...].reshape(2 * PATCH, D) for ref in (own_ref, other_ref)], axis=0
+        [ref[...].reshape(2 * PATCH, D) for ref in normed_refs], axis=0
     )
     contexts, outs = [], []
     for n, group in enumerate(groups):
@@ -218,21 +219,18 @@
 
 
 def early_body(facts_ref, own_ref, other_ref, *refs):
-    count = len(EARLY) * PIECES
-    total_ref, weight_ref, sems = refs[count:]
-    total_ref[...] = group_contexts(
-        EARLY, facts_ref, own_ref, other_ref, refs[:count], weight_ref, sems
-    )
-
-
-def late_body(facts_ref, own_ref, other_ref, early_ref, *refs):
-    count = len(LATE) * PIECES
-    own_out_ref, other_out_ref, weight_ref, sems = refs[count:]
-    total = group_contexts(LATE, facts_ref, own_ref, other_ref, refs[:count], weight_ref, sems)
+    own_total_ref, other_total_ref, weight_ref, sems = refs[-4:]
+    total = group_contexts(EARLY, facts_ref, (own_ref, other_ref), refs[:-4], weight_ref, sems)
+    own_total_ref[...] = total[:, : 2 * PATCH]
+    other_total_ref[...] = total[:, 2 * PATCH :]
+
+
+def late_body(facts_ref, normed_ref, early_ref, *refs):
+    out_ref, weight_ref, sems = refs[-3:]
+    total = group_contexts(LATE, facts_ref, (normed_ref,), refs[:-3], weight_ref, sems)
     total = by_z(total + early_ref[...])
-    for tile in range(4):
-        target = (own_out_ref, other_out_ref)[tile // 2]
-        target[tile % 2] = total[:, tile * PATCH : (tile + 1) * PATCH].astype(jnp.bfloat16)
+    for tile in range(2):
+        out_ref[tile] = total[:, tile * PATCH : (tile + 1) * PATCH].astype(jnp.bfloat16)
 
 
 def encode(body, groups, out_shape, facts, arrays, pieces):
@@ -313,13 +311,14 @@
     source, normed = normalise(facts, arrived.reshape(4, D, PATCH))
     other = lax.ppermute(normed, "core", swap)
 
-    early = jax.ShapeDtypeStruct((D, 4 * PATCH), jnp.float32)
+    early = jax.ShapeDtypeStruct((D, 2 * PATCH), jnp.float32)
     part = jax.ShapeDtypeStruct((2, D, PATCH), jnp.bfloat16)
-    total = encode(early_body, EARLY, early, facts, (normed, other), pieces)
-    own_part, other_part = encode(
-        late_body, LATE, (part, part), facts, (normed, other, total), pieces
-    )
+    own_total, other_total = encode(
+        early_body, EARLY, (early, early), facts, (normed, other), pieces
+    )
+    other_part = encode(late_body, LATE, part, facts, (other, other_total), pieces)
     back_part = lax.ppermute(other_part, "core", swap)
+    own_part = encode(late_body, LATE, part, facts, (normed, own_total), pieces)
     encoded = (
         source.astype(jnp.float32) + own_part.astype(jnp.float32) + back_part.astype(jnp.float32)
     ).astype(jnp.bfloat16)

time: 166 us -> 167 us (level)
  Pallas kernels: 15.7 us -> 17.8 us
  waiting for transfers between devices: 13.6 us -> 11.6 us
    pallas_call x2 -> x3, Pallas kernels: 10.2 us -> 12.3 us  [encode(): pl.pallas_call(body, out_shape=out_shape, in_specs=[pl.BlockSpec(memory_s...]
    ppermute x1, waiting for transfers between devices: 2.06 us -> 0.01 us  [local(): back_part = lax.ppermute(other_part, 'core', swap)]
  transfers between devices with their start and end apart: 18 -> 18, of which waited for: 7 -> 6; matrix products, arithmetic and copies ran while one was open for 0% -> 0% of each run, Pallas kernels for 6% -> 7%
where the time goes in v10:
time: 167 us; the launch traced here: 166 us
  starting transfers between devices  76.5 us (46%)
  blocking collectives  56.9 us (34%)
  Pallas kernels  17.8 us (11%)
  waiting for transfers between devices  11.6 us (7%)
  local copies, waits for them, and re-layouts  2.38 us (1%)
    all_gather x1, blocking collectives, local(): block = lax.all_gather(both, 'z', axis=0, tiled=True)  31.9 us
    ppermute x7, starting transfers between devices, around_y(): rising[k] = lax.ppermute(rising[k], ('y_hi', 'core', 'tensor'), ways(1))  27.8 us
    all_to_all x1, blocking collectives, local(): lax.all_to_all(encoded.reshape(8, D // 4, PATCH), ('bal_hi', 'tensor'), 0...  25 us
    ppermute x7, starting transfers between devices, around_y(): falling[k] = lax.ppermute(falling[k], ('y_hi', 'core', 'tensor'), ways(-1))  15.1 us
    pallas_call x3, Pallas kernels, encode(): pl.pallas_call(body, out_shape=out_shape, in_specs=[pl.BlockSpec(memory_s...  12.3 us
    ppermute x1, starting transfers between devices, local(): other = lax.ppermute(normed, 'core', swap)  11.8 us
    ppermute x1, starting transfers between devices, local(): got = lax.ppermute(send, 'core', swap)  11.8 us
    ppermute x7, waiting for transfers between devices, around_y(): falling[k] = lax.ppermute(falling[k], ('y_hi', 'core', 'tensor'), ways(-1))  9.08 us
  transfers between devices with their start and end apart: 18, of which 6 were waited for; matrix products, arithmetic and copies ran while one was open for 0% of the time, Pallas kernels for 7%

profile of v10, /device:TPU:1, one launch (start us, length us, event | category | flops | bytes accessed | tf_op | source)
XLA Modules:
  0.0 165.8 jit_solution(6525326449503564893)
XLA Ops:
  0.7 2.9 %rotate.1 = bf16[16,320,128]{2,1,0:T(8,128)(2,1)} custom-call(s32[12]{0:T(128)S(1)} %concatenate.6.facts_ref, bf16[16,320,128]{2,1,0:T(8,128)(2,1)} %bitcast.13), custom_call_target="tpu_custom_call" | custom-call | tf_op jit(solution)/shard_map/rotate/pallas_call | solution.py:91
  3.6 8.0 %all-to-all-start = ((bf16[16,320,128]{2,1,0:T(8,128)(2,1)}), bf16[16,320,128]{2,1,0:T(8,128)(2,1)S(1)}, u32[]{:S(2)}, u32[]{:S(2)}) async-start(bf16[16,320,128]{2,1,0:T(8,128)(2,1)} %rotate.1), calls=%async_computation | async-start | bytes 2621440 | tf_op jit(solution)/shard_map/all_to_all | solution.py:303
  12.6 11.8 %collective-permute-start.1 = (bf16[20,640]{1,0:T(8,128)(2,1)S(1)}, bf16[20,640]{1,0:T(8,128)(2,1)S(1)}, u32[]{:S(2)}, u32[]{:S(2)}) collective-permute-start(bf16[20,640]{1,0:T(8,128)(2,1)S(1)} %get-tuple-element.20), channel_id=1, source_target_pairs={{0,16},{16,0},{1,17},{17,1},{2,18},{18,2},{3,19},{19,3},{4,20},{20... | collective-permute-start | bytes 76808 | tf_op jit(solution)/shard_map/ppermute | solution.py:306
  25.2 31.9 %all_gather.3 = bf16[640,640]{1,0:T(8,128)(2,1)S(1)} all-gather(bf16[40,640]{1,0:T(8,128)(2,1)S(1)} %pad_maximum_fusion), channel_id=1, replica_groups=mesh['z'=16,'y_hi'=2,'core'=2,'bal_hi'=2,'bal_lo'=2,'tensor'=4] {'z'}, dimensions={0}, use_global_device_ids=true | all-gather | bytes 870400 | tf_op jit(solution)/shard_map/all_gather | solution.py:309
  57.2 5.2 %collective-permute-start.6 = (bf16[320,640]{1,0:T(8,128)(2,1)S(1)}, bf16[320,640]{1,0:T(8,128)(2,1)S(1)}, u32[]{:S(2)}, u32[]{:S(2)}) collective-permute-start(bf16[320,640]{1,0:T(8,128)(2,1)S(1)} %get-tuple-element.24.refs_0_), channel_id=1, source_target_pairs={{0,1},{16,51},{1,2},{17,16},{2,3},{18,17},{3,32},{19,18},{32,33},{... | collective-permute-start | bytes 1228808 | tf_op jit(solution)/shard_map/ppermute | solution.py:280
  62.4 1.9 %collective-permute-start.4 = (bf16[320,640]{1,0:T(8,128)(2,1)S(1)}, bf16[320,640]{1,0:T(8,128)(2,1)S(1)}, u32[]{:S(2)}, u32[]{:S(2)}) collective-permute-start(bf16[320,640]{1,0:T(8,128)(2,1)S(1)} %get-tuple-element.23.refs_1_), channel_id=1, source_target_pairs={{0,35},{16,17},{1,0},{17,18},{2,1},{18,19},{3,2},{19,48},{32,3},{4... | collective-permute-start | bytes 1228808 | tf_op jit(solution)/shard_map/ppermute | solution.py:283
  64.3 4.6 %collective-permute-start.8 = (bf16[320,640]{1,0:T(8,128)(2,1)S(1)}, bf16[320,640]{1,0:T(8,128)(2,1)S(1)}, u32[]{:S(2)}, u32[]{:S(2)}) collective-permute-start(bf16[320,640]{1,0:T(8,128)(2,1)S(1)} %get-tuple-element.23.refs_1_), channel_id=1, source_target_pairs={{0,1},{16,51},{1,2},{17,16},{2,3},{18,17},{3,32},{19,18},{32,33},{... | collective-permute-start | bytes 1228808 | tf_op jit(solution)/shard_map/ppermute | solution.py:280
  68.9 1.9 %collective-permute-start.2 = (bf16[320,640]{1,0:T(8,128)(2,1)S(1)}, bf16[320,640]{1,0:T(8,128)(2,1)}, u32[]{:S(2)}, u32[]{:S(2)}) collective-permute-start(bf16[320,640]{1,0:T(8,128)(2,1)S(1)} %get-tuple-element.24.refs_0_), channel_id=1, source_target_pairs={{0,35},{16,17},{1,0},{17,18},{2,1},{18,19},{3,2},{19,48},{32,3},{4... | collective-permute-start | bytes 1228808 | tf_op jit(solution)/shard_map/ppermute | solution.py:283
  70.8 4.6 %collective-permute-start.7 = (bf16[320,640]{1,0:T(8,128)(2,1)S(1)}, bf16[320,640]{1,0:T(8,128)(2,1)}, u32[]{:S(2)}, u32[]{:S(2)}) collective-permute-start(bf16[320,640]{1,0:T(8,128)(2,1)S(1)} %collective-permute-done.6.refs_10_), channel_id=1, source_target_pairs={{0,1},{16,51},{1,2},{17,16},{2,3},{18,17},{3,32},{19,18},{32,33},{... | collective-permute-start | bytes 1228808 | tf_op jit(solution)/shard_map/ppermute | solution.py:280
  75.5 1.9 %collective-permute-start.5 = (bf16[320,640]{1,0:T(8,128)(2,1)S(1)}, bf16[320,640]{1,0:T(8,128)(2,1)}, u32[]{:S(2)}, u32[]{:S(2)}) collective-permute-start(bf16[320,640]{1,0:T(8,128)(2,1)S(1)} %collective-permute-done.4.refs_5_), channel_id=1, source_target_pairs={{0,35},{16,17},{1,0},{17,18},{2,1},{18,19},{3,2},{19,48},{32,3},{4... | collective-permute-start | bytes 1228808 | tf_op jit(solution)/shard_map/ppermute | solution.py:283
  77.4 4.6 %collective-permute-start.9 = (bf16[320,640]{1,0:T(8,128)(2,1)S(1)}, bf16[320,640]{1,0:T(8,128)(2,1)}, u32[]{:S(2)}, u32[]{:S(2)}) collective-permute-start(bf16[320,640]{1,0:T(8,128)(2,1)S(1)} %collective-permute-done.8.refs_11_), channel_id=1, source_target_pairs={{0,1},{16,51},{1,2},{17,16},{2,3},{18,17},{3,32},{19,18},{32,33},{... | collective-permute-start | bytes 1228808 | tf_op jit(solution)/shard_map/ppermute | solution.py:280
  83.6 1.9 %collective-permute-start.3 = (bf16[320,640]{1,0:T(8,128)(2,1)}, bf16[320,640]{1,0:T(8,128)(2,1)}, u32[]{:S(2)}, u32[]{:S(2)}) collective-permute-start(bf16[320,640]{1,0:T(8,128)(2,1)} %collective-permute-done.2.refs_4_), channel_id=1, source_target_pairs={{0,35},{16,17},{1,0},{17,18},{2,1},{18,19},{3,2},{19,48},{32,3},{4... | collective-permute-start | bytes 1228808 | tf_op jit(solution)/shard_map/ppermute | solution.py:283
  87.3 11.8 %collective-permute-start = (bf16[2,128,1280]{2,1,0:T(8,128)(2,1)S(1)}, bf16[2,128,1280]{2,1,0:T(8,128)(2,1)S(1)}, u32[]{:S(2)}, u32[]{:S(2)}) collective-permute-start(bf16[2,128,1280]{2,1,0:T(8,128)(2,1)S(1)} %get-tuple-element.16.own_ref.normed_ref), channel_id=1, source_target_pairs={{0,16},{16,0},{1,17},{17,1},{2,18},{18,2},{3,19},{19,3},{4,20},{20... | collective-permute-start | bytes 1966088 | tf_op jit(solution)/shard_map/ppermute | solution.py:312
  99.1 1.9 %collective-permute-start.10 = (bf16[320,640]{1,0:T(8,128)(2,1)}, bf16[320,640]{1,0:T(8,128)(2,1)S(1)}, u32[]{:S(2)}, u32[]{:S(2)}) collective-permute-start(bf16[320,640]{1,0:T(8,128)(2,1)} %collective-permute-done.7.refs_2_), channel_id=1, source_target_pairs={{0,1},{16,51},{1,2},{17,16},{2,3},{18,17},{3,32},{19,18},{32,33},{... | collective-permute-start | bytes 1228808 | tf_op jit(solution)/shard_map/ppermute | solution.py:280
  101.1 3.4 %collective-permute-start.13 = (bf16[320,640]{1,0:T(8,128)(2,1)}, bf16[320,640]{1,0:T(8,128)(2,1)S(1)}, u32[]{:S(2)}, u32[]{:S(2)}) collective-permute-start(bf16[320,640]{1,0:T(8,128)(2,1)} %collective-permute-done.5.refs_1_), channel_id=1, source_target_pairs={{0,35},{16,17},{1,0},{17,18},{2,1},{18,19},{3,2},{19,48},{32,3},{4... | collective-permute-start | bytes 1228808 | tf_op jit(solution)/shard_map/ppermute | solution.py:283
  104.4 3.1 %collective-permute-start.11 = (bf16[320,640]{1,0:T(8,128)(2,1)}, bf16[320,640]{1,0:T(8,128)(2,1)S(1)}, u32[]{:S(2)}, u32[]{:S(2)}) collective-permute-start(bf16[320,640]{1,0:T(8,128)(2,1)} %collective-permute-done.9.refs_3_), channel_id=1, source_target_pairs={{0,1},{16,51},{1,2},{17,16},{2,3},{18,17},{3,32},{19,18},{32,33},{... | collective-permute-start | bytes 1228808 | tf_op jit(solution)/shard_map/ppermute | solution.py:280
  107.6 2.2 %collective-permute-start.12 = (bf16[320,640]{1,0:T(8,128)(2,1)}, bf16[320,640]{1,0:T(8,128)(2,1)S(1)}, u32[]{:S(2)}, u32[]{:S(2)}) collective-permute-start(bf16[320,640]{1,0:T(8,128)(2,1)} %collective-permute-done.3.refs_0_), channel_id=1, source_target_pairs={{0,35},{16,17},{1,0},{17,18},{2,1},{18,19},{3,2},{19,48},{32,3},{4... | collective-permute-start | bytes 1228808 | tf_op jit(solution)/shard_map/ppermute | solution.py:283
  110.2 3.9 %collective-permute-start.14 = (bf16[320,640]{1,0:T(8,128)(2,1)S(1)}, bf16[320,640]{1,0:T(8,128)(2,1)S(1)}, u32[]{:S(2)}, u32[]{:S(2)}) collective-permute-start(bf16[320,640]{1,0:T(8,128)(2,1)S(1)} %collective-permute-done.10.refs_6_), channel_id=1, source_target_pairs={{0,1},{16,51},{1,2},{17,16},{2,3},{18,17},{3,32},{19,18},{32,33},{... | collective-permute-start | bytes 1228808 | tf_op jit(solution)/shard_map/ppermute | solution.py:280
  119.0 5.7 %collective-permute-done.12.refs_8_ = bf16[320,640]{1,0:T(8,128)(2,1)S(1)} collective-permute-done((bf16[320,640]{1,0:T(8,128)(2,1)}, bf16[320,640]{1,0:T(8,128)(2,1)S(1)}, u32[]{:S(2)}, u32[]{:S(2)}) %collective-permute-start.12) | collective-permute-done | bytes 409632 | tf_op jit(solution)/shard_map/ppermute | solution.py:283
  125.4 6.9 %early_body.1 = (f32[1280,256]{1,0:T(8,128)S(1)}, f32[1280,256]{1,0:T(8,128)S(1)}) custom-call(s32[12]{0:T(128)S(1)} %concatenate.6.facts_ref, bf16[2,128,1280]{2,1,0:T(8,128)(2,1)S(1)} %get-tuple-element.16.own_ref.normed_ref, bf16[2,128,1280]{2,1,0:T(8,128)(2,1)S(1)} %collective-permute-done.other_ref.normed_ref, ...), custom_call_target="tpu_custom_call" | custom-call | flops 2516582400 | bytes 4915200 | tf_op jit(solution)/shard_map/early_body/pallas_call | solution.py:242
  132.3 2.7 %late_body.3 = bf16[2,1280,128]{2,1,0:T(8,128)(2,1)S(1)} custom-call(s32[12]{0:T(128)S(1)} %concatenate.6.facts_ref, bf16[2,128,1280]{2,1,0:T(8,128)(2,1)S(1)} %collective-permute-done.other_ref.normed_ref, f32[1280,256]{1,0:T(8,128)S(1)} %get-tuple-element.22.early_ref, bf16[320,640]{1,0:T(8,128)(2,1)S(1)} %get-tuple-element.24.refs_0_, ...), custom_call_target="tpu_custom_call" | custom-call | flops 838860800 | bytes 1638400 | tf_op jit(solution)/shard_map/late_body/pallas_call | solution.py:242
  135.1 1.9 %collective-permute-start.16 = (bf16[2,1280,128]{2,1,0:T(8,128)(2,1)S(1)}, bf16[2,1280,128]{2,1,0:T(8,128)(2,1)S(1)}, u32[]{:S(2)}, u32[]{:S(2)}) collective-permute-start(bf16[2,1280,128]{2,1,0:T(8,128)(2,1)S(1)} %late_body.3), channel_id=1, source_target_pairs={{0,16},{16,0},{1,17},{17,1},{2,18},{18,2},{3,19},{19,3},{4,20},{20... | collective-permute-start | bytes 1966088 | tf_op jit(solution)/shard_map/ppermute | solution.py:320
  137.0 2.7 %late_body.2 = bf16[2,1280,128]{2,1,0:T(8,128)(2,1)S(1)} custom-call(s32[12]{0:T(128)S(1)} %concatenate.6.facts_ref, bf16[2,128,1280]{2,1,0:T(8,128)(2,1)S(1)} %get-tuple-element.16.own_ref.normed_ref, f32[1280,256]{1,0:T(8,128)S(1)} %get-tuple-element.21.early_ref, bf16[320,640]{1,0:T(8,128)(2,1)S(1)} %get-tuple-element.24.refs_0_, ...), custom_call_target="tpu_custom_call" | custom-call | flops 838860800 | bytes 1638400 | tf_op jit(solution)/shard_map/late_body/pallas_call | solution.py:242
  140.0 25.0 %all_to_all.10 = bf16[8,320,128]{2,1,0:T(8,128)(2,1)S(1)} all-to-all(bf16[8,320,128]{2,1,0:T(8,128)(2,1)S(1)} %bitcast.11), channel_id=1, replica_groups=mesh['z'=16,'y_hi'=2,'core'=2,'bal_hi'=2,'bal_lo'=2,'tensor'=4] {'bal_hi..., dimensions={0} | all-to-all | bytes 1310720 | tf_op jit(solution)/shard_map/all_to_all | solution.py:325
  (40 shorter events, 13.2 us)
Async XLA Ops:
  3.6 81.9 %all-to-all-start = ((bf16[16,320,128]{2,1,0:T(8,128)(2,1)}), bf16[16,320,128]{2,1,0:T(8,128)(2,1)S(1)}, u32[]{:S(2)}, u32[]{:S(2)}) async-start(bf16[16,320,128]{2,1,0:T(8,128)(2,1)} %rotate.1), calls=%async_computation | async-start | bytes 2621440 | tf_op jit(solution)/shard_map/all_to_all | solution.py:303
  12.6 12.6 %collective-permute-start.1 = (bf16[20,640]{1,0:T(8,128)(2,1)S(1)}, bf16[20,640]{1,0:T(8,128)(2,1)S(1)}, u32[]{:S(2)}, u32[]{:S(2)}) collective-permute-start(bf16[20,640]{1,0:T(8,128)(2,1)S(1)} %get-tuple-element.20), channel_id=1, source_target_pairs={{0,16},{16,0},{1,17},{17,1},{2,18},{18,2},{3,19},{19,3},{4,20},{20... | collective-permute-start | bytes 76808 | tf_op jit(solution)/shard_map/ppermute | solution.py:306
  57.2 13.7 %collective-permute-start.6 = (bf16[320,640]{1,0:T(8,128)(2,1)S(1)}, bf16[320,640]{1,0:T(8,128)(2,1)S(1)}, u32[]{:S(2)}, u32[]{:S(2)}) collective-permute-start(bf16[320,640]{1,0:T(8,128)(2,1)S(1)} %get-tuple-element.24.refs_0_), channel_id=1, source_target_pairs={{0,1},{16,51},{1,2},{17,16},{2,3},{18,17},{3,32},{19,18},{32,33},{... | collective-permute-start | bytes 1228808 | tf_op jit(solution)/shard_map/ppermute | solution.py:280
  62.4 13.0 %collective-permute-start.4 = (bf16[320,640]{1,0:T(8,128)(2,1)S(1)}, bf16[320,640]{1,0:T(8,128)(2,1)S(1)}, u32[]{:S(2)}, u32[]{:S(2)}) collective-permute-start(bf16[320,640]{1,0:T(8,128)(2,1)S(1)} %get-tuple-element.23.refs_1_), channel_id=1, source_target_pairs={{0,35},{16,17},{1,0},{17,18},{2,1},{18,19},{3,2},{19,48},{32,3},{4... | collective-permute-start | bytes 1228808 | tf_op jit(solution)/shard_map/ppermute | solution.py:283
  64.3 13.1 %collective-permute-start.8 = (bf16[320,640]{1,0:T(8,128)(2,1)S(1)}, bf16[320,640]{1,0:T(8,128)(2,1)S(1)}, u32[]{:S(2)}, u32[]{:S(2)}) collective-permute-start(bf16[320,640]{1,0:T(8,128)(2,1)S(1)} %get-tuple-element.23.refs_1_), channel_id=1, source_target_pairs={{0,1},{16,51},{1,2},{17,16},{2,3},{18,17},{3,32},{19,18},{32,33},{... | collective-permute-start | bytes 1228808 | tf_op jit(solution)/shard_map/ppermute | solution.py:280
  68.9 14.7 %collective-permute-start.2 = (bf16[320,640]{1,0:T(8,128)(2,1)S(1)}, bf16[320,640]{1,0:T(8,128)(2,1)}, u32[]{:S(2)}, u32[]{:S(2)}) collective-permute-start(bf16[320,640]{1,0:T(8,128)(2,1)S(1)} %get-tuple-element.24.refs_0_), channel_id=1, source_target_pairs={{0,35},{16,17},{1,0},{17,18},{2,1},{18,19},{3,2},{19,48},{32,3},{4... | collective-permute-start | bytes 1228808 | tf_op jit(solution)/shard_map/ppermute | solution.py:283
  70.8 53.9 %copy-start = (bf16[320,640]{1,0:T(8,128)(2,1)}, bf16[320,640]{1,0:T(8,128)(2,1)S(1)}, u32[]{:S(2)}) copy-start(bf16[320,640]{1,0:T(8,128)(2,1)S(1)} %collective-permute-done.6.refs_10_) | copy-start | bytes 1228804
  70.8 28.3 %collective-permute-start.7 = (bf16[320,640]{1,0:T(8,128)(2,1)S(1)}, bf16[320,640]{1,0:T(8,128)(2,1)}, u32[]{:S(2)}, u32[]{:S(2)}) collective-permute-start(bf16[320,640]{1,0:T(8,128)(2,1)S(1)} %collective-permute-done.6.refs_10_), channel_id=1, source_target_pairs={{0,1},{16,51},{1,2},{17,16},{2,3},{18,17},{3,32},{19,18},{32,33},{... | collective-permute-start | bytes 1228808 | tf_op jit(solution)/shard_map/ppermute | solution.py:280
  75.4 49.3 %copy-start.1 = (bf16[320,640]{1,0:T(8,128)(2,1)}, bf16[320,640]{1,0:T(8,128)(2,1)S(1)}, u32[]{:S(2)}) copy-start(bf16[320,640]{1,0:T(8,128)(2,1)S(1)} %collective-permute-done.4.refs_5_) | copy-start | bytes 1228804
  75.5 25.6 %collective-permute-start.5 = (bf16[320,640]{1,0:T(8,128)(2,1)S(1)}, bf16[320,640]{1,0:T(8,128)(2,1)}, u32[]{:S(2)}, u32[]{:S(2)}) collective-permute-start(bf16[320,640]{1,0:T(8,128)(2,1)S(1)} %collective-permute-done.4.refs_5_), channel_id=1, source_target_pairs={{0,35},{16,17},{1,0},{17,18},{2,1},{18,19},{3,2},{19,48},{32,3},{4... | collective-permute-start | bytes 1228808 | tf_op jit(solution)/shard_map/ppermute | solution.py:283
  77.4 47.3 %copy-start.2 = (bf16[320,640]{1,0:T(8,128)(2,1)}, bf16[320,640]{1,0:T(8,128)(2,1)S(1)}, u32[]{:S(2)}) copy-start(bf16[320,640]{1,0:T(8,128)(2,1)S(1)} %collective-permute-done.8.refs_11_) | copy-start | bytes 1228804
  77.4 27.0 %collective-permute-start.9 = (bf16[320,640]{1,0:T(8,128)(2,1)S(1)}, bf16[320,640]{1,0:T(8,128)(2,1)}, u32[]{:S(2)}, u32[]{:S(2)}) collective-permute-start(bf16[320,640]{1,0:T(8,128)(2,1)S(1)} %collective-permute-done.8.refs_11_), channel_id=1, source_target_pairs={{0,1},{16,51},{1,2},{17,16},{2,3},{18,17},{3,32},{19,18},{32,33},{... | collective-permute-start | bytes 1228808 | tf_op jit(solution)/shard_map/ppermute | solution.py:280
  83.6 24.0 %collective-permute-start.3 = (bf16[320,640]{1,0:T(8,128)(2,1)}, bf16[320,640]{1,0:T(8,128)(2,1)}, u32[]{:S(2)}, u32[]{:S(2)}) collective-permute-start(bf16[320,640]{1,0:T(8,128)(2,1)} %collective-permute-done.2.refs_4_), channel_id=1, source_target_pairs={{0,35},{16,17},{1,0},{17,18},{2,1},{18,19},{3,2},{19,48},{32,3},{4... | collective-permute-start | bytes 1228808 | tf_op jit(solution)/shard_map/ppermute | solution.py:283
  87.3 37.4 %collective-permute-start = (bf16[2,128,1280]{2,1,0:T(8,128)(2,1)S(1)}, bf16[2,128,1280]{2,1,0:T(8,128)(2,1)S(1)}, u32[]{:S(2)}, u32[]{:S(2)}) collective-permute-start(bf16[2,128,1280]{2,1,0:T(8,128)(2,1)S(1)} %get-tuple-element.16.own_ref.normed_ref), channel_id=1, source_target_pairs={{0,16},{16,0},{1,17},{17,1},{2,18},{18,2},{3,19},{19,3},{4,20},{20... | collective-permute-start | bytes 1966088 | tf_op jit(solution)/shard_map/ppermute | solution.py:312
  99.1 11.1 %collective-permute-start.10 = (bf16[320,640]{1,0:T(8,128)(2,1)}, bf16[320,640]{1,0:T(8,128)(2,1)S(1)}, u32[]{:S(2)}, u32[]{:S(2)}) collective-permute-start(bf16[320,640]{1,0:T(8,128)(2,1)} %collective-permute-done.7.refs_2_), channel_id=1, source_target_pairs={{0,1},{16,51},{1,2},{17,16},{2,3},{18,17},{3,32},{19,18},{32,33},{... | collective-permute-start | bytes 1228808 | tf_op jit(solution)/shard_map/ppermute | solution.py:280
  101.1 14.9 %collective-permute-start.13 = (bf16[320,640]{1,0:T(8,128)(2,1)}, bf16[320,640]{1,0:T(8,128)(2,1)S(1)}, u32[]{:S(2)}, u32[]{:S(2)}) collective-permute-start(bf16[320,640]{1,0:T(8,128)(2,1)} %collective-permute-done.5.refs_1_), channel_id=1, source_target_pairs={{0,35},{16,17},{1,0},{17,18},{2,1},{18,19},{3,2},{19,48},{32,3},{4... | collective-permute-start | bytes 1228808 | tf_op jit(solution)/shard_map/ppermute | solution.py:283
  104.4 14.6 %collective-permute-start.11 = (bf16[320,640]{1,0:T(8,128)(2,1)}, bf16[320,640]{1,0:T(8,128)(2,1)S(1)}, u32[]{:S(2)}, u32[]{:S(2)}) collective-permute-start(bf16[320,640]{1,0:T(8,128)(2,1)} %collective-permute-done.9.refs_3_), channel_id=1, source_target_pairs={{0,1},{16,51},{1,2},{17,16},{2,3},{18,17},{3,32},{19,18},{32,33},{... | collective-permute-start | bytes 1228808 | tf_op jit(solution)/shard_map/ppermute | solution.py:280
  107.6 17.1 %collective-permute-start.12 = (bf16[320,640]{1,0:T(8,128)(2,1)}, bf16[320,640]{1,0:T(8,128)(2,1)S(1)}, u32[]{:S(2)}, u32[]{:S(2)}) collective-permute-start(bf16[320,640]{1,0:T(8,128)(2,1)} %collective-permute-done.3.refs_0_), channel_id=1, source_target_pairs={{0,35},{16,17},{1,0},{17,18},{2,1},{18,19},{3,2},{19,48},{32,3},{4... | collective-permute-start | bytes 1228808 | tf_op jit(solution)/shard_map/ppermute | solution.py:283
  110.2 14.5 %copy-start.3 = (bf16[320,640]{1,0:T(8,128)(2,1)}, bf16[320,640]{1,0:T(8,128)(2,1)S(1)}, u32[]{:S(2)}) copy-start(bf16[320,640]{1,0:T(8,128)(2,1)S(1)} %collective-permute-done.10.refs_6_) | copy-start | bytes 1228804
  110.2 22.1 %collective-permute-start.14 = (bf16[320,640]{1,0:T(8,128)(2,1)S(1)}, bf16[320,640]{1,0:T(8,128)(2,1)S(1)}, u32[]{:S(2)}, u32[]{:S(2)}) collective-permute-start(bf16[320,640]{1,0:T(8,128)(2,1)S(1)} %collective-permute-done.10.refs_6_), channel_id=1, source_target_pairs={{0,1},{16,51},{1,2},{17,16},{2,3},{18,17},{3,32},{19,18},{32,33},{... | collective-permute-start | bytes 1228808 | tf_op jit(solution)/shard_map/ppermute | solution.py:280
  115.9 8.8 %copy-start.4 = (bf16[320,640]{1,0:T(8,128)(2,1)}, bf16[320,640]{1,0:T(8,128)(2,1)S(1)}, u32[]{:S(2)}) copy-start(bf16[320,640]{1,0:T(8,128)(2,1)S(1)} %collective-permute-done.13.refs_9_) | copy-start | bytes 1228804
  115.9 16.4 %collective-permute-start.15 = (bf16[320,640]{1,0:T(8,128)(2,1)S(1)}, bf16[320,640]{1,0:T(8,128)(2,1)S(1)}, u32[]{:S(2)}, u32[]{:S(2)}) collective-permute-start(bf16[320,640]{1,0:T(8,128)(2,1)S(1)} %collective-permute-done.13.refs_9_), channel_id=1, source_target_pairs={{0,35},{16,17},{1,0},{17,18},{2,1},{18,19},{3,2},{19,48},{32,3},{4... | collective-permute-start | bytes 1228808 | tf_op jit(solution)/shard_map/ppermute | solution.py:283
  119.0 5.7 %copy-start.5 = (bf16[320,640]{1,0:T(8,128)(2,1)}, bf16[320,640]{1,0:T(8,128)(2,1)S(1)}, u32[]{:S(2)}) copy-start(bf16[320,640]{1,0:T(8,128)(2,1)S(1)} %collective-permute-done.11.refs_7_) | copy-start | bytes 1228804
  135.1 4.6 %collective-permute-start.16 = (bf16[2,1280,128]{2,1,0:T(8,128)(2,1)S(1)}, bf16[2,1280,128]{2,1,0:T(8,128)(2,1)S(1)}, u32[]{:S(2)}, u32[]{:S(2)}) collective-permute-start(bf16[2,1280,128]{2,1,0:T(8,128)(2,1)S(1)} %late_body.3), channel_id=1, source_target_pairs={{0,16},{16,0},{1,17},{17,1},{2,18},{18,2},{3,19},{19,3},{4,20},{20... | collective-permute-start | bytes 1966088 | tf_op jit(solution)/shard_map/ppermute | solution.py:320
  (1 other events, 0.8 us)
